TPU v7x, 1024 devices: a whole 8x8x8 slice. The times are simulated.
1024 devices in a mesh: expert: 16 (over x, core), fsdp: 64 (over y, z).
Axes of the slice: x: 8, y: 8, z: 8, core: 2. Of those that a mesh axis runs over, the one named last changes fastest.
Arguments:
- tokens: bfloat16 [2048, 4096], P('fsdp', 'expert'), may hold values from -6 to 6
- input_weight: bfloat16 [64, 4096, 1536], P('fsdp', 'expert'), may hold values from -0.09375 to 0.09375
- output_weight: bfloat16 [64, 768, 4096], P('fsdp', None, 'expert'), may hold values from -0.21875 to 0.21875
- routes: int32 [2048, 8], P('fsdp'), may hold values from 0 to 63, all different within a row; in each aligned block of 32 rows (0 to 31, 32 to 63, ...) at most 8 rows name the same one
- gates: float32 [2048, 8], P('fsdp'), may hold values from 0.05 to 1
- cotangent: bfloat16 [2048, 4096], P('fsdp', 'expert'), may hold values from -6 to 6
Outputs:
- mixed: bfloat16 [2048, 4096], P('fsdp', 'expert')
- grad_tokens: bfloat16 [2048, 4096], P('fsdp', 'expert')
- grad_input: bfloat16 [64, 4096, 1536], P('fsdp', 'expert')
- grad_output: bfloat16 [64, 768, 4096], P('fsdp', None, 'expert')
Inputs may be any that keep to these rules, and one draw needn't show every extreme that they name: `routes`: each token names 8 different experts. Among the tokens of one aligned block of 32 rows no expert is named more than 8 times, and in some block some expert is named exactly 8 times.
All inputs are finite; a program needn't handle non-finite values.
Results may differ from a plain program's by a relative error of at most 0.0064.
Values may be sent and summed in bfloat16 or wider, within the bound.
No kernel may reach another device: no remote copies, remote signals or barrier semaphores. Data moves between devices by JAX's collectives and lax.ppermute only.
A program may use at most 32 MiB of HBM per device.

v0:
```python
import jax
import jax.numpy as jnp
from jax import lax
from jax.sharding import PartitionSpec as P


def swish_terms(pre_act, hidden_units):
    gate_part = pre_act[:, :hidden_units]
    up_part = pre_act[:, hidden_units:]
    sigma = jax.nn.sigmoid(gate_part)
    activated = gate_part * sigma
    return (gate_part, up_part, sigma, activated)


def backward_pre(back_hidden, gate_part, up_part, sigma, activated):
    slope = sigma + gate_part * sigma * (1.0 - sigma)
    grad_gate = back_hidden * up_part * slope
    grad_up = back_hidden * activated
    return jnp.concatenate([grad_gate, grad_up], axis=1).astype(jnp.bfloat16)


def local(tokens, input_weight, output_weight, routes, gates, cotangent):
    block_tok, slice_width = tokens.shape
    route_count = routes.shape[1]
    experts = lax.axis_size("fsdp")
    hidden_units = output_weight.shape[1]
    capacity = min(block_tok, 2 * block_tok * route_count // experts)
    flat_routes = routes.reshape(-1)
    onehot = (flat_routes[:, None] == jnp.arange(experts, dtype=jnp.int32)[None, :]).astype(
        jnp.int32
    )
    earlier = jnp.cumsum(onehot, axis=0) - onehot
    slot_index = jnp.sum(earlier * onehot, axis=1).reshape(block_tok, route_count)
    hit_expert = routes[:, :, None] == jnp.arange(experts, dtype=jnp.int32)[None, None, :]
    hit_slot = slot_index[:, :, None] == jnp.arange(capacity, dtype=jnp.int32)[None, None, :]
    matched = hit_expert[:, :, :, None] & hit_slot[:, :, None, :]
    picker = jnp.transpose(jnp.any(matched, axis=1), (1, 2, 0)).astype(jnp.bfloat16)
    gate_map = jnp.transpose(
        jnp.sum(jnp.where(matched, gates[:, :, None, None], 0.0), axis=1), (1, 2, 0)
    )
    slot_gate = jnp.sum(gate_map, axis=2)
    send_rows = jnp.einsum(
        "ect,ts->ecs", picker, tokens, preferred_element_type=jnp.float32
    ).astype(jnp.bfloat16)
    picked_back = jnp.einsum("ect,ts->ecs", picker, cotangent, preferred_element_type=jnp.float32)
    send_back = (slot_gate[:, :, None] * picked_back).astype(jnp.bfloat16)
    routed_rows, routed_back = (
        lax.all_to_all(send_rows, "fsdp", split_axis=0, concat_axis=0, tiled=True),
        lax.all_to_all(send_back, "fsdp", split_axis=0, concat_axis=0, tiled=True),
    )
    compact_rows = routed_rows.reshape(experts * capacity, slice_width)
    compact_back = routed_back.reshape(experts * capacity, slice_width)
    weight_in = input_weight[0]
    weight_out = output_weight[0]
    contract_last = (((1,), (1,)), ((), ()))
    contract_first = (((0,), (0,)), ((), ()))
    pre_part = jnp.dot(compact_rows, weight_in, preferred_element_type=jnp.float32)
    back_part = lax.dot_general(
        compact_back, weight_out, contract_last, preferred_element_type=jnp.float32
    )
    pre_share, back_share = (
        lax.psum_scatter(pre_part, "expert", scatter_dimension=0, tiled=True),
        lax.psum_scatter(back_part, "expert", scatter_dimension=0, tiled=True),
    )
    gate_part, up_part, sigma, activated = swish_terms(pre_share, hidden_units)
    hidden_share = (activated * up_part).astype(jnp.bfloat16)
    grad_share = backward_pre(back_share, gate_part, up_part, sigma, activated)
    hidden, grad_pre = (
        lax.all_gather(hidden_share, "expert", axis=0, tiled=True),
        lax.all_gather(grad_share, "expert", axis=0, tiled=True),
    )
    out_rows = jnp.dot(hidden, weight_out, preferred_element_type=jnp.float32).astype(jnp.bfloat16)
    route_grad = lax.dot_general(
        grad_pre, weight_in, contract_last, preferred_element_type=jnp.float32
    ).astype(jnp.bfloat16)
    grad_input = lax.dot_general(
        compact_rows, grad_pre, contract_first, preferred_element_type=jnp.float32
    ).astype(jnp.bfloat16)[None]
    grad_output = lax.dot_general(
        hidden, compact_back, contract_first, preferred_element_type=jnp.float32
    ).astype(jnp.bfloat16)[None]
    out_slots = out_rows.reshape(experts, capacity, slice_width)
    grad_slots = route_grad.reshape(experts, capacity, slice_width)
    back_out, back_grad = (
        lax.all_to_all(out_slots, "fsdp", split_axis=0, concat_axis=0, tiled=True),
        lax.all_to_all(grad_slots, "fsdp", split_axis=0, concat_axis=0, tiled=True),
    )
    mixed = jnp.einsum(
        "ect,ecs->ts", gate_map, back_out.astype(jnp.float32), precision=lax.Precision.HIGHEST
    ).astype(jnp.bfloat16)
    grad_tokens = jnp.einsum(
        "ect,ecs->ts", picker, back_grad, preferred_element_type=jnp.float32
    ).astype(jnp.bfloat16)
    return (mixed, grad_tokens, grad_input, grad_output)


def solution(mesh):
    placed = (
        P("fsdp", "expert"),
        P("fsdp", "expert", None),
        P("fsdp", None, "expert"),
        P("fsdp", None),
        P("fsdp", None),
        P("fsdp", "expert"),
    )
    return jax.shard_map(
        local,
        mesh=mesh,
        in_specs=placed,
        out_specs=(
            P("fsdp", "expert"),
            P("fsdp", "expert"),
            P("fsdp", "expert", None),
            P("fsdp", None, "expert"),
        ),
        check_vma=False,
    )
```

profile of v0, /device:TPU:6, one launch (start us, length us, event | category | flops | bytes accessed | tf_op | source)
XLA Modules:
  0.0 264.4 jit_solution(4184289808514161681)
XLA Ops:
  7.2 0.9 copy.35
  8.3 0.1 iota_compare_fusion.1
  8.4 0.6 reduce-window.6
  9.0 0.2 slice_reduce_fusion
  9.2 0.1 fusion.20
  9.4 0.1 iota_compare_fusion
  9.6 0.4 and_reduce_fusion
  9.9 0.2 copy.40
  10.1 0.8 copy.39
  10.9 0.7 fusion.7
  11.7 0.9 fusion.1
  12.7 38.2 %all_to_all.20 = bf16[64,8,256]{2,1,0:T(8,128)(2,1)S(1)} all-to-all(bf16[64,8,256]{2,1,0:T(8,128)(2,1)S(1)} %fusion.1), channel_id=1, replica_groups=mesh['expert'=16,'fsdp'=64] {'fsdp'}, dimensions={0} | all-to-all | bytes 524288 | tf_op jit(solution)/shard_map/all_to_all | solution.py:49
  50.9 1.5 fusion.11
  52.5 0.2 convolution_convert_fusion.2
  52.7 18.3 %all_to_all.21 = bf16[64,8,256]{2,1,0:T(8,128)(2,1)S(1)} all-to-all(bf16[64,8,256]{2,1,0:T(8,128)(2,1)S(1)} %convolution_convert_fusion.2), channel_id=1, replica_groups=mesh['expert'=16,'fsdp'=64] {'fsdp'}, dimensions={0} | all-to-all | bytes 524288 | tf_op jit(solution)/shard_map/all_to_all | solution.py:48
  71.0 2.2 fusion.9
  73.3 31.3 %reduce-scatter.5.cloned.1.call-done = f32[32,768]{1,0:T(8,128)} async-done(((f32[512,768]{1,0:T(8,128)}), f32[32,768]{1,0:T(8,128)}) %reduce-scatter.5.cloned.1.call-update) | async-done | bytes 98320 | tf_op jit(solution)/shard_map/reduce_scatter | solution.py:63
  104.6 69.1 %reduce-scatter.3.cloned.1.call-done = f32[32,1536]{1,0:T(8,128)} async-done(((f32[512,1536]{1,0:T(8,128)}), f32[32,1536]{1,0:T(8,128)}) %reduce-scatter.3.cloned.1.call-update) | async-done | bytes 196624 | tf_op jit(solution)/shard_map/reduce_scatter | solution.py:62
  173.8 1.0 multiply_convert_fusion.1
  174.8 0.6 pad_maximum_fusion
  175.5 18.8 %all_gather.6 = bf16[512,768]{1,0:T(8,128)(2,1)S(1)} all-gather(bf16[32,768]{1,0:T(8,128)(2,1)S(1)} %get-tuple-element.6), channel_id=1, replica_groups=mesh['expert'=16,'fsdp'=64] {'expert'}, dimensions={0}, use_global_device_ids=true | all-gather | bytes 835584 | tf_op jit(solution)/shard_map/all_gather | solution.py:69
  194.2 1.1 fusion.4
  195.3 14.4 %all-to-all-start.1 = ((bf16[64,8,256]{2,1,0:T(8,128)(2,1)}), bf16[64,8,256]{2,1,0:T(8,128)(2,1)}, u32[]{:S(2)}, u32[]{:S(2)}) async-start(bf16[64,8,256]{2,1,0:T(8,128)(2,1)} %fusion.4), calls=%async_computation.2 | async-start | bytes 524288 | tf_op jit(solution)/shard_map/all_to_all | solution.py:85
  209.7 0.9 copy.48
  210.5 13.2 %all-gather.2.cloned.1.call-done = bf16[512,1536]{1,0:T(8,128)(2,1)} async-done(((bf16[32,1536]{1,0:T(8,128)(2,1)}), bf16[512,1536]{1,0:T(8,128)(2,1)}) %all-gather.2.cloned.1.call-update) | async-done | bytes 1572880 | tf_op jit(solution)/shard_map/all_gather | solution.py:70
  223.8 2.7 %fusion.3 = bf16[64,8,256]{2,1,0:T(8,128)(2,1)} fusion(bf16[512,1536]{1,0:T(8,128)(2,1)} %all-gather.2.cloned.1.call-done, bf16[1,256,1536]{2,1,0:T(8,128)(2,1)S(1)} %copy-done), kind=kOutput, calls=%fused_computation.11 | convolution fusion | flops 402784256 | bytes 2621440 | tf_op jit(solution)/shard_map/dot_general | solution.py:73
  226.5 14.5 %all-to-all-start.3 = ((bf16[64,8,256]{2,1,0:T(8,128)(2,1)}), bf16[64,8,256]{2,1,0:T(8,128)(2,1)}, u32[]{:S(2)}, u32[]{:S(2)}) async-start(bf16[64,8,256]{2,1,0:T(8,128)(2,1)} %fusion.3), calls=%async_computation.5 | async-start | bytes 524288 | tf_op jit(solution)/shard_map/all_to_all | solution.py:86
  241.1 2.2 fusion.2
  243.2 1.9 fusion.5
  245.1 1.5 fusion
  246.6 9.5 %all-to-all-done.3 = bf16[64,8,256]{2,1,0:T(8,128)(2,1)} async-done(((bf16[64,8,256]{2,1,0:T(8,128)(2,1)}), bf16[64,8,256]{2,1,0:T(8,128)(2,1)}, u32[]{:S(2)}, u32[]{:S(2)}) %all-to-all-start.3) | async-done | bytes 262176 | tf_op jit(solution)/shard_map/all_to_all | solution.py:86
  256.1 1.8 fusion.6
  (27 shorter events, 0.6 us)
Async XLA Ops:
  7.2 63.8 %copy-start = (bf16[1,256,1536]{2,1,0:T(8,128)(2,1)S(1)}, bf16[1,256,1536]{2,1,0:T(8,128)(2,1)}, u32[]{:S(2)}) copy-start(bf16[1,256,1536]{2,1,0:T(8,128)(2,1)} %param.7) | copy-start | bytes 2359300
  7.2 43.7 %copy-start.2 = (bf16[1,768,256]{2,1,0:T(8,128)(2,1)S(1)}, bf16[1,768,256]{2,1,0:T(8,128)(2,1)}, u32[]{:S(2)}) copy-start(bf16[1,768,256]{2,1,0:T(8,128)(2,1)} %param.8) | copy-start | bytes 1179652
  7.2 97.4 %reduce-scatter.5.cloned.1.call-start = ((), (), s32[]{:S(2)}) async-start(), calls=%async_computation.7 | async-start | bytes 1671168 | tf_op jit(solution)/shard_map/reduce_scatter | solution.py:63
  50.9 1.6 copy-start.3
  50.9 1.6 copy-start.5
  52.4 121.3 %reduce-scatter.3.cloned.1.call-start = ((), (), s32[]{:S(2)}) async-start(), calls=%async_computation.6 | async-start | bytes 3342336 | tf_op jit(solution)/shard_map/reduce_scatter | solution.py:62
  73.2 150.5 %all-gather.2.cloned.1.call-start = ((), (), s32[]{:S(2)}) async-start(), calls=%async_computation.8 | async-start | bytes 1671168 | tf_op jit(solution)/shard_map/all_gather | solution.py:70
  195.3 31.2 %all-to-all-start.1 = ((bf16[64,8,256]{2,1,0:T(8,128)(2,1)}), bf16[64,8,256]{2,1,0:T(8,128)(2,1)}, u32[]{:S(2)}, u32[]{:S(2)}) async-start(bf16[64,8,256]{2,1,0:T(8,128)(2,1)} %fusion.4), calls=%async_computation.2 | async-start | bytes 524288 | tf_op jit(solution)/shard_map/all_to_all | solution.py:85
  226.5 18.6 %copy-start.1 = (bf16[512,1536]{1,0:T(8,128)(2,1)S(1)}, bf16[512,1536]{1,0:T(8,128)(2,1)}, u32[]{:S(2)}) copy-start(bf16[512,1536]{1,0:T(8,128)(2,1)} %all-gather.2.cloned.1.call-done) | copy-start | bytes 4718596
  226.5 29.6 %all-to-all-start.3 = ((bf16[64,8,256]{2,1,0:T(8,128)(2,1)}), bf16[64,8,256]{2,1,0:T(8,128)(2,1)}, u32[]{:S(2)}, u32[]{:S(2)}) async-start(bf16[64,8,256]{2,1,0:T(8,128)(2,1)} %fusion.3), calls=%async_computation.5 | async-start | bytes 524288 | tf_op jit(solution)/shard_map/all_to_all | solution.py:86
  241.0 2.2 copy-start.4
Sparse Core Ops, SparseCore 0:
  52.5 52.0 reduce-scatter.4
  108.4 65.2 reduce-scatter.2
  176.8 46.9 all-gather.1
where the time goes:
time: 265 us; the launch traced here: 264 us
  waiting for transfers between devices  123 us (46%)
  blocking collectives  75.2 us (28%)
  starting transfers between devices  29 us (11%)
  matrix products  16.1 us (6%)
  between operations  13.9 us (5%)
  other arithmetic  3.77 us (1%)
  local copies, waits for them, and re-layouts  3.22 us (1%)
    reduce_scatter x1, waiting for transfers between devices, local(): lax.psum_scatter(pre_part, 'expert', scatter_dimension=0, tiled=True)  69.1 us
    all_to_all x1, blocking collectives, local(): lax.all_to_all(send_back, 'fsdp', split_axis=0, concat_axis=0, tiled=True)  38.2 us
    reduce_scatter x1, waiting for transfers between devices, local(): lax.psum_scatter(back_part, 'expert', scatter_dimension=0, tiled=True)  31.3 us
    all_gather x1, blocking collectives, local(): lax.all_gather(hidden_share, 'expert', axis=0, tiled=True)  18.8 us
    all_to_all x1, blocking collectives, local(): lax.all_to_all(send_rows, 'fsdp', split_axis=0, concat_axis=0, tiled=True)  18.3 us
    all_to_all x1, starting transfers between devices, local(): lax.all_to_all(grad_slots, 'fsdp', split_axis=0, concat_axis=0, tiled=True)  14.5 us
    all_to_all x1, starting transfers between devices, local(): lax.all_to_all(out_slots, 'fsdp', split_axis=0, concat_axis=0, tiled=True)  14.4 us
    all_gather x1, waiting for transfers between devices, local(): lax.all_gather(grad_share, 'expert', axis=0, tiled=True)  13.2 us
  transfers between devices with their start and end apart: 5, of which 4 were waited for; matrix products, arithmetic and copies ran while one was open for 5% of the time, Pallas kernels for 0%

commit v1 on v0

v1 whole, which is shorter than its diff:
```python
import jax
import jax.numpy as jnp
from jax import lax
from jax.sharding import PartitionSpec as P

LAST = (((1,), (1,)), ((), ()))
FIRST = (((0,), (0,)), ((), ()))


def dot(a, b, dims=(((1,), (0,)), ((), ()))):
    return lax.dot_general(a, b, dims, preferred_element_type=jnp.float32)


def swish_terms(pre_act, hidden_units):
    gate_part = pre_act[:, :hidden_units]
    up_part = pre_act[:, hidden_units:]
    sigma = jax.nn.sigmoid(gate_part)
    activated = gate_part * sigma
    return (gate_part, up_part, sigma, activated)


def local(tokens, input_weight, output_weight, routes, gates, cotangent):
    block_tok, width = tokens.shape
    route_count = routes.shape[1]
    experts = lax.axis_size("fsdp")
    ff = output_weight.shape[1]
    capacity = min(block_tok, 2 * block_tok * route_count // experts)
    rows = experts * capacity
    weight_in = input_weight[0]
    weight_out = output_weight[0]

    flat_routes = routes.reshape(-1)
    onehot = (flat_routes[:, None] == jnp.arange(experts, dtype=jnp.int32)[None, :]).astype(
        jnp.int32
    )
    earlier = jnp.cumsum(onehot, axis=0) - onehot
    slot_index = jnp.sum(earlier * onehot, axis=1).reshape(block_tok, route_count)
    target = routes * capacity + slot_index
    hit = target[:, :, None] == jnp.arange(rows, dtype=jnp.int32)[None, None, :]
    picker = jnp.any(hit, axis=1).astype(jnp.bfloat16)
    gate_map = jnp.sum(jnp.where(hit, gates[:, :, None], 0.0), axis=1)
    slot_gate = jnp.sum(gate_map, axis=0)
    send_rows = dot(picker, tokens, FIRST).astype(jnp.bfloat16)
    send_back = (slot_gate[:, None] * dot(picker, cotangent, FIRST)).astype(jnp.bfloat16)
    sent = jnp.concatenate(
        [send_rows.reshape(experts, capacity, width), send_back.reshape(experts, capacity, width)],
        axis=1,
    )
    got = lax.all_to_all(sent, "fsdp", split_axis=0, concat_axis=0, tiled=True)
    routed_rows = got[:, :capacity].reshape(rows, width)
    routed_back = got[:, capacity:].reshape(rows, width)

    chips = lax.axis_size("expert") // 2
    device = lax.axis_index("expert")
    piece = rows // (2 * chips)
    core = device & 1

    def half(values, which):
        pieces = values.reshape(chips, 2, piece, width)
        return lax.dynamic_index_in_dim(pieces, which, 1, keepdims=False).reshape(-1, width)

    def partial_sums(which):
        return jnp.concatenate(
            [
                dot(half(routed_rows, which), weight_in),
                dot(half(routed_back, which), weight_out, LAST),
            ],
            axis=1,
        )

    swap = [(d, d ^ 1) for d in range(2 * chips)]
    same_core = [[2 * i + c for i in range(chips)] for c in range(2)]
    arrived = lax.ppermute(partial_sums(1 - core).astype(jnp.bfloat16), "expert", swap)
    chip_sum = (partial_sums(core) + arrived.astype(jnp.float32)).astype(jnp.bfloat16)
    pieces = lax.all_to_all(
        chip_sum.reshape(chips, piece, 3 * ff),
        "expert",
        split_axis=0,
        concat_axis=0,
        tiled=True,
        axis_index_groups=same_core,
    )
    share = jnp.sum(pieces.astype(jnp.float32), axis=0)
    gate_part, up_part, sigma, activated = swish_terms(share[:, : 2 * ff], ff)
    back_hidden = share[:, 2 * ff :]
    slope = sigma + gate_part * sigma * (1.0 - sigma)
    hidden, grad_gate, grad_up = (
        lax.all_gather(part.astype(jnp.bfloat16), "expert", axis=0, tiled=True)
        for part in (activated * up_part, back_hidden * up_part * slope, back_hidden * activated)
    )
    grad_pre = jnp.concatenate([grad_gate, grad_up], axis=1)

    out_rows = dot(hidden, weight_out).astype(jnp.bfloat16)
    route_grad = dot(grad_pre, weight_in, LAST).astype(jnp.bfloat16)
    back = jnp.concatenate(
        [out_rows.reshape(experts, capacity, width), route_grad.reshape(experts, capacity, width)],
        axis=1,
    )
    home = lax.all_to_all(back, "fsdp", split_axis=0, concat_axis=0, tiled=True)
    grad_input = dot(routed_rows, grad_pre, FIRST).astype(jnp.bfloat16)[None]
    grad_output = dot(hidden, routed_back, FIRST).astype(jnp.bfloat16)[None]
    mixed = lax.dot(
        gate_map,
        home[:, :capacity].reshape(rows, width).astype(jnp.float32),
        precision=lax.Precision.HIGHEST,
    ).astype(jnp.bfloat16)
    grad_tokens = dot(picker, home[:, capacity:].reshape(rows, width)).astype(jnp.bfloat16)
    return (mixed, grad_tokens, grad_input, grad_output)


def solution(mesh):
    placed = (
        P("fsdp", "expert"),
        P("fsdp", "expert", None),
        P("fsdp", None, "expert"),
        P("fsdp", None),
        P("fsdp", None),
        P("fsdp", "expert"),
    )
    return jax.shard_map(
        local,
        mesh=mesh,
        in_specs=placed,
        out_specs=(
            P("fsdp", "expert"),
            P("fsdp", "expert"),
            P("fsdp", "expert", None),
            P("fsdp", None, "expert"),
        ),
        check_vma=False,
    )
```

time: 265 us -> 175 us (0.66)
  the two profiles are of different devices: /device:TPU:6 before, /device:TPU:34 now
where the time goes in v1:
time: 175 us; the launch traced here: 174 us
  blocking collectives  89.8 us (51%)
  waiting for transfers between devices  37.7 us (22%)
  starting transfers between devices  30.3 us (17%)
  matrix products  9.68 us (6%)
  other arithmetic  3.46 us (2%)
  local copies, waits for them, and re-layouts  2.75 us (2%)
    all_gather x3, blocking collectives, local(): lax.all_gather(part.astype(jnp.bfloat16), 'expert', axis=0, tiled=True)  52.3 us
    all_to_all x1, blocking collectives, local(): lax.all_to_all(chip_sum.reshape(chips, piece, 3 * ff), 'expert', split_ax...  37.5 us
    all_to_all x1, starting transfers between devices, local(): got = lax.all_to_all(sent, 'fsdp', split_axis=0, concat_axis=0, tiled=True)  23.2 us
    all_to_all x1, waiting for transfers between devices, local(): got = lax.all_to_all(sent, 'fsdp', split_axis=0, concat_axis=0, tiled=True)  19.4 us
    all_to_all x1, waiting for transfers between devices, local(): home = lax.all_to_all(back, 'fsdp', split_axis=0, concat_axis=0, tiled=True)  16.1 us
    dot_general x11, matrix products, dot(): return lax.dot_general(a, b, dims, preferred_element_type=jnp.float32)  8.83 us
    all_to_all x1, starting transfers between devices, local(): home = lax.all_to_all(back, 'fsdp', split_axis=0, concat_axis=0, tiled=True)  5.2 us
  transfers between devices with their start and end apart: 3, of which 3 were waited for; matrix products, arithmetic and copies ran while one was open for 3% of the time, Pallas kernels for 0%

profile of v1, /device:TPU:34, one launch (start us, length us, event | category | flops | bytes accessed | tf_op | source)
XLA Modules:
  0.0 174.5 jit_solution(18312731375290310337)
XLA Ops:
  0.6 0.8 copy.17
  1.7 0.8 copy.21
  2.4 0.6 reduce-window.6
  3.0 0.2 slice_reduce_fusion
  3.5 0.2 fusion.12
  3.7 0.2 select_reduce_fusion
  4.0 1.0 fusion.7
  5.0 1.0 fusion.5
  6.0 0.8 pad_maximum_fusion.1
  6.8 23.2 %all-to-all-start = ((bf16[64,16,256]{2,1,0:T(8,128)(2,1)}), bf16[64,16,256]{2,1,0:T(8,128)(2,1)S(1)}, u32[]{:S(2)}, u32[]{:S(2)}) async-start(bf16[64,16,256]{2,1,0:T(8,128)(2,1)} %pad_maximum_fusion.1), calls=%async_computation | async-start | bytes 1048576 | tf_op jit(solution)/shard_map/all_to_all | solution.py:49
  30.0 19.4 %all-to-all-done = bf16[64,16,256]{2,1,0:T(8,128)(2,1)S(1)} async-done(((bf16[64,16,256]{2,1,0:T(8,128)(2,1)}), bf16[64,16,256]{2,1,0:T(8,128)(2,1)S(1)}, u32[]{:S(2)}, u32[]{:S(2)}) %all-to-all-start) | async-done | bytes 524320 | tf_op jit(solution)/shard_map/all_to_all | solution.py:49
  49.5 0.3 convolution_convert_fusion.3
  49.8 0.4 convolution_convert_fusion
  50.3 1.9 %collective-permute-start = (bf16[256,2304]{1,0:T(8,128)(2,1)S(1)}, bf16[256,2304]{1,0:T(8,128)(2,1)S(1)}, u32[]{:S(2)}, u32[]{:S(2)}) collective-permute-start(bf16[256,2304]{1,0:T(8,128)(2,1)S(1)} %pad_maximum_fusion), channel_id=1, source_target_pairs={{0,64},{64,0},{128,192},{192,128},{256,320},{320,256},{384,448},{4... | collective-permute-start | bytes 3538952 | tf_op jit(solution)/shard_map/ppermute | solution.py:73
  52.2 0.3 fusion.15
  52.5 0.4 fusion.10
  52.9 2.1 %collective-permute-done = bf16[256,2304]{1,0:T(8,128)(2,1)S(1)} collective-permute-done((bf16[256,2304]{1,0:T(8,128)(2,1)S(1)}, bf16[256,2304]{1,0:T(8,128)(2,1)S(1)}, u32[]{:S(2)}, u32[]{:S(2)}) %collective-permute-start) | collective-permute-done | bytes 1179680 | tf_op jit(solution)/shard_map/ppermute | solution.py:73
  55.0 0.3 fusion.1
  55.3 37.5 %all_to_all.15 = bf16[8,32,2304]{2,1,0:T(8,128)(2,1)S(1)} all-to-all(bf16[8,32,2304]{2,1,0:T(8,128)(2,1)S(1)} %bitcast.78), channel_id=1, replica_groups={{0,128,256,384,512,640,768,896},{64,192,320,448,576,704,832,960},{1,129..., dimensions={0} | all-to-all | bytes 2359296 | tf_op jit(solution)/shard_map/all_to_all | solution.py:75
  93.0 17.7 %all_gather.9 = bf16[512,768]{1,0:T(8,128)(2,1)S(1)} all-gather(bf16[32,768]{1,0:T(8,128)(2,1)S(1)} %get-tuple-element.8), channel_id=1, replica_groups=mesh['expert'=16,'fsdp'=64] {'expert'}, dimensions={0}, use_global_device_ids=true | all-gather | bytes 835584 | tf_op jit(solution)/shard_map/all_gather | solution.py:88
  110.7 0.4 fusion.6
  111.1 0.5 copy-done.2
  111.6 16.8 %all_gather.10 = bf16[512,768]{1,0:T(8,128)(2,1)S(1)} all-gather(bf16[32,768]{1,0:T(8,128)(2,1)S(1)} %get-tuple-element.9), channel_id=1, replica_groups=mesh['expert'=16,'fsdp'=64] {'expert'}, dimensions={0}, use_global_device_ids=true | all-gather | bytes 835584 | tf_op jit(solution)/shard_map/all_gather | solution.py:88
  128.5 17.7 %all_gather.11 = bf16[512,768]{1,0:T(8,128)(2,1)S(1)} all-gather(bf16[32,768]{1,0:T(8,128)(2,1)S(1)} %get-tuple-element.10), channel_id=1, replica_groups=mesh['expert'=16,'fsdp'=64] {'expert'}, dimensions={0}, use_global_device_ids=true | all-gather | bytes 835584 | tf_op jit(solution)/shard_map/all_gather | solution.py:88
  146.3 0.6 fusion.4
  146.9 0.8 pad_maximum_fusion.2
  147.7 5.2 %all-to-all-start.2 = ((bf16[64,16,256]{2,1,0:T(8,128)(2,1)}), bf16[64,16,256]{2,1,0:T(8,128)(2,1)S(1)}, u32[]{:S(2)}, u32[]{:S(2)}) async-start(bf16[64,16,256]{2,1,0:T(8,128)(2,1)} %pad_maximum_fusion.2), calls=%async_computation.2 | async-start | bytes 1048576 | tf_op jit(solution)/shard_map/all_to_all | solution.py:99
  152.9 2.3 %fusion.3 = bf16[1,768,256]{2,1,0:T(8,128)(2,1)} fusion(bf16[512,768]{1,0:T(8,128)(2,1)} %copy-done.2, bf16[64,16,256]{2,1,0:T(8,128)(2,1)S(1)} %all-to-all-done), kind=kOutput, calls=%fused_computation.13 | convolution fusion | flops 201523200 | bytes 1441792 | tf_op jit(solution)/shard_map/dot_general | solution.py:11
  155.2 1.5 fusion
  156.7 16.1 %all-to-all-done.2 = bf16[64,16,256]{2,1,0:T(8,128)(2,1)S(1)} async-done(((bf16[64,16,256]{2,1,0:T(8,128)(2,1)}), bf16[64,16,256]{2,1,0:T(8,128)(2,1)S(1)}, u32[]{:S(2)}, u32[]{:S(2)}) %all-to-all-start.2) | async-done | bytes 524320 | tf_op jit(solution)/shard_map/all_to_all | solution.py:99
  172.9 0.8 convolution_convert_fusion.7
  173.6 0.9 convolution_convert_fusion.8
  (20 shorter events, 0.9 us)
Async XLA Ops:
  0.6 49.2 %copy-start = (bf16[1,256,1536]{2,1,0:T(8,128)(2,1)S(1)}, bf16[1,256,1536]{2,1,0:T(8,128)(2,1)}, u32[]{:S(2)}) copy-start(bf16[1,256,1536]{2,1,0:T(8,128)(2,1)} %param.7) | copy-start | bytes 2359300
  6.8 42.7 %copy-start.1 = (bf16[1,768,256]{2,1,0:T(8,128)(2,1)S(1)}, bf16[1,768,256]{2,1,0:T(8,128)(2,1)}, u32[]{:S(2)}) copy-start(bf16[1,768,256]{2,1,0:T(8,128)(2,1)} %param.8) | copy-start | bytes 1179652
  6.8 42.6 %all-to-all-start = ((bf16[64,16,256]{2,1,0:T(8,128)(2,1)}), bf16[64,16,256]{2,1,0:T(8,128)(2,1)S(1)}, u32[]{:S(2)}, u32[]{:S(2)}) async-start(bf16[64,16,256]{2,1,0:T(8,128)(2,1)} %pad_maximum_fusion.1), calls=%async_computation | async-start | bytes 1048576 | tf_op jit(solution)/shard_map/all_to_all | solution.py:49
  50.3 4.7 %collective-permute-start = (bf16[256,2304]{1,0:T(8,128)(2,1)S(1)}, bf16[256,2304]{1,0:T(8,128)(2,1)S(1)}, u32[]{:S(2)}, u32[]{:S(2)}) collective-permute-start(bf16[256,2304]{1,0:T(8,128)(2,1)S(1)} %pad_maximum_fusion), channel_id=1, source_target_pairs={{0,64},{64,0},{128,192},{192,128},{256,320},{320,256},{384,448},{4... | collective-permute-start | bytes 3538952 | tf_op jit(solution)/shard_map/ppermute | solution.py:73
  110.7 0.9 copy-start.2
  147.7 25.1 %all-to-all-start.2 = ((bf16[64,16,256]{2,1,0:T(8,128)(2,1)}), bf16[64,16,256]{2,1,0:T(8,128)(2,1)S(1)}, u32[]{:S(2)}, u32[]{:S(2)}) async-start(bf16[64,16,256]{2,1,0:T(8,128)(2,1)} %pad_maximum_fusion.2), calls=%async_computation.2 | async-start | bytes 1048576 | tf_op jit(solution)/shard_map/all_to_all | solution.py:99

commit v2 on v1

v2 whole, which is shorter than its diff:
```python
import jax
import jax.numpy as jnp
from jax import lax
from jax.experimental import pallas as pl
from jax.experimental.pallas import tpu as pltpu
from jax.sharding import PartitionSpec as P

PLAIN = (((1,), (0,)), ((), ()))
LAST = (((1,), (1,)), ((), ()))
FIRST = (((0,), (0,)), ((), ()))


def dot(a, b, dims=PLAIN):
    return lax.dot_general(a, b, dims, preferred_element_type=jnp.float32)


def bf16_parts(values):
    first = values.astype(jnp.bfloat16)
    rest = values - first.astype(jnp.float32)
    second = rest.astype(jnp.bfloat16)
    third = (rest - second.astype(jnp.float32)).astype(jnp.bfloat16)
    return first, second, third


def dispatch_kernel(capacity, routes_ref, gates_ref, tokens_ref, cotangent_ref, sent_ref, maps_ref):
    experts, _, width = sent_ref.shape
    count, route_count = routes_ref.shape
    rows = experts * capacity
    routes = routes_ref[...]
    gates = gates_ref[...]
    lane = lax.broadcasted_iota(jnp.int32, (count, experts), 1)
    named = jnp.zeros((count, experts), jnp.float32)
    gate_of = jnp.zeros((count, experts), jnp.float32)
    for k in range(route_count):
        hit = routes[:, k : k + 1] == lane
        named = jnp.where(hit, 1.0, named)
        gate_of = jnp.where(hit, gates[:, k : k + 1], gate_of)
    row = lax.broadcasted_iota(jnp.int32, (count, count), 0)
    column = lax.broadcasted_iota(jnp.int32, (count, count), 1)
    before = jnp.where(column < row, 1.0, 0.0).astype(jnp.bfloat16)
    named = named.astype(jnp.bfloat16)
    slot = dot(before, named).astype(jnp.bfloat16)
    first_row = lax.broadcasted_iota(jnp.int32, (experts, rows), 0) * capacity
    at = lax.broadcasted_iota(jnp.int32, (experts, rows), 1)
    inside = (at >= first_row) & (at < first_row + capacity)
    spread = jnp.where(inside, 1.0, 0.0).astype(jnp.bfloat16)
    local_slot = jnp.sum(jnp.where(inside, at - first_row, 0), axis=0, keepdims=True)
    picked = (dot(named, spread) > 0.5) & (dot(slot, spread) == local_slot.astype(jnp.float32))
    picker = jnp.where(picked, 1.0, 0.0).astype(jnp.bfloat16)
    ones = jnp.ones((count, width), jnp.bfloat16)
    row_gate = jnp.zeros((rows, width), jnp.float32)
    for i, part in enumerate(bf16_parts(gate_of)):
        spread_part = jnp.where(picked, dot(part, spread), 0.0).astype(jnp.bfloat16)
        maps_ref[i * count : (i + 1) * count, :] = spread_part
        row_gate = row_gate + dot(spread_part, ones, FIRST)
    maps_ref[3 * count : 4 * count, :] = picker
    send_rows = dot(picker, tokens_ref[...], FIRST)
    send_back = row_gate * dot(picker, cotangent_ref[...], FIRST)
    sent_ref[...] = jnp.concatenate(
        [send_rows.reshape(experts, capacity, width), send_back.reshape(experts, capacity, width)],
        axis=1,
    ).astype(jnp.bfloat16)


def combine_kernel(capacity, maps_ref, home_ref, mixed_ref, grad_ref):
    experts, _, width = home_ref.shape
    count = mixed_ref.shape[0]
    rows = experts * capacity
    home = home_ref[...].astype(jnp.float32)
    out = home[:, :capacity, :].reshape(rows, width).astype(jnp.bfloat16)
    grad = home[:, capacity:, :].reshape(rows, width).astype(jnp.bfloat16)
    total = dot(maps_ref[0:count, :], out)
    total = total + dot(maps_ref[count : 2 * count, :], out)
    total = total + dot(maps_ref[2 * count : 3 * count, :], out)
    mixed_ref[...] = total.astype(jnp.bfloat16)
    grad_ref[...] = dot(maps_ref[3 * count : 4 * count, :], grad).astype(jnp.bfloat16)


def call(kernel, out_shape, flops, *operands):
    def size(a):
        return a.size * a.dtype.itemsize

    moved = sum(map(size, operands)) + sum(map(size, jax.tree.leaves(out_shape)))
    return pl.pallas_call(
        kernel,
        out_shape=out_shape,
        compiler_params=pltpu.CompilerParams(vmem_limit_bytes=40 * 2**20),
        cost_estimate=pl.CostEstimate(flops=flops, bytes_accessed=moved, transcendentals=0),
    )(*operands)


def local(tokens, input_weight, output_weight, routes, gates, cotangent):
    block_tok, width = tokens.shape
    route_count = routes.shape[1]
    experts = lax.axis_size("fsdp")
    chips = lax.axis_size("expert") // 2
    ff = output_weight.shape[1]
    capacity = min(block_tok, 2 * block_tok * route_count // experts)
    rows = experts * capacity
    piece = rows // (2 * chips)
    core = lax.axis_index("expert") & 1
    weight_in = input_weight[0]
    weight_out = output_weight[0]
    swap = [(d, d ^ 1) for d in range(2 * chips)]
    same_core = [[2 * i + c for i in range(chips)] for c in range(2)]

    def exchange(values):
        return lax.all_to_all(values, "fsdp", split_axis=0, concat_axis=0, tiled=True)

    def exchange_chips(values):
        return lax.all_to_all(
            values, "expert", split_axis=0, concat_axis=0, tiled=True, axis_index_groups=same_core
        )

    def half(values, which):
        pieces = values.reshape(chips, 2, piece, width)
        return lax.dynamic_index_in_dim(pieces, which, 1, keepdims=False).reshape(-1, width)

    def both(mine, other):
        mine = mine.reshape(chips, piece, -1)
        other = other.reshape(chips, piece, -1)
        first = core == 0
        return jnp.stack(
            [jnp.where(first, mine, other), jnp.where(first, other, mine)], axis=1
        ).reshape(rows, -1)

    sent, maps = call(
        lambda *refs: dispatch_kernel(capacity, *refs),
        (
            jax.ShapeDtypeStruct((experts, 2 * capacity, width), jnp.bfloat16),
            jax.ShapeDtypeStruct((4 * block_tok, rows), jnp.bfloat16),
        ),
        10 * rows * block_tok * width,
        routes,
        gates,
        tokens,
        cotangent,
    )
    got = exchange(sent)
    routed_rows = got[:, :capacity].reshape(rows, width)
    routed_back = got[:, capacity:].reshape(rows, width)
    mine_rows, other_rows = half(routed_rows, core), half(routed_rows, 1 - core)
    mine_back, other_back = half(routed_back, core), half(routed_back, 1 - core)

    def partial_sums(some_rows, some_back):
        return jnp.concatenate(
            [dot(some_rows, weight_in), dot(some_back, weight_out, LAST)], axis=1
        )

    arrived = lax.ppermute(
        partial_sums(other_rows, other_back).astype(jnp.bfloat16), "expert", swap
    )
    chip_sum = partial_sums(mine_rows, mine_back) + arrived.astype(jnp.float32)
    pieces = exchange_chips(chip_sum.astype(jnp.bfloat16).reshape(chips, piece, 3 * ff))
    share = jnp.sum(pieces.astype(jnp.float32), axis=0)
    gate_part, up_part, back_hidden = share[:, :ff], share[:, ff : 2 * ff], share[:, 2 * ff :]
    sigma = jax.nn.sigmoid(gate_part)
    activated = gate_part * sigma
    slope = sigma + gate_part * sigma * (1.0 - sigma)
    grad_share = jnp.concatenate(
        [back_hidden * up_part * slope, back_hidden * activated], axis=1
    ).astype(jnp.bfloat16)
    hidden_share = (activated * up_part).astype(jnp.bfloat16)

    mine_grad = exchange_chips(
        jnp.broadcast_to(grad_share[None], (chips, *grad_share.shape))
    ).reshape(-1, 2 * ff)
    hidden = lax.all_gather(hidden_share, "expert", axis=0, tiled=True)
    mine_grad, hidden = lax.optimization_barrier((mine_grad, hidden))
    other_grad = lax.ppermute(mine_grad, "expert", swap)
    out_rows = dot(hidden, weight_out).astype(jnp.bfloat16)
    route_grad = both(
        dot(mine_grad, weight_in, LAST).astype(jnp.bfloat16),
        dot(other_grad, weight_in, LAST).astype(jnp.bfloat16),
    )
    back = jnp.concatenate(
        [out_rows.reshape(experts, capacity, width), route_grad.reshape(experts, capacity, width)],
        axis=1,
    )
    home = exchange(back)
    grad_input = (
        (dot(mine_rows, mine_grad, FIRST) + dot(other_rows, other_grad, FIRST))
        .astype(jnp.bfloat16)
    )[None]
    grad_output = dot(hidden, routed_back, FIRST).astype(jnp.bfloat16)[None]
    mixed, grad_tokens = call(
        lambda *refs: combine_kernel(capacity, *refs),
        (
            jax.ShapeDtypeStruct((block_tok, width), jnp.bfloat16),
            jax.ShapeDtypeStruct((block_tok, width), jnp.bfloat16),
        ),
        8 * rows * block_tok * width,
        maps,
        home,
    )
    return (mixed, grad_tokens, grad_input, grad_output)


def solution(mesh):
    placed = (
        P("fsdp", "expert"),
        P("fsdp", "expert", None),
        P("fsdp", None, "expert"),
        P("fsdp", None),
        P("fsdp", None),
        P("fsdp", "expert"),
    )
    return jax.shard_map(
        local,
        mesh=mesh,
        in_specs=placed,
        out_specs=(
            P("fsdp", "expert"),
            P("fsdp", "expert"),
            P("fsdp", "expert", None),
            P("fsdp", None, "expert"),
        ),
        check_vma=False,
    )
```

time: 175 us -> 164 us (0.937)
  the two profiles are of different devices: /device:TPU:34 before, /device:TPU:32 now
where the time goes in v2:
time: 164 us; the launch traced here: 163 us
  blocking collectives  71 us (43%)
  waiting for transfers between devices  38.2 us (23%)
  starting transfers between devices  36.3 us (22%)
  matrix products  7.58 us (5%)
  local copies, waits for them, and re-layouts  4.6 us (3%)
  Pallas kernels  2.66 us (2%)
  other arithmetic  2.04 us (1%)
    all_to_all x1, blocking collectives, exchange_chips(): lax.all_to_all(values, 'expert', split_axis=0, concat_axis=0, tiled=True,...  38.4 us
    all_to_all x2, waiting for transfers between devices, exchange(): lax.all_to_all(values, 'fsdp', split_axis=0, concat_axis=0, tiled=True)  34.8 us
    all_gather x1, blocking collectives, local(): hidden = lax.all_gather(hidden_share, 'expert', axis=0, tiled=True)  32.6 us
    all_to_all x2, starting transfers between devices, exchange(): lax.all_to_all(values, 'fsdp', split_axis=0, concat_axis=0, tiled=True)  28.4 us
    dot_general x10, matrix products, dot(): return lax.dot_general(a, b, dims, preferred_element_type=jnp.float32)  7.58 us
    all_to_all x1, starting transfers between devices, exchange_chips(): lax.all_to_all(values, 'expert', split_axis=0, concat_axis=0, tiled=True,...  3.68 us
    unnamed x20, local copies, waits for them, and re-layouts  3.57 us
  transfers between devices with their start and end apart: 5, of which 4 were waited for; matrix products, arithmetic and copies ran while one was open for 3% of the time, Pallas kernels for 0%

profile of v2, /device:TPU:32, one launch (start us, length us, event | category | flops | bytes accessed | tf_op | source)
XLA Modules:
  0.0 163.2 jit_solution(11426244909109624227)
XLA Ops:
  0.6 0.8 copy.10.refs_0_
  1.5 0.8 copy.11.refs_1_
  2.2 0.7 copy-done.1
  3.0 0.7 copy-done.2
  3.7 1.8 %shard_map.93 = (bf16[64,16,256]{2,1,0:T(8,128)(2,1)}, bf16[128,512]{1,0:T(8,128)(2,1)S(1)}) custom-call(s32[32,8]{1,0:T(8,128)S(1)} %copy.10.refs_0_, f32[32,8]{1,0:T(8,128)S(1)} %copy.11.refs_1_, bf16[32,256]{1,0:T(8,128)(2,1)S(1)} %copy-done.1, bf16[32,256]{1,0:T(8,128)(2,1)S(1)} %copy-done.2), custom_call_target="tpu_custom_call" | custom-call | flops 41943040 | bytes 690176 | tf_op jit(solution)/shard_map/pallas_call | solution.py:84
  5.4 23.2 %all-to-all-start = ((bf16[64,16,256]{2,1,0:T(8,128)(2,1)}), bf16[64,16,256]{2,1,0:T(8,128)(2,1)S(1)}, u32[]{:S(2)}, u32[]{:S(2)}) async-start(bf16[64,16,256]{2,1,0:T(8,128)(2,1)} %get-tuple-element.11), calls=%async_computation | async-start | bytes 1048576 | tf_op jit(solution)/shard_map/all_to_all | solution.py:108
  28.7 19.4 %all-to-all-done = bf16[64,16,256]{2,1,0:T(8,128)(2,1)S(1)} async-done(((bf16[64,16,256]{2,1,0:T(8,128)(2,1)}), bf16[64,16,256]{2,1,0:T(8,128)(2,1)S(1)}, u32[]{:S(2)}, u32[]{:S(2)}) %all-to-all-start) | async-done | bytes 524320 | tf_op jit(solution)/shard_map/all_to_all | solution.py:108
  48.2 0.3 convolution_convert_fusion.2
  48.5 0.4 convolution_convert_fusion
  49.0 1.9 %collective-permute-start = (bf16[256,2304]{1,0:T(8,128)(2,1)S(1)}, bf16[256,2304]{1,0:T(8,128)(2,1)S(1)}, u32[]{:S(2)}, u32[]{:S(2)}) collective-permute-start(bf16[256,2304]{1,0:T(8,128)(2,1)S(1)} %pad_maximum_fusion), channel_id=1, source_target_pairs={{0,64},{64,0},{128,192},{192,128},{256,320},{320,256},{384,448},{4... | collective-permute-start | bytes 3538952 | tf_op jit(solution)/shard_map/ppermute | solution.py:150
  50.9 0.3 fusion.12
  51.2 0.4 fusion.8
  51.6 2.1 %collective-permute-done = bf16[256,2304]{1,0:T(8,128)(2,1)S(1)} collective-permute-done((bf16[256,2304]{1,0:T(8,128)(2,1)S(1)}, bf16[256,2304]{1,0:T(8,128)(2,1)S(1)}, u32[]{:S(2)}, u32[]{:S(2)}) %collective-permute-start) | collective-permute-done | bytes 1179680 | tf_op jit(solution)/shard_map/ppermute | solution.py:150
  53.7 0.3 fusion.2
  54.0 38.4 %all_to_all.20 = bf16[8,32,2304]{2,1,0:T(8,128)(2,1)S(1)} all-to-all(bf16[8,32,2304]{2,1,0:T(8,128)(2,1)S(1)} %bitcast.57), channel_id=1, replica_groups={{0,128,256,384,512,640,768,896},{64,192,320,448,576,704,832,960},{1,129..., dimensions={0} | all-to-all | bytes 2359296 | tf_op jit(solution)/shard_map/all_to_all | solution.py:111
  92.5 0.7 multiply_convert_fusion
  93.2 0.9 broadcast_in_dim.12
  94.1 3.7 %all-to-all-start.2 = ((bf16[8,32,1536]{2,1,0:T(8,128)(2,1)}), bf16[8,32,1536]{2,1,0:T(8,128)(2,1)S(1)}, u32[]{:S(2)}, u32[]{:S(2)}) async-start(bf16[8,32,1536]{2,1,0:T(8,128)(2,1)} %broadcast_in_dim.12), calls=%async_computation.2 | async-start | bytes 1572864 | tf_op jit(solution)/shard_map/all_to_all | solution.py:111
  97.8 32.6 %all_gather.3 = bf16[512,768]{1,0:T(8,128)(2,1)S(1)} all-gather(bf16[32,768]{1,0:T(8,128)(2,1)S(1)} %copy-done.8), channel_id=1, replica_groups=mesh['expert'=16,'fsdp'=64] {'expert'}, dimensions={0}, use_global_device_ids=true | all-gather | bytes 835584 | tf_op jit(solution)/shard_map/all_gather | solution.py:168
  130.5 2.2 %collective-permute-start.1 = (bf16[256,1536]{1,0:T(8,128)(2,1)S(1)}, bf16[256,1536]{1,0:T(8,128)(2,1)}, u32[]{:S(2)}, u32[]{:S(2)}) collective-permute-start(bf16[256,1536]{1,0:T(8,128)(2,1)S(1)} %bitcast.54), channel_id=1, source_target_pairs={{0,64},{64,0},{128,192},{192,128},{256,320},{320,256},{384,448},{4... | collective-permute-start | bytes 2359304 | tf_op jit(solution)/shard_map/ppermute | solution.py:170
  132.7 0.4 fusion.4
  133.1 0.4 convolution_convert_fusion.5
  133.5 1.3 collective-permute-done.1
  134.8 1.5 broadcast_select_fusion.1
  136.3 0.8 pad_maximum_fusion.1
  137.2 5.2 %all-to-all-start.3 = ((bf16[64,16,256]{2,1,0:T(8,128)(2,1)}), bf16[64,16,256]{2,1,0:T(8,128)(2,1)S(1)}, u32[]{:S(2)}, u32[]{:S(2)}) async-start(bf16[64,16,256]{2,1,0:T(8,128)(2,1)} %pad_maximum_fusion.1), calls=%async_computation.3 | async-start | bytes 1048576 | tf_op jit(solution)/shard_map/all_to_all | solution.py:108
  142.4 1.2 fusion.3
  143.6 0.4 fusion.17
  144.0 0.5 copy-done.7
  144.5 2.4 %fusion.1 = bf16[1,256,1536]{2,1,0:T(8,128)(2,1)} fusion(f32[256,1536]{1,0:T(8,128)S(1)} %fusion.17, bf16[256,256]{1,0:T(8,128)(2,1)S(1)} %bitcast.61, bf16[256,1536]{1,0:T(8,128)(2,1)} %collective-permute-done.1), kind=kOutput, calls=%fused_computation.3 | convolution fusion | flops 202113024 | bytes 3276800 | tf_op jit(solution)/shard_map/dot_general | solution.py:14
  146.9 15.4 %all-to-all-done.3.refs_1_ = bf16[64,16,256]{2,1,0:T(8,128)(2,1)S(1)} async-done(((bf16[64,16,256]{2,1,0:T(8,128)(2,1)}), bf16[64,16,256]{2,1,0:T(8,128)(2,1)S(1)}, u32[]{:S(2)}, u32[]{:S(2)}) %all-to-all-start.3) | async-done | bytes 524320 | tf_op jit(solution)/shard_map/all_to_all | solution.py:108
  162.3 0.9 shard_map.94
  (22 shorter events, 0.4 us)
Async XLA Ops:
  0.6 47.9 %copy-start = (bf16[1,256,1536]{2,1,0:T(8,128)(2,1)S(1)}, bf16[1,256,1536]{2,1,0:T(8,128)(2,1)}, u32[]{:S(2)}) copy-start(bf16[1,256,1536]{2,1,0:T(8,128)(2,1)} %param.7) | copy-start | bytes 2359300
  2.2 0.7 copy-start.1
  3.0 0.7 copy-start.2
  5.4 42.7 %copy-start.3 = (bf16[1,768,256]{2,1,0:T(8,128)(2,1)S(1)}, bf16[1,768,256]{2,1,0:T(8,128)(2,1)}, u32[]{:S(2)}) copy-start(bf16[1,768,256]{2,1,0:T(8,128)(2,1)} %param.8) | copy-start | bytes 1179652
  5.4 42.6 %all-to-all-start = ((bf16[64,16,256]{2,1,0:T(8,128)(2,1)}), bf16[64,16,256]{2,1,0:T(8,128)(2,1)S(1)}, u32[]{:S(2)}, u32[]{:S(2)}) async-start(bf16[64,16,256]{2,1,0:T(8,128)(2,1)} %get-tuple-element.11), calls=%async_computation | async-start | bytes 1048576 | tf_op jit(solution)/shard_map/all_to_all | solution.py:108
  48.1 0.8 copy-start.6
  48.2 3.0 %copy-start.4 = (bf16[8,1,32,256]{3,2,1,0:T(8,128)(2,1)}, bf16[8,1,32,256]{3,2,1,0:T(8,128)(2,1)S(1)}, u32[]{:S(2)}) copy-start(bf16[8,1,32,256]{3,2,1,0:T(8,128)(2,1)S(1)} %get-tuple-element.27) | copy-start | bytes 393220
  49.0 4.7 %collective-permute-start = (bf16[256,2304]{1,0:T(8,128)(2,1)S(1)}, bf16[256,2304]{1,0:T(8,128)(2,1)S(1)}, u32[]{:S(2)}, u32[]{:S(2)}) collective-permute-start(bf16[256,2304]{1,0:T(8,128)(2,1)S(1)} %pad_maximum_fusion), channel_id=1, source_target_pairs={{0,64},{64,0},{128,192},{192,128},{256,320},{320,256},{384,448},{4... | collective-permute-start | bytes 3538952 | tf_op jit(solution)/shard_map/ppermute | solution.py:150
  94.1 3.7 %copy-start.8 = (bf16[32,768]{1,0:T(8,128)(2,1)S(1)}, bf16[32,768]{1,0:T(8,128)(2,1)}, u32[]{:S(2)}) copy-start(bf16[32,768]{1,0:T(8,128)(2,1)} %get-tuple-element.18) | copy-start | bytes 147460
  94.1 36.3 %all-to-all-start.2 = ((bf16[8,32,1536]{2,1,0:T(8,128)(2,1)}), bf16[8,32,1536]{2,1,0:T(8,128)(2,1)S(1)}, u32[]{:S(2)}, u32[]{:S(2)}) async-start(bf16[8,32,1536]{2,1,0:T(8,128)(2,1)} %broadcast_in_dim.12), calls=%async_computation.2 | async-start | bytes 1572864 | tf_op jit(solution)/shard_map/all_to_all | solution.py:111
  130.5 4.3 %collective-permute-start.1 = (bf16[256,1536]{1,0:T(8,128)(2,1)S(1)}, bf16[256,1536]{1,0:T(8,128)(2,1)}, u32[]{:S(2)}, u32[]{:S(2)}) collective-permute-start(bf16[256,1536]{1,0:T(8,128)(2,1)S(1)} %bitcast.54), channel_id=1, source_target_pairs={{0,64},{64,0},{128,192},{192,128},{256,320},{320,256},{384,448},{4... | collective-permute-start | bytes 2359304 | tf_op jit(solution)/shard_map/ppermute | solution.py:170
  137.2 25.1 %all-to-all-start.3 = ((bf16[64,16,256]{2,1,0:T(8,128)(2,1)}), bf16[64,16,256]{2,1,0:T(8,128)(2,1)S(1)}, u32[]{:S(2)}, u32[]{:S(2)}) async-start(bf16[64,16,256]{2,1,0:T(8,128)(2,1)} %pad_maximum_fusion.1), calls=%async_computation.3 | async-start | bytes 1048576 | tf_op jit(solution)/shard_map/all_to_all | solution.py:108
  142.4 1.2 copy-start.5
  143.6 0.9 copy-start.7

commit v3 on v2

--- a/solution.py
+++ b/solution.py
@@ -8,6 +8,7 @@
 PLAIN = (((1,), (0,)), ((), ()))
 LAST = (((1,), (1,)), ((), ()))
 FIRST = (((0,), (0,)), ((), ()))
+UNIT = 32
 
 
 def dot(a, b, dims=PLAIN):
@@ -76,14 +77,125 @@
     grad_ref[...] = dot(maps_ref[3 * count : 4 * count, :], grad).astype(jnp.bfloat16)
 
 
-def call(kernel, out_shape, flops, *operands):
+def unit_order(me, chips):
+    chip, core = lax.div(me, 2), lax.rem(me, 2)
+    sign, twin = 1 - 2 * core, 1 - core
+    opposite = 2 * lax.rem(chip + 4, chips)
+    order = [2 * chip + twin]
+    for distance in (1, 2, 3):
+        at = 2 * lax.rem(chip - sign * distance + chips, chips)
+        order += [at + core, at + twin]
+    order += [2 * chip + core, opposite + core]
+    for distance in (1, 2, 3):
+        at = 2 * lax.rem(chip + sign * distance + chips, chips)
+        order += [at + twin, at + core]
+    return order + [opposite + twin]
+
+
+def sums_kernel(capacity, me_ref, got_ref, twin_got_ref, in_ref, twin_in_ref, out_ref, twin_out_ref,
+                rows_ref, back_ref, own_ref, far_ref, near_ref, middle_ref, third_ref,
+                twin_rows, twin_back):
+    experts, _, width = got_ref.shape
+    units = rows_ref.shape[0] // UNIT
+    blocks = UNIT // capacity
+    for k, unit in enumerate(unit_order(me_ref[0], units // 2)):
+        here = slice(k * UNIT, (k + 1) * UNIT)
+        for source, row_to, back_to in (
+            (got_ref, rows_ref, back_ref),
+            (twin_got_ref, twin_rows, twin_back),
+        ):
+            block = source[pl.ds(unit * blocks, blocks)].astype(jnp.float32)
+            row_to[here, :] = block[:, :capacity].reshape(UNIT, width).astype(jnp.bfloat16)
+            back_to[here, :] = block[:, capacity:].reshape(UNIT, width).astype(jnp.bfloat16)
+    part = slice(7 * UNIT, 15 * UNIT)
+    ff = out_ref.shape[0]
+
+    def put(columns, total):
+        own_ref[:, columns] = total[:UNIT]
+        far_ref[:, columns] = total[UNIT : 2 * UNIT].astype(jnp.bfloat16)
+        near_ref[:, columns] = total[2 * UNIT : 4 * UNIT].astype(jnp.bfloat16)
+        middle_ref[:, columns] = total[4 * UNIT : 6 * UNIT]
+        third_ref[:, columns] = total[6 * UNIT :].astype(jnp.bfloat16)
+
+    step = ff // 2
+    for start in range(0, 2 * ff, step):
+        columns = slice(start, start + step)
+        put(
+            columns,
+            dot(rows_ref[part, :], in_ref[:, columns]) + dot(twin_rows[part, :], twin_in_ref[:, columns]),
+        )
+    for start in range(0, ff, step):
+        some = slice(start, start + step)
+        put(
+            slice(2 * ff + start, 2 * ff + start + step),
+            dot(back_ref[part, :], out_ref[some, :], LAST)
+            + dot(twin_back[part, :], twin_out_ref[some, :], LAST),
+        )
+
+
+def gateway_kernel(middle_ref, third_ref, far_ref, sum_ref):
+    total = middle_ref[...] + third_ref[...].astype(jnp.float32)
+    sum_ref[:UNIT, :] = total[:UNIT].astype(jnp.bfloat16)
+    sum_ref[UNIT:, :] = (total[UNIT:] + far_ref[...].astype(jnp.float32)).astype(jnp.bfloat16)
+
+
+def twin_part_kernel(near_ref, passed_ref, sum_ref):
+    sum_ref[...] = near_ref[:UNIT, :].astype(jnp.float32) + passed_ref[:UNIT, :].astype(jnp.float32)
+
+
+def swish_kernel(own_ref, near_ref, passed_ref, twin_ref, mid_ref):
+    share = (
+        own_ref[...]
+        + near_ref[UNIT:, :].astype(jnp.float32)
+        + passed_ref[UNIT:, :].astype(jnp.float32)
+        + twin_ref[...]
+    )
+    ff = share.shape[1] // 3
+    gate_part, up_part, back_hidden = share[:, :ff], share[:, ff : 2 * ff], share[:, 2 * ff :]
+    sigma = jax.nn.sigmoid(gate_part)
+    activated = gate_part * sigma
+    slope = sigma + gate_part * sigma * (1.0 - sigma)
+    mid_ref[:, :ff] = (activated * up_part).astype(jnp.bfloat16)
+    mid_ref[:, ff : 2 * ff] = (back_hidden * up_part * slope).astype(jnp.bfloat16)
+    mid_ref[:, 2 * ff :] = (back_hidden * activated).astype(jnp.bfloat16)
+
+
+def results_kernel(capacity, me_ref, in_ref, out_ref, *refs):
+    parts, (back_ref, full_ref) = refs[:-2], refs[-2:]
+    at = 0
+    for part in parts:
+        count = part.shape[0]
+        full_ref[at : at + count, :] = part[...]
+        at += count
+    ff, width = out_ref.shape
+    out = dot(full_ref[:, :ff], out_ref[...])
+    grad = dot(full_ref[:, ff:], in_ref[...], LAST)
+    units = full_ref.shape[0] // UNIT
+    blocks = UNIT // capacity
+    for k, unit in enumerate(unit_order(me_ref[0], units // 2)):
+        here = slice(k * UNIT, (k + 1) * UNIT)
+        back_ref[pl.ds(unit * blocks, blocks)] = jnp.concatenate(
+            [
+                out[here].reshape(blocks, capacity, width),
+                grad[here].reshape(blocks, capacity, width),
+            ],
+            axis=1,
+        ).astype(jnp.bfloat16)
+
+
+def call(kernel, out_shape, flops, *operands, scratch=(), scalar_first=False):
     def size(a):
         return a.size * a.dtype.itemsize
 
     moved = sum(map(size, operands)) + sum(map(size, jax.tree.leaves(out_shape)))
+    specs = [pl.BlockSpec(memory_space=pltpu.VMEM) for _ in operands]
+    if scalar_first:
+        specs[0] = pl.BlockSpec(memory_space=pltpu.SMEM)
     return pl.pallas_call(
         kernel,
         out_shape=out_shape,
+        in_specs=specs,
+        scratch_shapes=scratch,
         compiler_params=pltpu.CompilerParams(vmem_limit_bytes=40 * 2**20),
         cost_estimate=pl.CostEstimate(flops=flops, bytes_accessed=moved, transcendentals=0),
     )(*operands)
@@ -97,32 +209,24 @@
     ff = output_weight.shape[1]
     capacity = min(block_tok, 2 * block_tok * route_count // experts)
     rows = experts * capacity
-    piece = rows // (2 * chips)
-    core = lax.axis_index("expert") & 1
     weight_in = input_weight[0]
     weight_out = output_weight[0]
-    swap = [(d, d ^ 1) for d in range(2 * chips)]
-    same_core = [[2 * i + c for i in range(chips)] for c in range(2)]
+    me = lax.axis_index("expert").reshape(1)
+    bf16, f32 = jnp.bfloat16, jnp.float32
 
     def exchange(values):
         return lax.all_to_all(values, "fsdp", split_axis=0, concat_axis=0, tiled=True)
 
-    def exchange_chips(values):
-        return lax.all_to_all(
-            values, "expert", split_axis=0, concat_axis=0, tiled=True, axis_index_groups=same_core
-        )
-
-    def half(values, which):
-        pieces = values.reshape(chips, 2, piece, width)
-        return lax.dynamic_index_in_dim(pieces, which, 1, keepdims=False).reshape(-1, width)
-
-    def both(mine, other):
-        mine = mine.reshape(chips, piece, -1)
-        other = other.reshape(chips, piece, -1)
-        first = core == 0
-        return jnp.stack(
-            [jnp.where(first, mine, other), jnp.where(first, other, mine)], axis=1
-        ).reshape(rows, -1)
+    def swap(values):
+        return lax.ppermute(values, "expert", [(d, d ^ 1) for d in range(2 * chips)])
+
+    def along(values, distance):
+        up = [(2 * i, 2 * ((i + distance) % chips)) for i in range(chips)]
+        down = [(2 * i + 1, 2 * ((i - distance) % chips) + 1) for i in range(chips)]
+        return lax.ppermute(values, "expert", up + down)
+
+    def array(count, columns, dtype):
+        return jax.ShapeDtypeStruct((count, columns), dtype)
 
     sent, maps = call(
         lambda *refs: dispatch_kernel(capacity, *refs),
@@ -136,53 +240,74 @@
         tokens,
         cotangent,
     )
-    got = exchange(sent)
-    routed_rows = got[:, :capacity].reshape(rows, width)
-    routed_back = got[:, capacity:].reshape(rows, width)
-    mine_rows, other_rows = half(routed_rows, core), half(routed_rows, 1 - core)
-    mine_back, other_back = half(routed_back, core), half(routed_back, 1 - core)
-
-    def partial_sums(some_rows, some_back):
-        return jnp.concatenate(
-            [dot(some_rows, weight_in), dot(some_back, weight_out, LAST)], axis=1
-        )
-
-    arrived = lax.ppermute(
-        partial_sums(other_rows, other_back).astype(jnp.bfloat16), "expert", swap
-    )
-    chip_sum = partial_sums(mine_rows, mine_back) + arrived.astype(jnp.float32)
-    pieces = exchange_chips(chip_sum.astype(jnp.bfloat16).reshape(chips, piece, 3 * ff))
-    share = jnp.sum(pieces.astype(jnp.float32), axis=0)
-    gate_part, up_part, back_hidden = share[:, :ff], share[:, ff : 2 * ff], share[:, 2 * ff :]
-    sigma = jax.nn.sigmoid(gate_part)
-    activated = gate_part * sigma
-    slope = sigma + gate_part * sigma * (1.0 - sigma)
-    grad_share = jnp.concatenate(
-        [back_hidden * up_part * slope, back_hidden * activated], axis=1
-    ).astype(jnp.bfloat16)
-    hidden_share = (activated * up_part).astype(jnp.bfloat16)
-
-    mine_grad = exchange_chips(
-        jnp.broadcast_to(grad_share[None], (chips, *grad_share.shape))
-    ).reshape(-1, 2 * ff)
-    hidden = lax.all_gather(hidden_share, "expert", axis=0, tiled=True)
-    mine_grad, hidden = lax.optimization_barrier((mine_grad, hidden))
-    other_grad = lax.ppermute(mine_grad, "expert", swap)
-    out_rows = dot(hidden, weight_out).astype(jnp.bfloat16)
-    route_grad = both(
-        dot(mine_grad, weight_in, LAST).astype(jnp.bfloat16),
-        dot(other_grad, weight_in, LAST).astype(jnp.bfloat16),
-    )
-    back = jnp.concatenate(
-        [out_rows.reshape(experts, capacity, width), route_grad.reshape(experts, capacity, width)],
-        axis=1,
+    sent, *ready = lax.optimization_barrier((sent, weight_in, weight_out))
+    got, twin_in, twin_out = lax.optimization_barrier((exchange(sent), *map(swap, ready)))
+    all_columns = 3 * ff
+    routed_rows, routed_back, own, far, near, middle, third = call(
+        lambda *refs: sums_kernel(capacity, *refs),
+        (
+            array(rows, width, bf16),
+            array(rows, width, bf16),
+            array(UNIT, all_columns, f32),
+            array(UNIT, all_columns, bf16),
+            array(2 * UNIT, all_columns, bf16),
+            array(2 * UNIT, all_columns, f32),
+            array(2 * UNIT, all_columns, bf16),
+        ),
+        4 * 8 * UNIT * width * all_columns,
+        me,
+        got,
+        swap(got),
+        weight_in,
+        twin_in,
+        weight_out,
+        twin_out,
+        scratch=[pltpu.VMEM((rows, width), bf16), pltpu.VMEM((rows, width), bf16)],
+        scalar_first=True,
+    )
+    third = along(third, 1)
+    far = along(far, 2)
+    near = along(near, 1)
+    passed = along(
+        call(gateway_kernel, array(2 * UNIT, all_columns, bf16), rows * ff, middle, third, far), 2
+    )
+    twin_part = swap(call(twin_part_kernel, array(UNIT, all_columns, f32), rows * ff, near, passed))
+    mid = call(
+        swish_kernel, array(UNIT, all_columns, bf16), rows * ff, own, near, passed, twin_part
+    )
+
+    twin_mid = swap(mid)
+    chip_mid = jnp.concatenate([mid, twin_mid], axis=0)
+    second = along(chip_mid, 2)
+    first = along(chip_mid, 1)
+    third = along(second, 1)
+    far = along(second[:UNIT], 2)
+    back, full = call(
+        lambda *refs: results_kernel(capacity, *refs),
+        (
+            jax.ShapeDtypeStruct((experts, 2 * capacity, width), bf16),
+            array(rows, all_columns, bf16),
+        ),
+        2 * rows * width * all_columns,
+        me,
+        weight_in,
+        weight_out,
+        twin_mid,
+        first,
+        second,
+        third,
+        mid,
+        far,
+        swap(first),
+        swap(second),
+        swap(third),
+        swap(far),
+        scalar_first=True,
     )
     home = exchange(back)
-    grad_input = (
-        (dot(mine_rows, mine_grad, FIRST) + dot(other_rows, other_grad, FIRST))
-        .astype(jnp.bfloat16)
-    )[None]
-    grad_output = dot(hidden, routed_back, FIRST).astype(jnp.bfloat16)[None]
+    hidden, grad_pre = full[:, :ff], full[:, ff:]
+    grad_input = dot(routed_rows, grad_pre, FIRST).astype(bf16)[None]
+    grad_output = dot(hidden, routed_back, FIRST).astype(bf16)[None]
     mixed, grad_tokens = call(
         lambda *refs: combine_kernel(capacity, *refs),
         (

time: 164 us -> 149 us (0.909)
  the two profiles are of different devices: /device:TPU:32 before, /device:TPU:34 now
where the time goes in v3:
time: 149 us; the launch traced here: 148 us
  starting transfers between devices  79.9 us (54%)
  waiting for transfers between devices  54.1 us (36%)
  Pallas kernels  5.46 us (4%)
  local copies, waits for them, and re-layouts  5.11 us (3%)
  matrix products  2.64 us (2%)
    ppermute x8, starting transfers between devices, along(): return lax.ppermute(values, 'expert', up + down)  32.7 us
    all_to_all x2, waiting for transfers between devices, exchange(): lax.all_to_all(values, 'fsdp', split_axis=0, concat_axis=0, tiled=True)  30.8 us
    all_to_all x2, starting transfers between devices, exchange(): lax.all_to_all(values, 'fsdp', split_axis=0, concat_axis=0, tiled=True)  28.3 us
    ppermute x9, starting transfers between devices, swap(): lax.ppermute(values, 'expert', [(d, d ^ 1) for d in range(2 * chips)])  18.9 us
    ppermute x8, waiting for transfers between devices, along(): return lax.ppermute(values, 'expert', up + down)  16.1 us
    ppermute x9, waiting for transfers between devices, swap(): lax.ppermute(values, 'expert', [(d, d ^ 1) for d in range(2 * chips)])  7.14 us
    pallas_call x7, Pallas kernels, call(): pl.pallas_call(kernel, out_shape=out_shape, in_specs=specs, scratch_shape...  5.46 us
    unnamed x14, local copies, waits for them, and re-layouts  5.1 us
  transfers between devices with their start and end apart: 19, of which 11 were waited for; matrix products, arithmetic and copies ran while one was open for 2% of the time, Pallas kernels for 0%

profile of v3, /device:TPU:34, one launch (start us, length us, event | category | flops | bytes accessed | tf_op | source)
XLA Modules:
  0.0 148.1 jit_solution(14592598923699286009)
XLA Ops:
  3.6 1.8 %shard_map.93 = (bf16[64,16,256]{2,1,0:T(8,128)(2,1)}, bf16[128,512]{1,0:T(8,128)(2,1)S(1)}) custom-call(s32[32,8]{1,0:T(8,128)S(1)} %copy.10.refs_0_, f32[32,8]{1,0:T(8,128)S(1)} %copy.11.refs_1_, bf16[32,256]{1,0:T(8,128)(2,1)S(1)} %copy-done.4, bf16[32,256]{1,0:T(8,128)(2,1)S(1)} %copy-done.5), custom_call_target="tpu_custom_call" | custom-call | flops 41943040 | bytes 690176 | tf_op jit(solution)/shard_map/pallas_call | solution.py:194
  5.4 23.1 %all-to-all-start = ((bf16[64,16,256]{2,1,0:T(8,128)(2,1)}), bf16[64,16,256]{2,1,0:T(8,128)(2,1)S(1)}, u32[]{:S(2)}, u32[]{:S(2)}) async-start(bf16[64,16,256]{2,1,0:T(8,128)(2,1)} %get-tuple-element.25), calls=%async_computation | async-start | bytes 1048576 | tf_op jit(solution)/shard_map/all_to_all | solution.py:218
  28.4 1.9 %collective-permute-start = (bf16[256,1536]{1,0:T(8,128)(2,1)}, bf16[256,1536]{1,0:T(8,128)(2,1)S(1)}, u32[]{:S(2)}, u32[]{:S(2)}) collective-permute-start(bf16[256,1536]{1,0:T(8,128)(2,1)} %bitcast.9), channel_id=1, source_target_pairs={{0,64},{64,0},{128,192},{192,128},{256,320},{320,256},{384,448},{4... | collective-permute-start | bytes 2359304 | tf_op jit(solution)/shard_map/ppermute | solution.py:221
  30.4 2.4 %collective-permute-start.1 = (bf16[768,256]{1,0:T(8,128)(2,1)}, bf16[768,256]{1,0:T(8,128)(2,1)S(1)}, u32[]{:S(2)}, u32[]{:S(2)}) collective-permute-start(bf16[768,256]{1,0:T(8,128)(2,1)} %bitcast.12), channel_id=1, source_target_pairs={{0,64},{64,0},{128,192},{192,128},{256,320},{320,256},{384,448},{4... | collective-permute-start | bytes 1179656 | tf_op jit(solution)/shard_map/ppermute | solution.py:221
  32.8 1.5 %collective-permute-done.1.refs_6_ = bf16[768,256]{1,0:T(8,128)(2,1)S(1)} collective-permute-done((bf16[768,256]{1,0:T(8,128)(2,1)}, bf16[768,256]{1,0:T(8,128)(2,1)S(1)}, u32[]{:S(2)}, u32[]{:S(2)}) %collective-permute-start.1) | collective-permute-done | bytes 393248 | tf_op jit(solution)/shard_map/ppermute | solution.py:221
  34.3 13.5 %all-to-all-done.refs_1_ = bf16[64,16,256]{2,1,0:T(8,128)(2,1)S(1)} async-done(((bf16[64,16,256]{2,1,0:T(8,128)(2,1)}), bf16[64,16,256]{2,1,0:T(8,128)(2,1)S(1)}, u32[]{:S(2)}, u32[]{:S(2)}) %all-to-all-start) | async-done | bytes 524320 | tf_op jit(solution)/shard_map/all_to_all | solution.py:218
  47.8 1.9 %collective-permute-start.2 = (bf16[64,16,256]{2,1,0:T(8,128)(2,1)S(1)}, bf16[64,16,256]{2,1,0:T(8,128)(2,1)S(1)}, u32[]{:S(2)}, u32[]{:S(2)}) collective-permute-start(bf16[64,16,256]{2,1,0:T(8,128)(2,1)S(1)} %all-to-all-done.refs_1_), channel_id=1, source_target_pairs={{0,64},{64,0},{128,192},{192,128},{256,320},{320,256},{384,448},{4... | collective-permute-start | bytes 1572872 | tf_op jit(solution)/shard_map/ppermute | solution.py:221
  49.8 1.9 %collective-permute-done.2.refs_2_ = bf16[64,16,256]{2,1,0:T(8,128)(2,1)S(1)} collective-permute-done((bf16[64,16,256]{2,1,0:T(8,128)(2,1)S(1)}, bf16[64,16,256]{2,1,0:T(8,128)(2,1)S(1)}, u32[]{:S(2)}, u32[]{:S(2)}) %collective-permute-start.2) | collective-permute-done | bytes 524320 | tf_op jit(solution)/shard_map/ppermute | solution.py:221
  54.8 3.5 %collective-permute-start.4 = (bf16[64,2304]{1,0:T(8,128)(2,1)S(1)}, bf16[64,2304]{1,0:T(8,128)(2,1)S(1)}, u32[]{:S(2)}, u32[]{:S(2)}) collective-permute-start(bf16[64,2304]{1,0:T(8,128)(2,1)S(1)} %get-tuple-element.34), channel_id=1, source_target_pairs={{0,128},{128,256},{256,384},{384,512},{512,640},{640,768},{768,896... | collective-permute-start | bytes 884744 | tf_op jit(solution)/shard_map/ppermute | solution.py:226
  58.3 5.5 %collective-permute-start.5 = (bf16[32,2304]{1,0:T(8,128)(2,1)S(1)}, bf16[32,2304]{1,0:T(8,128)(2,1)S(1)}, u32[]{:S(2)}, u32[]{:S(2)}) collective-permute-start(bf16[32,2304]{1,0:T(8,128)(2,1)S(1)} %get-tuple-element.35), channel_id=1, source_target_pairs={{0,256},{128,384},{256,512},{384,640},{512,768},{640,896},{768,0},... | collective-permute-start | bytes 442376 | tf_op jit(solution)/shard_map/ppermute | solution.py:226
  63.8 2.5 %collective-permute-start.3 = (bf16[64,2304]{1,0:T(8,128)(2,1)S(1)}, bf16[64,2304]{1,0:T(8,128)(2,1)S(1)}, u32[]{:S(2)}, u32[]{:S(2)}) collective-permute-start(bf16[64,2304]{1,0:T(8,128)(2,1)S(1)} %get-tuple-element.32), channel_id=1, source_target_pairs={{0,128},{128,256},{256,384},{384,512},{512,640},{640,768},{768,896... | collective-permute-start | bytes 884744 | tf_op jit(solution)/shard_map/ppermute | solution.py:226
  66.4 2.6 %collective-permute-done.5.far_ref = bf16[32,2304]{1,0:T(8,128)(2,1)S(1)} collective-permute-done((bf16[32,2304]{1,0:T(8,128)(2,1)S(1)}, bf16[32,2304]{1,0:T(8,128)(2,1)S(1)}, u32[]{:S(2)}, u32[]{:S(2)}) %collective-permute-start.5) | collective-permute-done | bytes 147488 | tf_op jit(solution)/shard_map/ppermute | solution.py:226
  69.1 3.1 %collective-permute-start.6 = (bf16[64,2304]{1,0:T(8,128)(2,1)S(1)}, bf16[64,2304]{1,0:T(8,128)(2,1)S(1)}, u32[]{:S(2)}, u32[]{:S(2)}) collective-permute-start(bf16[64,2304]{1,0:T(8,128)(2,1)S(1)} %shard_map.95), channel_id=1, source_target_pairs={{0,256},{128,384},{256,512},{384,640},{512,768},{640,896},{768,0},... | collective-permute-start | bytes 884744 | tf_op jit(solution)/shard_map/ppermute | solution.py:226
  72.5 9.9 %collective-permute-done.6.passed_ref = bf16[64,2304]{1,0:T(8,128)(2,1)S(1)} collective-permute-done((bf16[64,2304]{1,0:T(8,128)(2,1)S(1)}, bf16[64,2304]{1,0:T(8,128)(2,1)S(1)}, u32[]{:S(2)}, u32[]{:S(2)}) %collective-permute-start.6) | collective-permute-done | bytes 294944 | tf_op jit(solution)/shard_map/ppermute | solution.py:226
  82.4 1.9 %collective-permute-start.7 = (f32[32,2304]{1,0:T(8,128)S(1)}, f32[32,2304]{1,0:T(8,128)S(1)}, u32[]{:S(2)}, u32[]{:S(2)}) collective-permute-start(f32[32,2304]{1,0:T(8,128)S(1)} %shard_map.96), channel_id=1, source_target_pairs={{0,64},{64,0},{128,192},{192,128},{256,320},{320,256},{384,448},{4... | collective-permute-start | bytes 884744 | tf_op jit(solution)/shard_map/ppermute | solution.py:221
  84.3 1.5 %collective-permute-done.7.twin_ref = f32[32,2304]{1,0:T(8,128)S(1)} collective-permute-done((f32[32,2304]{1,0:T(8,128)S(1)}, f32[32,2304]{1,0:T(8,128)S(1)}, u32[]{:S(2)}, u32[]{:S(2)}) %collective-permute-start.7) | collective-permute-done | bytes 294944 | tf_op jit(solution)/shard_map/ppermute | solution.py:221
  86.0 2.0 %collective-permute-start.8 = (bf16[32,2304]{1,0:T(8,128)(2,1)S(1)}, bf16[32,2304]{1,0:T(8,128)(2,1)S(1)}, u32[]{:S(2)}, u32[]{:S(2)}) collective-permute-start(bf16[32,2304]{1,0:T(8,128)(2,1)S(1)} %shard_map.97.refs_7_), channel_id=1, source_target_pairs={{0,64},{64,0},{128,192},{192,128},{256,320},{320,256},{384,448},{4... | collective-permute-start | bytes 442376 | tf_op jit(solution)/shard_map/ppermute | solution.py:221
  88.0 1.2 collective-permute-done.8.refs_3_
  89.3 1.9 %collective-permute-start.10 = (bf16[64,2304]{1,0:T(8,128)(2,1)S(1)}, bf16[64,2304]{1,0:T(8,128)(2,1)S(1)}, u32[]{:S(2)}, u32[]{:S(2)}) collective-permute-start(bf16[64,2304]{1,0:T(8,128)(2,1)S(1)} %pad_maximum_fusion), channel_id=1, source_target_pairs={{0,256},{128,384},{256,512},{384,640},{512,768},{640,896},{768,0},... | collective-permute-start | bytes 884744 | tf_op jit(solution)/shard_map/ppermute | solution.py:226
  91.2 6.7 %collective-permute-start.9 = (bf16[64,2304]{1,0:T(8,128)(2,1)S(1)}, bf16[64,2304]{1,0:T(8,128)(2,1)S(1)}, u32[]{:S(2)}, u32[]{:S(2)}) collective-permute-start(bf16[64,2304]{1,0:T(8,128)(2,1)S(1)} %pad_maximum_fusion), channel_id=1, source_target_pairs={{0,128},{128,256},{256,384},{384,512},{512,640},{640,768},{768,896... | collective-permute-start | bytes 884744 | tf_op jit(solution)/shard_map/ppermute | solution.py:226
  97.9 3.3 %collective-permute-done.10.refs_5_ = bf16[64,2304]{1,0:T(8,128)(2,1)S(1)} collective-permute-done((bf16[64,2304]{1,0:T(8,128)(2,1)S(1)}, bf16[64,2304]{1,0:T(8,128)(2,1)S(1)}, u32[]{:S(2)}, u32[]{:S(2)}) %collective-permute-start.10) | collective-permute-done | bytes 294944 | tf_op jit(solution)/shard_map/ppermute | solution.py:226
  101.3 2.8 %collective-permute-start.11 = (bf16[64,2304]{1,0:T(8,128)(2,1)S(1)}, bf16[64,2304]{1,0:T(8,128)(2,1)S(1)}, u32[]{:S(2)}, u32[]{:S(2)}) collective-permute-start(bf16[64,2304]{1,0:T(8,128)(2,1)S(1)} %collective-permute-done.10.refs_5_), channel_id=1, source_target_pairs={{0,128},{128,256},{256,384},{384,512},{512,640},{640,768},{768,896... | collective-permute-start | bytes 884744 | tf_op jit(solution)/shard_map/ppermute | solution.py:226
  104.1 6.6 %collective-permute-start.12 = (bf16[32,2304]{1,0:T(8,128)(2,1)S(1)}, bf16[32,2304]{1,0:T(8,128)(2,1)S(1)}, u32[]{:S(2)}, u32[]{:S(2)}) collective-permute-start(bf16[32,2304]{1,0:T(8,128)(2,1)S(1)} %slice.12), channel_id=1, source_target_pairs={{0,256},{128,384},{256,512},{384,640},{512,768},{640,896},{768,0},... | collective-permute-start | bytes 442376 | tf_op jit(solution)/shard_map/ppermute | solution.py:226
  110.7 1.9 %collective-permute-start.14 = (bf16[64,2304]{1,0:T(8,128)(2,1)S(1)}, bf16[64,2304]{1,0:T(8,128)(2,1)S(1)}, u32[]{:S(2)}, u32[]{:S(2)}) collective-permute-start(bf16[64,2304]{1,0:T(8,128)(2,1)S(1)} %collective-permute-done.10.refs_5_), channel_id=1, source_target_pairs={{0,64},{64,0},{128,192},{192,128},{256,320},{320,256},{384,448},{4... | collective-permute-start | bytes 884744 | tf_op jit(solution)/shard_map/ppermute | solution.py:221
  112.6 2.4 %collective-permute-start.13 = (bf16[64,2304]{1,0:T(8,128)(2,1)S(1)}, bf16[64,2304]{1,0:T(8,128)(2,1)S(1)}, u32[]{:S(2)}, u32[]{:S(2)}) collective-permute-start(bf16[64,2304]{1,0:T(8,128)(2,1)S(1)} %collective-permute-done.9.refs_4_), channel_id=1, source_target_pairs={{0,64},{64,0},{128,192},{192,128},{256,320},{320,256},{384,448},{4... | collective-permute-start | bytes 884744 | tf_op jit(solution)/shard_map/ppermute | solution.py:221
  115.0 1.9 %collective-permute-start.15 = (bf16[64,2304]{1,0:T(8,128)(2,1)S(1)}, bf16[64,2304]{1,0:T(8,128)(2,1)S(1)}, u32[]{:S(2)}, u32[]{:S(2)}) collective-permute-start(bf16[64,2304]{1,0:T(8,128)(2,1)S(1)} %collective-permute-done.11.refs_6_), channel_id=1, source_target_pairs={{0,64},{64,0},{128,192},{192,128},{256,320},{320,256},{384,448},{4... | collective-permute-start | bytes 884744 | tf_op jit(solution)/shard_map/ppermute | solution.py:221
  117.0 2.4 %collective-permute-start.16 = (bf16[32,2304]{1,0:T(8,128)(2,1)S(1)}, bf16[32,2304]{1,0:T(8,128)(2,1)S(1)}, u32[]{:S(2)}, u32[]{:S(2)}) collective-permute-start(bf16[32,2304]{1,0:T(8,128)(2,1)S(1)} %collective-permute-done.12.refs_8_), channel_id=1, source_target_pairs={{0,64},{64,0},{128,192},{192,128},{256,320},{320,256},{384,448},{4... | collective-permute-start | bytes 442376 | tf_op jit(solution)/shard_map/ppermute | solution.py:221
  120.4 1.6 %shard_map.98 = (bf16[64,16,256]{2,1,0:T(8,128)(2,1)}, bf16[512,2304]{1,0:T(8,128)(2,1)S(1)}) custom-call(s32[1]{0:T(128)} %bitcast.refs_0_, bf16[256,1536]{1,0:T(8,128)(2,1)S(1)} %bitcast.11, bf16[768,256]{1,0:T(8,128)(2,1)S(1)} %bitcast.14, bf16[32,2304]{1,0:T(8,128)(2,1)S(1)} %collective-permute-done.8.refs_3_, ...), custom_call_target="tpu_custom_call" | custom-call | flops 603979776 | bytes 6422532 | tf_op jit(solution)/shard_map/pallas_call | solution.py:194
  122.0 5.2 %all-to-all-start.1 = ((bf16[64,16,256]{2,1,0:T(8,128)(2,1)}), bf16[64,16,256]{2,1,0:T(8,128)(2,1)S(1)}, u32[]{:S(2)}, u32[]{:S(2)}) async-start(bf16[64,16,256]{2,1,0:T(8,128)(2,1)} %get-tuple-element.36), calls=%async_computation.1 | async-start | bytes 1048576 | tf_op jit(solution)/shard_map/all_to_all | solution.py:218
  127.2 1.2 fusion.2
  128.4 1.5 fusion
  129.9 17.3 %all-to-all-done.1.refs_1_ = bf16[64,16,256]{2,1,0:T(8,128)(2,1)S(1)} async-done(((bf16[64,16,256]{2,1,0:T(8,128)(2,1)}), bf16[64,16,256]{2,1,0:T(8,128)(2,1)S(1)}, u32[]{:S(2)}, u32[]{:S(2)}) %all-to-all-start.1) | async-done | bytes 524320 | tf_op jit(solution)/shard_map/all_to_all | solution.py:218
  (31 shorter events, 8.4 us)
Async XLA Ops:
  2.2 0.7 copy-start.4
  2.9 0.7 copy-start.5
  5.4 42.5 %all-to-all-start = ((bf16[64,16,256]{2,1,0:T(8,128)(2,1)}), bf16[64,16,256]{2,1,0:T(8,128)(2,1)S(1)}, u32[]{:S(2)}, u32[]{:S(2)}) async-start(bf16[64,16,256]{2,1,0:T(8,128)(2,1)} %get-tuple-element.25), calls=%async_computation | async-start | bytes 1048576 | tf_op jit(solution)/shard_map/all_to_all | solution.py:218
  28.4 5.9 %collective-permute-start = (bf16[256,1536]{1,0:T(8,128)(2,1)}, bf16[256,1536]{1,0:T(8,128)(2,1)S(1)}, u32[]{:S(2)}, u32[]{:S(2)}) collective-permute-start(bf16[256,1536]{1,0:T(8,128)(2,1)} %bitcast.9), channel_id=1, source_target_pairs={{0,64},{64,0},{128,192},{192,128},{256,320},{320,256},{384,448},{4... | collective-permute-start | bytes 2359304 | tf_op jit(solution)/shard_map/ppermute | solution.py:221
  30.4 4.0 %collective-permute-start.1 = (bf16[768,256]{1,0:T(8,128)(2,1)}, bf16[768,256]{1,0:T(8,128)(2,1)S(1)}, u32[]{:S(2)}, u32[]{:S(2)}) collective-permute-start(bf16[768,256]{1,0:T(8,128)(2,1)} %bitcast.12), channel_id=1, source_target_pairs={{0,64},{64,0},{128,192},{192,128},{256,320},{320,256},{384,448},{4... | collective-permute-start | bytes 1179656 | tf_op jit(solution)/shard_map/ppermute | solution.py:221
  47.8 3.8 %collective-permute-start.2 = (bf16[64,16,256]{2,1,0:T(8,128)(2,1)S(1)}, bf16[64,16,256]{2,1,0:T(8,128)(2,1)S(1)}, u32[]{:S(2)}, u32[]{:S(2)}) collective-permute-start(bf16[64,16,256]{2,1,0:T(8,128)(2,1)S(1)} %all-to-all-done.refs_1_), channel_id=1, source_target_pairs={{0,64},{64,0},{128,192},{192,128},{256,320},{320,256},{384,448},{4... | collective-permute-start | bytes 1572872 | tf_op jit(solution)/shard_map/ppermute | solution.py:221
  51.6 1.1 copy-start
  52.8 1.0 copy-start.2
  54.7 65.6 %copy-start.1 = (bf16[1,256,1536]{2,1,0:T(8,128)(2,1)S(1)}, bf16[1,256,1536]{2,1,0:T(8,128)(2,1)}, u32[]{:S(2)}) copy-start(bf16[1,256,1536]{2,1,0:T(8,128)(2,1)} %param.7) | copy-start | bytes 2359300
  54.7 65.6 %copy-start.3 = (bf16[1,768,256]{2,1,0:T(8,128)(2,1)S(1)}, bf16[1,768,256]{2,1,0:T(8,128)(2,1)}, u32[]{:S(2)}) copy-start(bf16[1,768,256]{2,1,0:T(8,128)(2,1)} %param.8) | copy-start | bytes 1179652
  54.8 14.2 %collective-permute-start.4 = (bf16[64,2304]{1,0:T(8,128)(2,1)S(1)}, bf16[64,2304]{1,0:T(8,128)(2,1)S(1)}, u32[]{:S(2)}, u32[]{:S(2)}) collective-permute-start(bf16[64,2304]{1,0:T(8,128)(2,1)S(1)} %get-tuple-element.34), channel_id=1, source_target_pairs={{0,128},{128,256},{256,384},{384,512},{512,640},{640,768},{768,896... | collective-permute-start | bytes 884744 | tf_op jit(solution)/shard_map/ppermute | solution.py:226
  58.3 10.7 %collective-permute-start.5 = (bf16[32,2304]{1,0:T(8,128)(2,1)S(1)}, bf16[32,2304]{1,0:T(8,128)(2,1)S(1)}, u32[]{:S(2)}, u32[]{:S(2)}) collective-permute-start(bf16[32,2304]{1,0:T(8,128)(2,1)S(1)} %get-tuple-element.35), channel_id=1, source_target_pairs={{0,256},{128,384},{256,512},{384,640},{512,768},{640,896},{768,0},... | collective-permute-start | bytes 442376 | tf_op jit(solution)/shard_map/ppermute | solution.py:226
  63.8 8.6 %collective-permute-start.3 = (bf16[64,2304]{1,0:T(8,128)(2,1)S(1)}, bf16[64,2304]{1,0:T(8,128)(2,1)S(1)}, u32[]{:S(2)}, u32[]{:S(2)}) collective-permute-start(bf16[64,2304]{1,0:T(8,128)(2,1)S(1)} %get-tuple-element.32), channel_id=1, source_target_pairs={{0,128},{128,256},{256,384},{384,512},{512,640},{640,768},{768,896... | collective-permute-start | bytes 884744 | tf_op jit(solution)/shard_map/ppermute | solution.py:226
  69.1 13.3 %collective-permute-start.6 = (bf16[64,2304]{1,0:T(8,128)(2,1)S(1)}, bf16[64,2304]{1,0:T(8,128)(2,1)S(1)}, u32[]{:S(2)}, u32[]{:S(2)}) collective-permute-start(bf16[64,2304]{1,0:T(8,128)(2,1)S(1)} %shard_map.95), channel_id=1, source_target_pairs={{0,256},{128,384},{256,512},{384,640},{512,768},{640,896},{768,0},... | collective-permute-start | bytes 884744 | tf_op jit(solution)/shard_map/ppermute | solution.py:226
  82.4 3.5 %collective-permute-start.7 = (f32[32,2304]{1,0:T(8,128)S(1)}, f32[32,2304]{1,0:T(8,128)S(1)}, u32[]{:S(2)}, u32[]{:S(2)}) collective-permute-start(f32[32,2304]{1,0:T(8,128)S(1)} %shard_map.96), channel_id=1, source_target_pairs={{0,64},{64,0},{128,192},{192,128},{256,320},{320,256},{384,448},{4... | collective-permute-start | bytes 884744 | tf_op jit(solution)/shard_map/ppermute | solution.py:221
  86.0 3.3 %collective-permute-start.8 = (bf16[32,2304]{1,0:T(8,128)(2,1)S(1)}, bf16[32,2304]{1,0:T(8,128)(2,1)S(1)}, u32[]{:S(2)}, u32[]{:S(2)}) collective-permute-start(bf16[32,2304]{1,0:T(8,128)(2,1)S(1)} %shard_map.97.refs_7_), channel_id=1, source_target_pairs={{0,64},{64,0},{128,192},{192,128},{256,320},{320,256},{384,448},{4... | collective-permute-start | bytes 442376 | tf_op jit(solution)/shard_map/ppermute | solution.py:221
  89.3 12.0 %collective-permute-start.10 = (bf16[64,2304]{1,0:T(8,128)(2,1)S(1)}, bf16[64,2304]{1,0:T(8,128)(2,1)S(1)}, u32[]{:S(2)}, u32[]{:S(2)}) collective-permute-start(bf16[64,2304]{1,0:T(8,128)(2,1)S(1)} %pad_maximum_fusion), channel_id=1, source_target_pairs={{0,256},{128,384},{256,512},{384,640},{512,768},{640,896},{768,0},... | collective-permute-start | bytes 884744 | tf_op jit(solution)/shard_map/ppermute | solution.py:226
  91.2 21.4 %collective-permute-start.9 = (bf16[64,2304]{1,0:T(8,128)(2,1)S(1)}, bf16[64,2304]{1,0:T(8,128)(2,1)S(1)}, u32[]{:S(2)}, u32[]{:S(2)}) collective-permute-start(bf16[64,2304]{1,0:T(8,128)(2,1)S(1)} %pad_maximum_fusion), channel_id=1, source_target_pairs={{0,128},{128,256},{256,384},{384,512},{512,640},{640,768},{768,896... | collective-permute-start | bytes 884744 | tf_op jit(solution)/shard_map/ppermute | solution.py:226
  101.3 13.7 %collective-permute-start.11 = (bf16[64,2304]{1,0:T(8,128)(2,1)S(1)}, bf16[64,2304]{1,0:T(8,128)(2,1)S(1)}, u32[]{:S(2)}, u32[]{:S(2)}) collective-permute-start(bf16[64,2304]{1,0:T(8,128)(2,1)S(1)} %collective-permute-done.10.refs_5_), channel_id=1, source_target_pairs={{0,128},{128,256},{256,384},{384,512},{512,640},{640,768},{768,896... | collective-permute-start | bytes 884744 | tf_op jit(solution)/shard_map/ppermute | solution.py:226
  104.1 12.9 %collective-permute-start.12 = (bf16[32,2304]{1,0:T(8,128)(2,1)S(1)}, bf16[32,2304]{1,0:T(8,128)(2,1)S(1)}, u32[]{:S(2)}, u32[]{:S(2)}) collective-permute-start(bf16[32,2304]{1,0:T(8,128)(2,1)S(1)} %slice.12), channel_id=1, source_target_pairs={{0,256},{128,384},{256,512},{384,640},{512,768},{640,896},{768,0},... | collective-permute-start | bytes 442376 | tf_op jit(solution)/shard_map/ppermute | solution.py:226
  110.7 8.7 %collective-permute-start.14 = (bf16[64,2304]{1,0:T(8,128)(2,1)S(1)}, bf16[64,2304]{1,0:T(8,128)(2,1)S(1)}, u32[]{:S(2)}, u32[]{:S(2)}) collective-permute-start(bf16[64,2304]{1,0:T(8,128)(2,1)S(1)} %collective-permute-done.10.refs_5_), channel_id=1, source_target_pairs={{0,64},{64,0},{128,192},{192,128},{256,320},{320,256},{384,448},{4... | collective-permute-start | bytes 884744 | tf_op jit(solution)/shard_map/ppermute | solution.py:221
  112.6 6.8 %collective-permute-start.13 = (bf16[64,2304]{1,0:T(8,128)(2,1)S(1)}, bf16[64,2304]{1,0:T(8,128)(2,1)S(1)}, u32[]{:S(2)}, u32[]{:S(2)}) collective-permute-start(bf16[64,2304]{1,0:T(8,128)(2,1)S(1)} %collective-permute-done.9.refs_4_), channel_id=1, source_target_pairs={{0,64},{64,0},{128,192},{192,128},{256,320},{320,256},{384,448},{4... | collective-permute-start | bytes 884744 | tf_op jit(solution)/shard_map/ppermute | solution.py:221
  115.0 5.3 %collective-permute-start.15 = (bf16[64,2304]{1,0:T(8,128)(2,1)S(1)}, bf16[64,2304]{1,0:T(8,128)(2,1)S(1)}, u32[]{:S(2)}, u32[]{:S(2)}) collective-permute-start(bf16[64,2304]{1,0:T(8,128)(2,1)S(1)} %collective-permute-done.11.refs_6_), channel_id=1, source_target_pairs={{0,64},{64,0},{128,192},{192,128},{256,320},{320,256},{384,448},{4... | collective-permute-start | bytes 884744 | tf_op jit(solution)/shard_map/ppermute | solution.py:221
  117.0 3.4 %collective-permute-start.16 = (bf16[32,2304]{1,0:T(8,128)(2,1)S(1)}, bf16[32,2304]{1,0:T(8,128)(2,1)S(1)}, u32[]{:S(2)}, u32[]{:S(2)}) collective-permute-start(bf16[32,2304]{1,0:T(8,128)(2,1)S(1)} %collective-permute-done.12.refs_8_), channel_id=1, source_target_pairs={{0,64},{64,0},{128,192},{192,128},{256,320},{320,256},{384,448},{4... | collective-permute-start | bytes 442376 | tf_op jit(solution)/shard_map/ppermute | solution.py:221
  122.0 25.1 %all-to-all-start.1 = ((bf16[64,16,256]{2,1,0:T(8,128)(2,1)}), bf16[64,16,256]{2,1,0:T(8,128)(2,1)S(1)}, u32[]{:S(2)}, u32[]{:S(2)}) async-start(bf16[64,16,256]{2,1,0:T(8,128)(2,1)} %get-tuple-element.36), calls=%async_computation.1 | async-start | bytes 1048576 | tf_op jit(solution)/shard_map/all_to_all | solution.py:218

commit v4 on v3

--- a/solution.py
+++ b/solution.py
@@ -23,40 +23,67 @@
     return first, second, third
 
 
-def dispatch_kernel(capacity, routes_ref, gates_ref, tokens_ref, cotangent_ref, sent_ref, maps_ref):
+def dispatch_kernel(capacity, routes_hbm, gates_hbm, tokens_hbm, cotangent_hbm, sent_ref, maps_ref,
+                    routes_ref, gates_ref, tokens_ref, cotangent_ref, arrived):
     experts, _, width = sent_ref.shape
-    count, route_count = routes_ref.shape
-    rows = experts * capacity
-    routes = routes_ref[...]
-    gates = gates_ref[...]
-    lane = lax.broadcasted_iota(jnp.int32, (count, experts), 1)
-    named = jnp.zeros((count, experts), jnp.float32)
-    gate_of = jnp.zeros((count, experts), jnp.float32)
-    for k in range(route_count):
-        hit = routes[:, k : k + 1] == lane
-        named = jnp.where(hit, 1.0, named)
-        gate_of = jnp.where(hit, gates[:, k : k + 1], gate_of)
-    row = lax.broadcasted_iota(jnp.int32, (count, count), 0)
-    column = lax.broadcasted_iota(jnp.int32, (count, count), 1)
-    before = jnp.where(column < row, 1.0, 0.0).astype(jnp.bfloat16)
-    named = named.astype(jnp.bfloat16)
-    slot = dot(before, named).astype(jnp.bfloat16)
-    first_row = lax.broadcasted_iota(jnp.int32, (experts, rows), 0) * capacity
-    at = lax.broadcasted_iota(jnp.int32, (experts, rows), 1)
+    rows, lanes = maps_ref.shape
+    route_count, count = routes_hbm.shape
+    copies = [
+        pltpu.make_async_copy(source, target, arrived.at[i])
+        for i, (source, target) in enumerate(
+            (
+                (routes_hbm, routes_ref),
+                (gates_hbm, gates_ref),
+                (tokens_hbm, tokens_ref.at[3 * count : 4 * count]),
+                (cotangent_hbm, cotangent_ref.at[3 * count : 4 * count]),
+            )
+        )
+    ]
+    for copy in copies:
+        copy.start()
+    tokens_ref[: 3 * count, :] = jnp.zeros((3 * count, width), jnp.bfloat16)
+    cotangent_ref[: 3 * count, :] = jnp.zeros((3 * count, width), jnp.bfloat16)
+    token = lax.broadcasted_iota(jnp.int32, (count, lanes), 0)
+    lane = lax.broadcasted_iota(jnp.int32, (count, lanes), 1)
+    group = [lane == token + i * count for i in range(4)]
+    group = [jnp.where(one, 1.0, 0.0).astype(jnp.bfloat16) for one in group]
+    first_row = lax.broadcasted_iota(jnp.int32, (rows, experts), 1) * capacity
+    at = lax.broadcasted_iota(jnp.int32, (rows, experts), 0)
     inside = (at >= first_row) & (at < first_row + capacity)
     spread = jnp.where(inside, 1.0, 0.0).astype(jnp.bfloat16)
-    local_slot = jnp.sum(jnp.where(inside, at - first_row, 0), axis=0, keepdims=True)
-    picked = (dot(named, spread) > 0.5) & (dot(slot, spread) == local_slot.astype(jnp.float32))
-    picker = jnp.where(picked, 1.0, 0.0).astype(jnp.bfloat16)
-    ones = jnp.ones((count, width), jnp.bfloat16)
-    row_gate = jnp.zeros((rows, width), jnp.float32)
-    for i, part in enumerate(bf16_parts(gate_of)):
-        spread_part = jnp.where(picked, dot(part, spread), 0.0).astype(jnp.bfloat16)
-        maps_ref[i * count : (i + 1) * count, :] = spread_part
-        row_gate = row_gate + dot(spread_part, ones, FIRST)
-    maps_ref[3 * count : 4 * count, :] = picker
-    send_rows = dot(picker, tokens_ref[...], FIRST)
-    send_back = row_gate * dot(picker, cotangent_ref[...], FIRST)
+    local_slot = jnp.sum(jnp.where(inside, at - first_row, 0), axis=1, keepdims=True)
+    copies[0].wait()
+    copies[1].wait()
+    everywhere = group[0] + group[1] + group[2] + group[3]
+    routes = dot(routes_ref[...].astype(jnp.float32).astype(jnp.bfloat16), everywhere)
+    ones = jnp.ones((route_count, count), jnp.bfloat16)
+    values = jnp.zeros((route_count, lanes), jnp.float32)
+    for part, lanes_of in zip((*bf16_parts(gates_ref[...]), ones), group):
+        values = values + dot(part, lanes_of)
+    expert = lax.broadcasted_iota(jnp.int32, (experts, lanes), 0).astype(jnp.float32)
+    named = jnp.zeros((experts, lanes), jnp.float32)
+    value_of = jnp.zeros((experts, lanes), jnp.float32)
+    for k in range(route_count):
+        hit = routes[k : k + 1, :] == expert
+        named = jnp.where(hit, 1.0, named)
+        value_of = jnp.where(hit, values[k : k + 1, :], value_of)
+    other = lax.broadcasted_iota(jnp.int32, (lanes, lanes), 0)
+    mine = lax.broadcasted_iota(jnp.int32, (lanes, lanes), 1)
+    for _ in range(3):
+        mine = jnp.where(mine >= count, mine - count, mine)
+    before = jnp.where(other < mine, 1.0, 0.0).astype(jnp.bfloat16)
+    named = named.astype(jnp.bfloat16)
+    slot = dot(named, before).astype(jnp.bfloat16)
+    picked = (dot(spread, named) > 0.5) & (dot(spread, slot) == local_slot.astype(jnp.float32))
+    maps = jnp.where(picked, dot(spread, value_of.astype(jnp.bfloat16)), 0.0)
+    is_gate = lax.broadcasted_iota(jnp.int32, (rows, lanes), 1) < 3 * count
+    row_gate = jnp.sum(jnp.where(is_gate, maps, 0.0), axis=1, keepdims=True)
+    maps = maps.astype(jnp.bfloat16)
+    maps_ref[...] = maps
+    copies[2].wait()
+    copies[3].wait()
+    send_rows = dot(maps, tokens_ref[...])
+    send_back = row_gate * dot(maps, cotangent_ref[...])
     sent_ref[...] = jnp.concatenate(
         [send_rows.reshape(experts, capacity, width), send_back.reshape(experts, capacity, width)],
         axis=1,
@@ -70,22 +97,26 @@
     home = home_ref[...].astype(jnp.float32)
     out = home[:, :capacity, :].reshape(rows, width).astype(jnp.bfloat16)
     grad = home[:, capacity:, :].reshape(rows, width).astype(jnp.bfloat16)
-    total = dot(maps_ref[0:count, :], out)
-    total = total + dot(maps_ref[count : 2 * count, :], out)
-    total = total + dot(maps_ref[2 * count : 3 * count, :], out)
+    total = dot(maps_ref[...], out, FIRST)
+    total = total[:count] + total[count : 2 * count] + total[2 * count : 3 * count]
     mixed_ref[...] = total.astype(jnp.bfloat16)
-    grad_ref[...] = dot(maps_ref[3 * count : 4 * count, :], grad).astype(jnp.bfloat16)
+    grad_ref[...] = dot(maps_ref[...], grad, FIRST)[3 * count :].astype(jnp.bfloat16)
+
+
+def stage_kernel(in_ref, out_ref, staged_in_ref, staged_out_ref):
+    staged_in_ref[...] = in_ref[...]
+    staged_out_ref[...] = out_ref[...]
 
 
 def unit_order(me, chips):
     chip, core = lax.div(me, 2), lax.rem(me, 2)
     sign, twin = 1 - 2 * core, 1 - core
     opposite = 2 * lax.rem(chip + 4, chips)
-    order = [2 * chip + twin]
+    order = []
     for distance in (1, 2, 3):
         at = 2 * lax.rem(chip - sign * distance + chips, chips)
         order += [at + core, at + twin]
-    order += [2 * chip + core, opposite + core]
+    order += [2 * chip + core, 2 * chip + twin, opposite + core]
     for distance in (1, 2, 3):
         at = 2 * lax.rem(chip + sign * distance + chips, chips)
         order += [at + twin, at + core]
@@ -107,15 +138,15 @@
             block = source[pl.ds(unit * blocks, blocks)].astype(jnp.float32)
             row_to[here, :] = block[:, :capacity].reshape(UNIT, width).astype(jnp.bfloat16)
             back_to[here, :] = block[:, capacity:].reshape(UNIT, width).astype(jnp.bfloat16)
-    part = slice(7 * UNIT, 15 * UNIT)
+    part = slice(6 * UNIT, 15 * UNIT)
     ff = out_ref.shape[0]
 
     def put(columns, total):
-        own_ref[:, columns] = total[:UNIT]
-        far_ref[:, columns] = total[UNIT : 2 * UNIT].astype(jnp.bfloat16)
-        near_ref[:, columns] = total[2 * UNIT : 4 * UNIT].astype(jnp.bfloat16)
-        middle_ref[:, columns] = total[4 * UNIT : 6 * UNIT]
-        third_ref[:, columns] = total[6 * UNIT :].astype(jnp.bfloat16)
+        own_ref[:, columns] = total[: 2 * UNIT]
+        far_ref[:, columns] = total[2 * UNIT : 3 * UNIT].astype(jnp.bfloat16)
+        near_ref[:, columns] = total[3 * UNIT : 5 * UNIT].astype(jnp.bfloat16)
+        middle_ref[:, columns] = total[5 * UNIT : 7 * UNIT]
+        third_ref[:, columns] = total[7 * UNIT :].astype(jnp.bfloat16)
 
     step = ff // 2
     for start in range(0, 2 * ff, step):
@@ -139,16 +170,14 @@
     sum_ref[UNIT:, :] = (total[UNIT:] + far_ref[...].astype(jnp.float32)).astype(jnp.bfloat16)
 
 
-def twin_part_kernel(near_ref, passed_ref, sum_ref):
-    sum_ref[...] = near_ref[:UNIT, :].astype(jnp.float32) + passed_ref[:UNIT, :].astype(jnp.float32)
-
-
-def swish_kernel(own_ref, near_ref, passed_ref, twin_ref, mid_ref):
-    share = (
-        own_ref[...]
-        + near_ref[UNIT:, :].astype(jnp.float32)
-        + passed_ref[UNIT:, :].astype(jnp.float32)
-        + twin_ref[...]
+def arrived_kernel(near_ref, passed_ref, sum_ref):
+    sum_ref[...] = near_ref[...].astype(jnp.float32) + passed_ref[...].astype(jnp.float32)
+
+
+def swish_kernel(own_ref, arrived_ref, twin_ref, mid_ref):
+    arrived, twin = arrived_ref[...], twin_ref[...]
+    share = own_ref[...] + jnp.concatenate(
+        [arrived[UNIT:] + twin[:UNIT], arrived[:UNIT] + twin[UNIT:]], axis=0
     )
     ff = share.shape[1] // 3
     gate_part, up_part, back_hidden = share[:, :ff], share[:, ff : 2 * ff], share[:, 2 * ff :]
@@ -183,12 +212,13 @@
         ).astype(jnp.bfloat16)
 
 
-def call(kernel, out_shape, flops, *operands, scratch=(), scalar_first=False):
+def call(kernel, out_shape, flops, *operands, scratch=(), scalar_first=False, in_place=False):
     def size(a):
         return a.size * a.dtype.itemsize
 
     moved = sum(map(size, operands)) + sum(map(size, jax.tree.leaves(out_shape)))
-    specs = [pl.BlockSpec(memory_space=pltpu.VMEM) for _ in operands]
+    space = pl.ANY if in_place else pltpu.VMEM
+    specs = [pl.BlockSpec(memory_space=space) for _ in operands]
     if scalar_first:
         specs[0] = pl.BlockSpec(memory_space=pltpu.SMEM)
     return pl.pallas_call(
@@ -196,7 +226,7 @@
         out_shape=out_shape,
         in_specs=specs,
         scratch_shapes=scratch,
-        compiler_params=pltpu.CompilerParams(vmem_limit_bytes=40 * 2**20),
+        compiler_params=pltpu.CompilerParams(vmem_limit_bytes=(60 if in_place else 24) * 2**20),
         cost_estimate=pl.CostEstimate(flops=flops, bytes_accessed=moved, transcendentals=0),
     )(*operands)
 
@@ -232,29 +262,40 @@
         lambda *refs: dispatch_kernel(capacity, *refs),
         (
             jax.ShapeDtypeStruct((experts, 2 * capacity, width), jnp.bfloat16),
-            jax.ShapeDtypeStruct((4 * block_tok, rows), jnp.bfloat16),
+            jax.ShapeDtypeStruct((rows, 4 * block_tok), jnp.bfloat16),
         ),
         10 * rows * block_tok * width,
-        routes,
-        gates,
+        routes.T,
+        gates.T,
         tokens,
         cotangent,
+        scratch=[
+            pltpu.VMEM((route_count, block_tok), jnp.int32),
+            pltpu.VMEM((route_count, block_tok), f32),
+            pltpu.VMEM((4 * block_tok, width), bf16),
+            pltpu.VMEM((4 * block_tok, width), bf16),
+            pltpu.SemaphoreType.DMA((4,)),
+        ],
+        in_place=True,
     )
     sent, *ready = lax.optimization_barrier((sent, weight_in, weight_out))
-    got, twin_in, twin_out = lax.optimization_barrier((exchange(sent), *map(swap, ready)))
+    staged = call(
+        stage_kernel, (array(width, 2 * ff, bf16), array(ff, width, bf16)), width * ff, *ready
+    )
+    got, twin_in, twin_out = lax.optimization_barrier((exchange(sent), *map(swap, staged)))
     all_columns = 3 * ff
     routed_rows, routed_back, own, far, near, middle, third = call(
         lambda *refs: sums_kernel(capacity, *refs),
         (
             array(rows, width, bf16),
             array(rows, width, bf16),
-            array(UNIT, all_columns, f32),
+            array(2 * UNIT, all_columns, f32),
             array(UNIT, all_columns, bf16),
             array(2 * UNIT, all_columns, bf16),
             array(2 * UNIT, all_columns, f32),
             array(2 * UNIT, all_columns, bf16),
         ),
-        4 * 8 * UNIT * width * all_columns,
+        4 * 9 * UNIT * width * all_columns,
         me,
         got,
         swap(got),
@@ -271,13 +312,11 @@
     passed = along(
         call(gateway_kernel, array(2 * UNIT, all_columns, bf16), rows * ff, middle, third, far), 2
     )
-    twin_part = swap(call(twin_part_kernel, array(UNIT, all_columns, f32), rows * ff, near, passed))
-    mid = call(
-        swish_kernel, array(UNIT, all_columns, bf16), rows * ff, own, near, passed, twin_part
-    )
-
-    twin_mid = swap(mid)
-    chip_mid = jnp.concatenate([mid, twin_mid], axis=0)
+    arrived = call(arrived_kernel, array(2 * UNIT, all_columns, f32), rows * ff, near, passed)
+    chip_mid = call(
+        swish_kernel, array(2 * UNIT, all_columns, bf16), rows * ff, own, arrived, swap(arrived)
+    )
+
     second = along(chip_mid, 2)
     first = along(chip_mid, 1)
     third = along(second, 1)
@@ -292,11 +331,10 @@
         me,
         weight_in,
         weight_out,
-        twin_mid,
         first,
         second,
         third,
-        mid,
+        chip_mid,
         far,
         swap(first),
         swap(second),

time: 149 us -> 143 us (0.960)
  waiting for transfers between devices: 54.1 us -> 50.1 us
  starting transfers between devices: 79.9 us -> 77.8 us
  local copies, waits for them, and re-layouts: 5.11 us -> 3.56 us
    all_to_all x2, waiting for transfers between devices: 30.8 us -> 27.8 us  [exchange(): lax.all_to_all(values, 'fsdp', split_axis=0, concat_axis=0, tiled=True)]
    ppermute x9 -> x8, starting transfers between devices: 18.9 us -> 16.8 us  [swap(): lax.ppermute(values, 'expert', [(d, d ^ 1) for d in range(2 * chips)])]
    unnamed x14 -> x16, local copies, waits for them, and re-layouts: 5.1 us -> 3.55 us
    ppermute x9 -> x8, waiting for transfers between devices: 7.14 us -> 6.16 us  [swap(): lax.ppermute(values, 'expert', [(d, d ^ 1) for d in range(2 * chips)])]
    pallas_call x7 -> x8, Pallas kernels: 5.46 us -> 6.35 us  [call(): pl.pallas_call(kernel, out_shape=out_shape, in_specs=specs, scratch_shape...]
  transfers between devices with their start and end apart: 19 -> 18, of which waited for: 11 -> 10; matrix products, arithmetic and copies ran while one was open for 2% -> 3% of each run, Pallas kernels for 0% -> 0%
where the time goes in v4:
time: 143 us; the launch traced here: 142 us
  starting transfers between devices  77.8 us (54%)
  waiting for transfers between devices  50.1 us (35%)
  Pallas kernels  6.35 us (4%)
  matrix products  3.62 us (3%)
  local copies, waits for them, and re-layouts  3.56 us (2%)
    ppermute x8, starting transfers between devices, along(): return lax.ppermute(values, 'expert', up + down)  32.6 us
    all_to_all x2, starting transfers between devices, exchange(): lax.all_to_all(values, 'fsdp', split_axis=0, concat_axis=0, tiled=True)  28.4 us
    all_to_all x2, waiting for transfers between devices, exchange(): lax.all_to_all(values, 'fsdp', split_axis=0, concat_axis=0, tiled=True)  27.8 us
    ppermute x8, starting transfers between devices, swap(): lax.ppermute(values, 'expert', [(d, d ^ 1) for d in range(2 * chips)])  16.8 us
    ppermute x8, waiting for transfers between devices, along(): return lax.ppermute(values, 'expert', up + down)  16.1 us
    pallas_call x8, Pallas kernels, call(): pl.pallas_call(kernel, out_shape=out_shape, in_specs=specs, scratch_shape...  6.35 us
    ppermute x8, waiting for transfers between devices, swap(): lax.ppermute(values, 'expert', [(d, d ^ 1) for d in range(2 * chips)])  6.16 us
    dot_general x2, matrix products, dot(): return lax.dot_general(a, b, dims, preferred_element_type=jnp.float32)  3.62 us
  transfers between devices with their start and end apart: 18, of which 10 were waited for; matrix products, arithmetic and copies ran while one was open for 3% of the time, Pallas kernels for 0%

profile of v4, /device:TPU:34, one launch (start us, length us, event | category | flops | bytes accessed | tf_op | source)
XLA Modules:
  0.0 142.4 jit_solution(4022574944186586463)
XLA Ops:
  0.7 2.4 %shard_map.93 = (bf16[64,16,256]{2,1,0:T(8,128)(2,1)}, bf16[512,128]{1,0:T(8,128)(2,1)}) custom-call(s32[8,32]{1,0:T(8,128)} %bitcast.17, f32[8,32]{1,0:T(8,128)} %bitcast.18, bf16[32,256]{1,0:T(8,128)(2,1)} %refs_2_.1, bf16[32,256]{1,0:T(8,128)(2,1)} %refs_3_.1), custom_call_target="tpu_custom_call" | custom-call | flops 41943040 | bytes 690176 | tf_op jit(solution)/shard_map/pallas_call | solution.py:224
  3.1 23.1 %all-to-all-start = ((bf16[64,16,256]{2,1,0:T(8,128)(2,1)}), bf16[64,16,256]{2,1,0:T(8,128)(2,1)S(1)}, u32[]{:S(2)}, u32[]{:S(2)}) async-start(bf16[64,16,256]{2,1,0:T(8,128)(2,1)} %get-tuple-element.27), calls=%async_computation | async-start | bytes 1048576 | tf_op jit(solution)/shard_map/all_to_all | solution.py:248
  26.2 1.1 copy-done
  28.4 1.9 %collective-permute-start = (bf16[256,1536]{1,0:T(8,128)(2,1)S(1)}, bf16[256,1536]{1,0:T(8,128)(2,1)S(1)}, u32[]{:S(2)}, u32[]{:S(2)}) collective-permute-start(bf16[256,1536]{1,0:T(8,128)(2,1)S(1)} %get-tuple-element.30), channel_id=1, source_target_pairs={{0,64},{64,0},{128,192},{192,128},{256,320},{320,256},{384,448},{4... | collective-permute-start | bytes 2359304 | tf_op jit(solution)/shard_map/ppermute | solution.py:251
  30.3 2.4 %collective-permute-start.1 = (bf16[768,256]{1,0:T(8,128)(2,1)S(1)}, bf16[768,256]{1,0:T(8,128)(2,1)S(1)}, u32[]{:S(2)}, u32[]{:S(2)}) collective-permute-start(bf16[768,256]{1,0:T(8,128)(2,1)S(1)} %get-tuple-element.31), channel_id=1, source_target_pairs={{0,64},{64,0},{128,192},{192,128},{256,320},{320,256},{384,448},{4... | collective-permute-start | bytes 1179656 | tf_op jit(solution)/shard_map/ppermute | solution.py:251
  32.7 1.3 collective-permute-done.1.refs_6_
  34.1 11.5 %all-to-all-done.refs_1_ = bf16[64,16,256]{2,1,0:T(8,128)(2,1)S(1)} async-done(((bf16[64,16,256]{2,1,0:T(8,128)(2,1)}), bf16[64,16,256]{2,1,0:T(8,128)(2,1)S(1)}, u32[]{:S(2)}, u32[]{:S(2)}) %all-to-all-start) | async-done | bytes 524320 | tf_op jit(solution)/shard_map/all_to_all | solution.py:248
  45.6 1.9 %collective-permute-start.2 = (bf16[64,16,256]{2,1,0:T(8,128)(2,1)S(1)}, bf16[64,16,256]{2,1,0:T(8,128)(2,1)S(1)}, u32[]{:S(2)}, u32[]{:S(2)}) collective-permute-start(bf16[64,16,256]{2,1,0:T(8,128)(2,1)S(1)} %all-to-all-done.refs_1_), channel_id=1, source_target_pairs={{0,64},{64,0},{128,192},{192,128},{256,320},{320,256},{384,448},{4... | collective-permute-start | bytes 1572872 | tf_op jit(solution)/shard_map/ppermute | solution.py:251
  47.5 1.9 %collective-permute-done.2.refs_2_ = bf16[64,16,256]{2,1,0:T(8,128)(2,1)S(1)} collective-permute-done((bf16[64,16,256]{2,1,0:T(8,128)(2,1)S(1)}, bf16[64,16,256]{2,1,0:T(8,128)(2,1)S(1)}, u32[]{:S(2)}, u32[]{:S(2)}) %collective-permute-start.2) | collective-permute-done | bytes 524320 | tf_op jit(solution)/shard_map/ppermute | solution.py:251
  49.4 1.1 shard_map.95
  51.9 3.4 %collective-permute-start.4 = (bf16[64,2304]{1,0:T(8,128)(2,1)S(1)}, bf16[64,2304]{1,0:T(8,128)(2,1)S(1)}, u32[]{:S(2)}, u32[]{:S(2)}) collective-permute-start(bf16[64,2304]{1,0:T(8,128)(2,1)S(1)} %get-tuple-element.38), channel_id=1, source_target_pairs={{0,128},{128,256},{256,384},{384,512},{512,640},{640,768},{768,896... | collective-permute-start | bytes 884744 | tf_op jit(solution)/shard_map/ppermute | solution.py:256
  55.3 5.5 %collective-permute-start.5 = (bf16[32,2304]{1,0:T(8,128)(2,1)S(1)}, bf16[32,2304]{1,0:T(8,128)(2,1)S(1)}, u32[]{:S(2)}, u32[]{:S(2)}) collective-permute-start(bf16[32,2304]{1,0:T(8,128)(2,1)S(1)} %get-tuple-element.39), channel_id=1, source_target_pairs={{0,256},{128,384},{256,512},{384,640},{512,768},{640,896},{768,0},... | collective-permute-start | bytes 442376 | tf_op jit(solution)/shard_map/ppermute | solution.py:256
  60.8 2.5 %collective-permute-start.3 = (bf16[64,2304]{1,0:T(8,128)(2,1)S(1)}, bf16[64,2304]{1,0:T(8,128)(2,1)S(1)}, u32[]{:S(2)}, u32[]{:S(2)}) collective-permute-start(bf16[64,2304]{1,0:T(8,128)(2,1)S(1)} %get-tuple-element.36), channel_id=1, source_target_pairs={{0,128},{128,256},{256,384},{384,512},{512,640},{640,768},{768,896... | collective-permute-start | bytes 884744 | tf_op jit(solution)/shard_map/ppermute | solution.py:256
  63.3 2.6 %collective-permute-done.5.far_ref = bf16[32,2304]{1,0:T(8,128)(2,1)S(1)} collective-permute-done((bf16[32,2304]{1,0:T(8,128)(2,1)S(1)}, bf16[32,2304]{1,0:T(8,128)(2,1)S(1)}, u32[]{:S(2)}, u32[]{:S(2)}) %collective-permute-start.5) | collective-permute-done | bytes 147488 | tf_op jit(solution)/shard_map/ppermute | solution.py:256
  66.1 3.1 %collective-permute-start.6 = (bf16[64,2304]{1,0:T(8,128)(2,1)S(1)}, bf16[64,2304]{1,0:T(8,128)(2,1)S(1)}, u32[]{:S(2)}, u32[]{:S(2)}) collective-permute-start(bf16[64,2304]{1,0:T(8,128)(2,1)S(1)} %shard_map.96), channel_id=1, source_target_pairs={{0,256},{128,384},{256,512},{384,640},{512,768},{640,896},{768,0},... | collective-permute-start | bytes 884744 | tf_op jit(solution)/shard_map/ppermute | solution.py:256
  69.5 9.9 %collective-permute-done.6.passed_ref = bf16[64,2304]{1,0:T(8,128)(2,1)S(1)} collective-permute-done((bf16[64,2304]{1,0:T(8,128)(2,1)S(1)}, bf16[64,2304]{1,0:T(8,128)(2,1)S(1)}, u32[]{:S(2)}, u32[]{:S(2)}) %collective-permute-start.6) | collective-permute-done | bytes 294944 | tf_op jit(solution)/shard_map/ppermute | solution.py:256
  79.4 1.9 %collective-permute-start.7 = (f32[64,2304]{1,0:T(8,128)S(1)}, f32[64,2304]{1,0:T(8,128)S(1)}, u32[]{:S(2)}, u32[]{:S(2)}) collective-permute-start(f32[64,2304]{1,0:T(8,128)S(1)} %shard_map.97.arrived_ref), channel_id=1, source_target_pairs={{0,64},{64,0},{128,192},{192,128},{256,320},{320,256},{384,448},{4... | collective-permute-start | bytes 1769480 | tf_op jit(solution)/shard_map/ppermute | solution.py:251
  81.3 2.0 %collective-permute-done.7.twin_ref = f32[64,2304]{1,0:T(8,128)S(1)} collective-permute-done((f32[64,2304]{1,0:T(8,128)S(1)}, f32[64,2304]{1,0:T(8,128)S(1)}, u32[]{:S(2)}, u32[]{:S(2)}) %collective-permute-start.7) | collective-permute-done | bytes 589856 | tf_op jit(solution)/shard_map/ppermute | solution.py:251
  83.4 1.9 %collective-permute-start.9 = (bf16[64,2304]{1,0:T(8,128)(2,1)S(1)}, bf16[64,2304]{1,0:T(8,128)(2,1)S(1)}, u32[]{:S(2)}, u32[]{:S(2)}) collective-permute-start(bf16[64,2304]{1,0:T(8,128)(2,1)S(1)} %shard_map.98.refs_6_), channel_id=1, source_target_pairs={{0,256},{128,384},{256,512},{384,640},{512,768},{640,896},{768,0},... | collective-permute-start | bytes 884744 | tf_op jit(solution)/shard_map/ppermute | solution.py:256
  85.4 6.8 %collective-permute-start.8 = (bf16[64,2304]{1,0:T(8,128)(2,1)S(1)}, bf16[64,2304]{1,0:T(8,128)(2,1)S(1)}, u32[]{:S(2)}, u32[]{:S(2)}) collective-permute-start(bf16[64,2304]{1,0:T(8,128)(2,1)S(1)} %shard_map.98.refs_6_), channel_id=1, source_target_pairs={{0,128},{128,256},{256,384},{384,512},{512,640},{640,768},{768,896... | collective-permute-start | bytes 884744 | tf_op jit(solution)/shard_map/ppermute | solution.py:256
  92.2 3.3 %collective-permute-done.9.refs_4_ = bf16[64,2304]{1,0:T(8,128)(2,1)S(1)} collective-permute-done((bf16[64,2304]{1,0:T(8,128)(2,1)S(1)}, bf16[64,2304]{1,0:T(8,128)(2,1)S(1)}, u32[]{:S(2)}, u32[]{:S(2)}) %collective-permute-start.9) | collective-permute-done | bytes 294944 | tf_op jit(solution)/shard_map/ppermute | solution.py:256
  95.5 2.7 %collective-permute-start.10 = (bf16[64,2304]{1,0:T(8,128)(2,1)S(1)}, bf16[64,2304]{1,0:T(8,128)(2,1)S(1)}, u32[]{:S(2)}, u32[]{:S(2)}) collective-permute-start(bf16[64,2304]{1,0:T(8,128)(2,1)S(1)} %collective-permute-done.9.refs_4_), channel_id=1, source_target_pairs={{0,128},{128,256},{256,384},{384,512},{512,640},{640,768},{768,896... | collective-permute-start | bytes 884744 | tf_op jit(solution)/shard_map/ppermute | solution.py:256
  98.3 6.6 %collective-permute-start.11 = (bf16[32,2304]{1,0:T(8,128)(2,1)S(1)}, bf16[32,2304]{1,0:T(8,128)(2,1)S(1)}, u32[]{:S(2)}, u32[]{:S(2)}) collective-permute-start(bf16[32,2304]{1,0:T(8,128)(2,1)S(1)} %slice.12), channel_id=1, source_target_pairs={{0,256},{128,384},{256,512},{384,640},{512,768},{640,896},{768,0},... | collective-permute-start | bytes 442376 | tf_op jit(solution)/shard_map/ppermute | solution.py:256
  104.9 1.9 %collective-permute-start.13 = (bf16[64,2304]{1,0:T(8,128)(2,1)S(1)}, bf16[64,2304]{1,0:T(8,128)(2,1)S(1)}, u32[]{:S(2)}, u32[]{:S(2)}) collective-permute-start(bf16[64,2304]{1,0:T(8,128)(2,1)S(1)} %collective-permute-done.9.refs_4_), channel_id=1, source_target_pairs={{0,64},{64,0},{128,192},{192,128},{256,320},{320,256},{384,448},{4... | collective-permute-start | bytes 884744 | tf_op jit(solution)/shard_map/ppermute | solution.py:251
  106.8 2.4 %collective-permute-start.12 = (bf16[64,2304]{1,0:T(8,128)(2,1)S(1)}, bf16[64,2304]{1,0:T(8,128)(2,1)S(1)}, u32[]{:S(2)}, u32[]{:S(2)}) collective-permute-start(bf16[64,2304]{1,0:T(8,128)(2,1)S(1)} %collective-permute-done.8.refs_3_), channel_id=1, source_target_pairs={{0,64},{64,0},{128,192},{192,128},{256,320},{320,256},{384,448},{4... | collective-permute-start | bytes 884744 | tf_op jit(solution)/shard_map/ppermute | solution.py:251
  109.2 1.9 %collective-permute-start.14 = (bf16[64,2304]{1,0:T(8,128)(2,1)S(1)}, bf16[64,2304]{1,0:T(8,128)(2,1)S(1)}, u32[]{:S(2)}, u32[]{:S(2)}) collective-permute-start(bf16[64,2304]{1,0:T(8,128)(2,1)S(1)} %collective-permute-done.10.refs_5_), channel_id=1, source_target_pairs={{0,64},{64,0},{128,192},{192,128},{256,320},{320,256},{384,448},{4... | collective-permute-start | bytes 884744 | tf_op jit(solution)/shard_map/ppermute | solution.py:251
  111.2 2.4 %collective-permute-start.15 = (bf16[32,2304]{1,0:T(8,128)(2,1)S(1)}, bf16[32,2304]{1,0:T(8,128)(2,1)S(1)}, u32[]{:S(2)}, u32[]{:S(2)}) collective-permute-start(bf16[32,2304]{1,0:T(8,128)(2,1)S(1)} %collective-permute-done.11.refs_7_), channel_id=1, source_target_pairs={{0,64},{64,0},{128,192},{192,128},{256,320},{320,256},{384,448},{4... | collective-permute-start | bytes 442376 | tf_op jit(solution)/shard_map/ppermute | solution.py:251
  114.6 1.6 %shard_map.99 = (bf16[64,16,256]{2,1,0:T(8,128)(2,1)}, bf16[512,2304]{1,0:T(8,128)(2,1)S(1)}) custom-call(s32[1]{0:T(128)} %bitcast.2.refs_0_, bf16[256,1536]{1,0:T(8,128)(2,1)S(1)} %bitcast.13, bf16[768,256]{1,0:T(8,128)(2,1)S(1)} %bitcast.16, bf16[64,2304]{1,0:T(8,128)(2,1)S(1)} %collective-permute-done.8.refs_3_, ...), custom_call_target="tpu_custom_call" | custom-call | flops 603979776 | bytes 6422532 | tf_op jit(solution)/shard_map/pallas_call | solution.py:224
  116.2 5.4 %all-to-all-start.1 = ((bf16[64,16,256]{2,1,0:T(8,128)(2,1)}), bf16[64,16,256]{2,1,0:T(8,128)(2,1)S(1)}, u32[]{:S(2)}, u32[]{:S(2)}) async-start(bf16[64,16,256]{2,1,0:T(8,128)(2,1)} %get-tuple-element.40), calls=%async_computation.1 | async-start | bytes 1048576 | tf_op jit(solution)/shard_map/all_to_all | solution.py:248
  121.6 2.1 %fusion.2 = bf16[1,768,256]{2,1,0:T(8,128)(2,1)} fusion(bf16[512,256]{1,0:T(8,128)(2,1)} %copy-done.7, bf16[512,2304]{1,0:T(8,128)(2,1)S(1)} %get-tuple-element.44), kind=kOutput, calls=%fused_computation.4 | convolution fusion | flops 201523200 | bytes 1441792 | tf_op jit(solution)/shard_map/dot_general | solution.py:15
  123.7 1.5 %fusion = bf16[1,256,1536]{2,1,0:T(8,128)(2,1)} fusion(bf16[512,256]{1,0:T(8,128)(2,1)S(1)} %copy-done.6, bf16[512,2304]{1,0:T(8,128)(2,1)S(1)} %get-tuple-element.44), kind=kOutput, calls=%fused_computation.1 | convolution fusion | flops 403046400 | bytes 2621440 | tf_op jit(solution)/shard_map/dot_general | solution.py:15
  125.2 16.3 %all-to-all-done.1.refs_1_ = bf16[64,16,256]{2,1,0:T(8,128)(2,1)S(1)} async-done(((bf16[64,16,256]{2,1,0:T(8,128)(2,1)}), bf16[64,16,256]{2,1,0:T(8,128)(2,1)S(1)}, u32[]{:S(2)}, u32[]{:S(2)}) %all-to-all-start.1) | async-done | bytes 524320 | tf_op jit(solution)/shard_map/all_to_all | solution.py:248
  (31 shorter events, 4.9 us)
Async XLA Ops:
  0.6 48.8 %copy-start.3 = (bf16[1,768,256]{2,1,0:T(8,128)(2,1)S(1)}, bf16[1,768,256]{2,1,0:T(8,128)(2,1)}, u32[]{:S(2)}) copy-start(bf16[1,768,256]{2,1,0:T(8,128)(2,1)} %param.8) | copy-start | bytes 1179652
  0.6 48.7 %copy-start.1 = (bf16[1,256,1536]{2,1,0:T(8,128)(2,1)S(1)}, bf16[1,256,1536]{2,1,0:T(8,128)(2,1)}, u32[]{:S(2)}) copy-start(bf16[1,256,1536]{2,1,0:T(8,128)(2,1)} %param.7) | copy-start | bytes 2359300
  3.1 42.5 %all-to-all-start = ((bf16[64,16,256]{2,1,0:T(8,128)(2,1)}), bf16[64,16,256]{2,1,0:T(8,128)(2,1)S(1)}, u32[]{:S(2)}, u32[]{:S(2)}) async-start(bf16[64,16,256]{2,1,0:T(8,128)(2,1)} %get-tuple-element.27), calls=%async_computation | async-start | bytes 1048576 | tf_op jit(solution)/shard_map/all_to_all | solution.py:248
  26.2 1.1 copy-start
  27.3 1.0 copy-start.2
  28.4 5.7 %collective-permute-start = (bf16[256,1536]{1,0:T(8,128)(2,1)S(1)}, bf16[256,1536]{1,0:T(8,128)(2,1)S(1)}, u32[]{:S(2)}, u32[]{:S(2)}) collective-permute-start(bf16[256,1536]{1,0:T(8,128)(2,1)S(1)} %get-tuple-element.30), channel_id=1, source_target_pairs={{0,64},{64,0},{128,192},{192,128},{256,320},{320,256},{384,448},{4... | collective-permute-start | bytes 2359304 | tf_op jit(solution)/shard_map/ppermute | solution.py:251
  30.3 3.7 %collective-permute-start.1 = (bf16[768,256]{1,0:T(8,128)(2,1)S(1)}, bf16[768,256]{1,0:T(8,128)(2,1)S(1)}, u32[]{:S(2)}, u32[]{:S(2)}) collective-permute-start(bf16[768,256]{1,0:T(8,128)(2,1)S(1)} %get-tuple-element.31), channel_id=1, source_target_pairs={{0,64},{64,0},{128,192},{192,128},{256,320},{320,256},{384,448},{4... | collective-permute-start | bytes 1179656 | tf_op jit(solution)/shard_map/ppermute | solution.py:251
  45.6 3.8 %collective-permute-start.2 = (bf16[64,16,256]{2,1,0:T(8,128)(2,1)S(1)}, bf16[64,16,256]{2,1,0:T(8,128)(2,1)S(1)}, u32[]{:S(2)}, u32[]{:S(2)}) collective-permute-start(bf16[64,16,256]{2,1,0:T(8,128)(2,1)S(1)} %all-to-all-done.refs_1_), channel_id=1, source_target_pairs={{0,64},{64,0},{128,192},{192,128},{256,320},{320,256},{384,448},{4... | collective-permute-start | bytes 1572872 | tf_op jit(solution)/shard_map/ppermute | solution.py:251
  50.5 0.7 copy-start.5
  51.2 0.7 copy-start.7
  51.9 14.1 %collective-permute-start.4 = (bf16[64,2304]{1,0:T(8,128)(2,1)S(1)}, bf16[64,2304]{1,0:T(8,128)(2,1)S(1)}, u32[]{:S(2)}, u32[]{:S(2)}) collective-permute-start(bf16[64,2304]{1,0:T(8,128)(2,1)S(1)} %get-tuple-element.38), channel_id=1, source_target_pairs={{0,128},{128,256},{256,384},{384,512},{512,640},{640,768},{768,896... | collective-permute-start | bytes 884744 | tf_op jit(solution)/shard_map/ppermute | solution.py:256
  55.3 10.7 %collective-permute-start.5 = (bf16[32,2304]{1,0:T(8,128)(2,1)S(1)}, bf16[32,2304]{1,0:T(8,128)(2,1)S(1)}, u32[]{:S(2)}, u32[]{:S(2)}) collective-permute-start(bf16[32,2304]{1,0:T(8,128)(2,1)S(1)} %get-tuple-element.39), channel_id=1, source_target_pairs={{0,256},{128,384},{256,512},{384,640},{512,768},{640,896},{768,0},... | collective-permute-start | bytes 442376 | tf_op jit(solution)/shard_map/ppermute | solution.py:256
  60.8 8.6 %collective-permute-start.3 = (bf16[64,2304]{1,0:T(8,128)(2,1)S(1)}, bf16[64,2304]{1,0:T(8,128)(2,1)S(1)}, u32[]{:S(2)}, u32[]{:S(2)}) collective-permute-start(bf16[64,2304]{1,0:T(8,128)(2,1)S(1)} %get-tuple-element.36), channel_id=1, source_target_pairs={{0,128},{128,256},{256,384},{384,512},{512,640},{640,768},{768,896... | collective-permute-start | bytes 884744 | tf_op jit(solution)/shard_map/ppermute | solution.py:256
  66.1 13.3 %collective-permute-start.6 = (bf16[64,2304]{1,0:T(8,128)(2,1)S(1)}, bf16[64,2304]{1,0:T(8,128)(2,1)S(1)}, u32[]{:S(2)}, u32[]{:S(2)}) collective-permute-start(bf16[64,2304]{1,0:T(8,128)(2,1)S(1)} %shard_map.96), channel_id=1, source_target_pairs={{0,256},{128,384},{256,512},{384,640},{512,768},{640,896},{768,0},... | collective-permute-start | bytes 884744 | tf_op jit(solution)/shard_map/ppermute | solution.py:256
  79.4 3.9 %collective-permute-start.7 = (f32[64,2304]{1,0:T(8,128)S(1)}, f32[64,2304]{1,0:T(8,128)S(1)}, u32[]{:S(2)}, u32[]{:S(2)}) collective-permute-start(f32[64,2304]{1,0:T(8,128)S(1)} %shard_map.97.arrived_ref), channel_id=1, source_target_pairs={{0,64},{64,0},{128,192},{192,128},{256,320},{320,256},{384,448},{4... | collective-permute-start | bytes 1769480 | tf_op jit(solution)/shard_map/ppermute | solution.py:251
  83.4 12.1 %collective-permute-start.9 = (bf16[64,2304]{1,0:T(8,128)(2,1)S(1)}, bf16[64,2304]{1,0:T(8,128)(2,1)S(1)}, u32[]{:S(2)}, u32[]{:S(2)}) collective-permute-start(bf16[64,2304]{1,0:T(8,128)(2,1)S(1)} %shard_map.98.refs_6_), channel_id=1, source_target_pairs={{0,256},{128,384},{256,512},{384,640},{512,768},{640,896},{768,0},... | collective-permute-start | bytes 884744 | tf_op jit(solution)/shard_map/ppermute | solution.py:256
  85.4 21.4 %collective-permute-start.8 = (bf16[64,2304]{1,0:T(8,128)(2,1)S(1)}, bf16[64,2304]{1,0:T(8,128)(2,1)S(1)}, u32[]{:S(2)}, u32[]{:S(2)}) collective-permute-start(bf16[64,2304]{1,0:T(8,128)(2,1)S(1)} %shard_map.98.refs_6_), channel_id=1, source_target_pairs={{0,128},{128,256},{256,384},{384,512},{512,640},{640,768},{768,896... | collective-permute-start | bytes 884744 | tf_op jit(solution)/shard_map/ppermute | solution.py:256
  95.5 13.7 %collective-permute-start.10 = (bf16[64,2304]{1,0:T(8,128)(2,1)S(1)}, bf16[64,2304]{1,0:T(8,128)(2,1)S(1)}, u32[]{:S(2)}, u32[]{:S(2)}) collective-permute-start(bf16[64,2304]{1,0:T(8,128)(2,1)S(1)} %collective-permute-done.9.refs_4_), channel_id=1, source_target_pairs={{0,128},{128,256},{256,384},{384,512},{512,640},{640,768},{768,896... | collective-permute-start | bytes 884744 | tf_op jit(solution)/shard_map/ppermute | solution.py:256
  98.3 12.9 %collective-permute-start.11 = (bf16[32,2304]{1,0:T(8,128)(2,1)S(1)}, bf16[32,2304]{1,0:T(8,128)(2,1)S(1)}, u32[]{:S(2)}, u32[]{:S(2)}) collective-permute-start(bf16[32,2304]{1,0:T(8,128)(2,1)S(1)} %slice.12), channel_id=1, source_target_pairs={{0,256},{128,384},{256,512},{384,640},{512,768},{640,896},{768,0},... | collective-permute-start | bytes 442376 | tf_op jit(solution)/shard_map/ppermute | solution.py:256
  104.9 9.7 %collective-permute-start.13 = (bf16[64,2304]{1,0:T(8,128)(2,1)S(1)}, bf16[64,2304]{1,0:T(8,128)(2,1)S(1)}, u32[]{:S(2)}, u32[]{:S(2)}) collective-permute-start(bf16[64,2304]{1,0:T(8,128)(2,1)S(1)} %collective-permute-done.9.refs_4_), channel_id=1, source_target_pairs={{0,64},{64,0},{128,192},{192,128},{256,320},{320,256},{384,448},{4... | collective-permute-start | bytes 884744 | tf_op jit(solution)/shard_map/ppermute | solution.py:251
  106.8 7.8 %collective-permute-start.12 = (bf16[64,2304]{1,0:T(8,128)(2,1)S(1)}, bf16[64,2304]{1,0:T(8,128)(2,1)S(1)}, u32[]{:S(2)}, u32[]{:S(2)}) collective-permute-start(bf16[64,2304]{1,0:T(8,128)(2,1)S(1)} %collective-permute-done.8.refs_3_), channel_id=1, source_target_pairs={{0,64},{64,0},{128,192},{192,128},{256,320},{320,256},{384,448},{4... | collective-permute-start | bytes 884744 | tf_op jit(solution)/shard_map/ppermute | solution.py:251
  109.2 5.3 %collective-permute-start.14 = (bf16[64,2304]{1,0:T(8,128)(2,1)S(1)}, bf16[64,2304]{1,0:T(8,128)(2,1)S(1)}, u32[]{:S(2)}, u32[]{:S(2)}) collective-permute-start(bf16[64,2304]{1,0:T(8,128)(2,1)S(1)} %collective-permute-done.10.refs_5_), channel_id=1, source_target_pairs={{0,64},{64,0},{128,192},{192,128},{256,320},{320,256},{384,448},{4... | collective-permute-start | bytes 884744 | tf_op jit(solution)/shard_map/ppermute | solution.py:251
  111.2 3.4 %collective-permute-start.15 = (bf16[32,2304]{1,0:T(8,128)(2,1)S(1)}, bf16[32,2304]{1,0:T(8,128)(2,1)S(1)}, u32[]{:S(2)}, u32[]{:S(2)}) collective-permute-start(bf16[32,2304]{1,0:T(8,128)(2,1)S(1)} %collective-permute-done.11.refs_7_), channel_id=1, source_target_pairs={{0,64},{64,0},{128,192},{192,128},{256,320},{320,256},{384,448},{4... | collective-permute-start | bytes 442376 | tf_op jit(solution)/shard_map/ppermute | solution.py:251
  116.2 7.5 %copy-start.6 = (bf16[512,256]{1,0:T(8,128)(2,1)S(1)}, bf16[512,256]{1,0:T(8,128)(2,1)}, u32[]{:S(2)}) copy-start(bf16[512,256]{1,0:T(8,128)(2,1)} %copy-done.5) | copy-start | bytes 786436
  116.2 25.3 %all-to-all-start.1 = ((bf16[64,16,256]{2,1,0:T(8,128)(2,1)}), bf16[64,16,256]{2,1,0:T(8,128)(2,1)S(1)}, u32[]{:S(2)}, u32[]{:S(2)}) async-start(bf16[64,16,256]{2,1,0:T(8,128)(2,1)} %get-tuple-element.40), calls=%async_computation.1 | async-start | bytes 1048576 | tf_op jit(solution)/shard_map/all_to_all | solution.py:248
  121.6 19.9 %copy-start.4 = (bf16[512,128]{1,0:T(8,128)(2,1)S(1)}, bf16[512,128]{1,0:T(8,128)(2,1)}, u32[]{:S(2)}) copy-start(bf16[512,128]{1,0:T(8,128)(2,1)} %get-tuple-element.25.refs_0_) | copy-start | bytes 393220

commit v5 on v4

--- a/solution.py
+++ b/solution.py
@@ -317,9 +317,9 @@
         swish_kernel, array(2 * UNIT, all_columns, bf16), rows * ff, own, arrived, swap(arrived)
     )
 
+    first = along(chip_mid, 1)
     second = along(chip_mid, 2)
-    first = along(chip_mid, 1)
-    third = along(second, 1)
+    third = along(first, 2)
     far = along(second[:UNIT], 2)
     back, full = call(
         lambda *refs: results_kernel(capacity, *refs),

time: 143 us -> 143 us (level)
  starting transfers between devices: 77.8 us -> 79.4 us
    ppermute x8, starting transfers between devices: 32.6 us -> 34.2 us  [along(): return lax.ppermute(values, 'expert', up + down)]
where the time goes in v5:
time: 143 us
  starting transfers between devices  79.4 us (56%)
  waiting for transfers between devices  48.7 us (34%)
  Pallas kernels  6.35 us (4%)
  matrix products  3.62 us (3%)
  local copies, waits for them, and re-layouts  3.56 us (2%)
    ppermute x8, starting transfers between devices, along(): return lax.ppermute(values, 'expert', up + down)  34.2 us
    all_to_all x2, starting transfers between devices, exchange(): lax.all_to_all(values, 'fsdp', split_axis=0, concat_axis=0, tiled=True)  28.4 us
    all_to_all x2, waiting for transfers between devices, exchange(): lax.all_to_all(values, 'fsdp', split_axis=0, concat_axis=0, tiled=True)  27.8 us
    ppermute x8, starting transfers between devices, swap(): lax.ppermute(values, 'expert', [(d, d ^ 1) for d in range(2 * chips)])  16.8 us
    ppermute x8, waiting for transfers between devices, along(): return lax.ppermute(values, 'expert', up + down)  14.8 us
    pallas_call x8, Pallas kernels, call(): pl.pallas_call(kernel, out_shape=out_shape, in_specs=specs, scratch_shape...  6.35 us
    ppermute x8, waiting for transfers between devices, swap(): lax.ppermute(values, 'expert', [(d, d ^ 1) for d in range(2 * chips)])  6.16 us
    dot_general x2, matrix products, dot(): return lax.dot_general(a, b, dims, preferred_element_type=jnp.float32)  3.62 us
  transfers between devices with their start and end apart: 18, of which 10 were waited for; matrix products, arithmetic and copies ran while one was open for 3% of the time, Pallas kernels for 0%

profile of v5, /device:TPU:34, one launch (start us, length us, event | category | flops | bytes accessed | tf_op | source)
XLA Modules:
  0.0 142.6 jit_solution(10956206904093273788)
XLA Ops:
  0.7 2.4 %shard_map.93 = (bf16[64,16,256]{2,1,0:T(8,128)(2,1)}, bf16[512,128]{1,0:T(8,128)(2,1)}) custom-call(s32[8,32]{1,0:T(8,128)} %bitcast.17, f32[8,32]{1,0:T(8,128)} %bitcast.18, bf16[32,256]{1,0:T(8,128)(2,1)} %refs_2_.1, bf16[32,256]{1,0:T(8,128)(2,1)} %refs_3_.1), custom_call_target="tpu_custom_call" | custom-call | flops 41943040 | bytes 690176 | tf_op jit(solution)/shard_map/pallas_call | solution.py:224
  3.1 23.1 %all-to-all-start = ((bf16[64,16,256]{2,1,0:T(8,128)(2,1)}), bf16[64,16,256]{2,1,0:T(8,128)(2,1)S(1)}, u32[]{:S(2)}, u32[]{:S(2)}) async-start(bf16[64,16,256]{2,1,0:T(8,128)(2,1)} %get-tuple-element.27), calls=%async_computation | async-start | bytes 1048576 | tf_op jit(solution)/shard_map/all_to_all | solution.py:248
  26.2 1.1 copy-done
  28.4 1.9 %collective-permute-start = (bf16[256,1536]{1,0:T(8,128)(2,1)S(1)}, bf16[256,1536]{1,0:T(8,128)(2,1)S(1)}, u32[]{:S(2)}, u32[]{:S(2)}) collective-permute-start(bf16[256,1536]{1,0:T(8,128)(2,1)S(1)} %get-tuple-element.30), channel_id=1, source_target_pairs={{0,64},{64,0},{128,192},{192,128},{256,320},{320,256},{384,448},{4... | collective-permute-start | bytes 2359304 | tf_op jit(solution)/shard_map/ppermute | solution.py:251
  30.3 2.4 %collective-permute-start.1 = (bf16[768,256]{1,0:T(8,128)(2,1)S(1)}, bf16[768,256]{1,0:T(8,128)(2,1)S(1)}, u32[]{:S(2)}, u32[]{:S(2)}) collective-permute-start(bf16[768,256]{1,0:T(8,128)(2,1)S(1)} %get-tuple-element.31), channel_id=1, source_target_pairs={{0,64},{64,0},{128,192},{192,128},{256,320},{320,256},{384,448},{4... | collective-permute-start | bytes 1179656 | tf_op jit(solution)/shard_map/ppermute | solution.py:251
  32.7 1.3 collective-permute-done.1.refs_6_
  34.1 11.5 %all-to-all-done.refs_1_ = bf16[64,16,256]{2,1,0:T(8,128)(2,1)S(1)} async-done(((bf16[64,16,256]{2,1,0:T(8,128)(2,1)}), bf16[64,16,256]{2,1,0:T(8,128)(2,1)S(1)}, u32[]{:S(2)}, u32[]{:S(2)}) %all-to-all-start) | async-done | bytes 524320 | tf_op jit(solution)/shard_map/all_to_all | solution.py:248
  45.6 1.9 %collective-permute-start.2 = (bf16[64,16,256]{2,1,0:T(8,128)(2,1)S(1)}, bf16[64,16,256]{2,1,0:T(8,128)(2,1)S(1)}, u32[]{:S(2)}, u32[]{:S(2)}) collective-permute-start(bf16[64,16,256]{2,1,0:T(8,128)(2,1)S(1)} %all-to-all-done.refs_1_), channel_id=1, source_target_pairs={{0,64},{64,0},{128,192},{192,128},{256,320},{320,256},{384,448},{4... | collective-permute-start | bytes 1572872 | tf_op jit(solution)/shard_map/ppermute | solution.py:251
  47.5 1.9 %collective-permute-done.2.refs_2_ = bf16[64,16,256]{2,1,0:T(8,128)(2,1)S(1)} collective-permute-done((bf16[64,16,256]{2,1,0:T(8,128)(2,1)S(1)}, bf16[64,16,256]{2,1,0:T(8,128)(2,1)S(1)}, u32[]{:S(2)}, u32[]{:S(2)}) %collective-permute-start.2) | collective-permute-done | bytes 524320 | tf_op jit(solution)/shard_map/ppermute | solution.py:251
  49.4 1.1 shard_map.95
  51.9 3.4 %collective-permute-start.4 = (bf16[64,2304]{1,0:T(8,128)(2,1)S(1)}, bf16[64,2304]{1,0:T(8,128)(2,1)S(1)}, u32[]{:S(2)}, u32[]{:S(2)}) collective-permute-start(bf16[64,2304]{1,0:T(8,128)(2,1)S(1)} %get-tuple-element.38), channel_id=1, source_target_pairs={{0,128},{128,256},{256,384},{384,512},{512,640},{640,768},{768,896... | collective-permute-start | bytes 884744 | tf_op jit(solution)/shard_map/ppermute | solution.py:256
  55.3 5.5 %collective-permute-start.5 = (bf16[32,2304]{1,0:T(8,128)(2,1)S(1)}, bf16[32,2304]{1,0:T(8,128)(2,1)S(1)}, u32[]{:S(2)}, u32[]{:S(2)}) collective-permute-start(bf16[32,2304]{1,0:T(8,128)(2,1)S(1)} %get-tuple-element.39), channel_id=1, source_target_pairs={{0,256},{128,384},{256,512},{384,640},{512,768},{640,896},{768,0},... | collective-permute-start | bytes 442376 | tf_op jit(solution)/shard_map/ppermute | solution.py:256
  60.8 2.5 %collective-permute-start.3 = (bf16[64,2304]{1,0:T(8,128)(2,1)S(1)}, bf16[64,2304]{1,0:T(8,128)(2,1)S(1)}, u32[]{:S(2)}, u32[]{:S(2)}) collective-permute-start(bf16[64,2304]{1,0:T(8,128)(2,1)S(1)} %get-tuple-element.36), channel_id=1, source_target_pairs={{0,128},{128,256},{256,384},{384,512},{512,640},{640,768},{768,896... | collective-permute-start | bytes 884744 | tf_op jit(solution)/shard_map/ppermute | solution.py:256
  63.3 2.6 %collective-permute-done.5.far_ref = bf16[32,2304]{1,0:T(8,128)(2,1)S(1)} collective-permute-done((bf16[32,2304]{1,0:T(8,128)(2,1)S(1)}, bf16[32,2304]{1,0:T(8,128)(2,1)S(1)}, u32[]{:S(2)}, u32[]{:S(2)}) %collective-permute-start.5) | collective-permute-done | bytes 147488 | tf_op jit(solution)/shard_map/ppermute | solution.py:256
  66.1 3.1 %collective-permute-start.6 = (bf16[64,2304]{1,0:T(8,128)(2,1)S(1)}, bf16[64,2304]{1,0:T(8,128)(2,1)S(1)}, u32[]{:S(2)}, u32[]{:S(2)}) collective-permute-start(bf16[64,2304]{1,0:T(8,128)(2,1)S(1)} %shard_map.96), channel_id=1, source_target_pairs={{0,256},{128,384},{256,512},{384,640},{512,768},{640,896},{768,0},... | collective-permute-start | bytes 884744 | tf_op jit(solution)/shard_map/ppermute | solution.py:256
  69.5 9.9 %collective-permute-done.6.passed_ref = bf16[64,2304]{1,0:T(8,128)(2,1)S(1)} collective-permute-done((bf16[64,2304]{1,0:T(8,128)(2,1)S(1)}, bf16[64,2304]{1,0:T(8,128)(2,1)S(1)}, u32[]{:S(2)}, u32[]{:S(2)}) %collective-permute-start.6) | collective-permute-done | bytes 294944 | tf_op jit(solution)/shard_map/ppermute | solution.py:256
  79.4 1.9 %collective-permute-start.7 = (f32[64,2304]{1,0:T(8,128)S(1)}, f32[64,2304]{1,0:T(8,128)S(1)}, u32[]{:S(2)}, u32[]{:S(2)}) collective-permute-start(f32[64,2304]{1,0:T(8,128)S(1)} %shard_map.97.arrived_ref), channel_id=1, source_target_pairs={{0,64},{64,0},{128,192},{192,128},{256,320},{320,256},{384,448},{4... | collective-permute-start | bytes 1769480 | tf_op jit(solution)/shard_map/ppermute | solution.py:251
  81.3 2.0 %collective-permute-done.7.twin_ref = f32[64,2304]{1,0:T(8,128)S(1)} collective-permute-done((f32[64,2304]{1,0:T(8,128)S(1)}, f32[64,2304]{1,0:T(8,128)S(1)}, u32[]{:S(2)}, u32[]{:S(2)}) %collective-permute-start.7) | collective-permute-done | bytes 589856 | tf_op jit(solution)/shard_map/ppermute | solution.py:251
  83.4 2.2 %collective-permute-start.8 = (bf16[64,2304]{1,0:T(8,128)(2,1)S(1)}, bf16[64,2304]{1,0:T(8,128)(2,1)S(1)}, u32[]{:S(2)}, u32[]{:S(2)}) collective-permute-start(bf16[64,2304]{1,0:T(8,128)(2,1)S(1)} %shard_map.98.refs_6_), channel_id=1, source_target_pairs={{0,128},{128,256},{256,384},{384,512},{512,640},{640,768},{768,896... | collective-permute-start | bytes 884744 | tf_op jit(solution)/shard_map/ppermute | solution.py:256
  85.7 6.5 %collective-permute-start.9 = (bf16[64,2304]{1,0:T(8,128)(2,1)S(1)}, bf16[64,2304]{1,0:T(8,128)(2,1)S(1)}, u32[]{:S(2)}, u32[]{:S(2)}) collective-permute-start(bf16[64,2304]{1,0:T(8,128)(2,1)S(1)} %shard_map.98.refs_6_), channel_id=1, source_target_pairs={{0,256},{128,384},{256,512},{384,640},{512,768},{640,896},{768,0},... | collective-permute-start | bytes 884744 | tf_op jit(solution)/shard_map/ppermute | solution.py:256
  92.2 5.7 %collective-permute-start.10 = (bf16[64,2304]{1,0:T(8,128)(2,1)S(1)}, bf16[64,2304]{1,0:T(8,128)(2,1)S(1)}, u32[]{:S(2)}, u32[]{:S(2)}) collective-permute-start(bf16[64,2304]{1,0:T(8,128)(2,1)S(1)} %collective-permute-done.8.refs_3_), channel_id=1, source_target_pairs={{0,256},{128,384},{256,512},{384,640},{512,768},{640,896},{768,0},... | collective-permute-start | bytes 884744 | tf_op jit(solution)/shard_map/ppermute | solution.py:256
  97.9 2.0 %collective-permute-done.9.refs_4_ = bf16[64,2304]{1,0:T(8,128)(2,1)S(1)} collective-permute-done((bf16[64,2304]{1,0:T(8,128)(2,1)S(1)}, bf16[64,2304]{1,0:T(8,128)(2,1)S(1)}, u32[]{:S(2)}, u32[]{:S(2)}) %collective-permute-start.9) | collective-permute-done | bytes 294944 | tf_op jit(solution)/shard_map/ppermute | solution.py:256
  99.9 5.2 %collective-permute-start.11 = (bf16[32,2304]{1,0:T(8,128)(2,1)S(1)}, bf16[32,2304]{1,0:T(8,128)(2,1)S(1)}, u32[]{:S(2)}, u32[]{:S(2)}) collective-permute-start(bf16[32,2304]{1,0:T(8,128)(2,1)S(1)} %slice.12), channel_id=1, source_target_pairs={{0,256},{128,384},{256,512},{384,640},{512,768},{640,896},{768,0},... | collective-permute-start | bytes 442376 | tf_op jit(solution)/shard_map/ppermute | solution.py:256
  105.1 1.9 %collective-permute-start.13 = (bf16[64,2304]{1,0:T(8,128)(2,1)S(1)}, bf16[64,2304]{1,0:T(8,128)(2,1)S(1)}, u32[]{:S(2)}, u32[]{:S(2)}) collective-permute-start(bf16[64,2304]{1,0:T(8,128)(2,1)S(1)} %collective-permute-done.9.refs_4_), channel_id=1, source_target_pairs={{0,64},{64,0},{128,192},{192,128},{256,320},{320,256},{384,448},{4... | collective-permute-start | bytes 884744 | tf_op jit(solution)/shard_map/ppermute | solution.py:251
  107.0 2.4 %collective-permute-start.12 = (bf16[64,2304]{1,0:T(8,128)(2,1)S(1)}, bf16[64,2304]{1,0:T(8,128)(2,1)S(1)}, u32[]{:S(2)}, u32[]{:S(2)}) collective-permute-start(bf16[64,2304]{1,0:T(8,128)(2,1)S(1)} %collective-permute-done.8.refs_3_), channel_id=1, source_target_pairs={{0,64},{64,0},{128,192},{192,128},{256,320},{320,256},{384,448},{4... | collective-permute-start | bytes 884744 | tf_op jit(solution)/shard_map/ppermute | solution.py:251
  109.5 1.9 %collective-permute-start.14 = (bf16[64,2304]{1,0:T(8,128)(2,1)S(1)}, bf16[64,2304]{1,0:T(8,128)(2,1)S(1)}, u32[]{:S(2)}, u32[]{:S(2)}) collective-permute-start(bf16[64,2304]{1,0:T(8,128)(2,1)S(1)} %collective-permute-done.10.refs_5_), channel_id=1, source_target_pairs={{0,64},{64,0},{128,192},{192,128},{256,320},{320,256},{384,448},{4... | collective-permute-start | bytes 884744 | tf_op jit(solution)/shard_map/ppermute | solution.py:251
  111.4 2.4 %collective-permute-start.15 = (bf16[32,2304]{1,0:T(8,128)(2,1)S(1)}, bf16[32,2304]{1,0:T(8,128)(2,1)S(1)}, u32[]{:S(2)}, u32[]{:S(2)}) collective-permute-start(bf16[32,2304]{1,0:T(8,128)(2,1)S(1)} %collective-permute-done.11.refs_7_), channel_id=1, source_target_pairs={{0,64},{64,0},{128,192},{192,128},{256,320},{320,256},{384,448},{4... | collective-permute-start | bytes 442376 | tf_op jit(solution)/shard_map/ppermute | solution.py:251
  114.8 1.6 %shard_map.99 = (bf16[64,16,256]{2,1,0:T(8,128)(2,1)}, bf16[512,2304]{1,0:T(8,128)(2,1)S(1)}) custom-call(s32[1]{0:T(128)} %bitcast.2.refs_0_, bf16[256,1536]{1,0:T(8,128)(2,1)S(1)} %bitcast.13, bf16[768,256]{1,0:T(8,128)(2,1)S(1)} %bitcast.16, bf16[64,2304]{1,0:T(8,128)(2,1)S(1)} %collective-permute-done.8.refs_3_, ...), custom_call_target="tpu_custom_call" | custom-call | flops 603979776 | bytes 6422532 | tf_op jit(solution)/shard_map/pallas_call | solution.py:224
  116.4 5.3 %all-to-all-start.1 = ((bf16[64,16,256]{2,1,0:T(8,128)(2,1)}), bf16[64,16,256]{2,1,0:T(8,128)(2,1)S(1)}, u32[]{:S(2)}, u32[]{:S(2)}) async-start(bf16[64,16,256]{2,1,0:T(8,128)(2,1)} %get-tuple-element.40), calls=%async_computation.1 | async-start | bytes 1048576 | tf_op jit(solution)/shard_map/all_to_all | solution.py:248
  121.8 2.1 %fusion.2 = bf16[1,768,256]{2,1,0:T(8,128)(2,1)} fusion(bf16[512,256]{1,0:T(8,128)(2,1)} %copy-done.7, bf16[512,2304]{1,0:T(8,128)(2,1)S(1)} %get-tuple-element.44), kind=kOutput, calls=%fused_computation.4 | convolution fusion | flops 201523200 | bytes 1441792 | tf_op jit(solution)/shard_map/dot_general | solution.py:15
  123.9 1.5 %fusion = bf16[1,256,1536]{2,1,0:T(8,128)(2,1)} fusion(bf16[512,256]{1,0:T(8,128)(2,1)S(1)} %copy-done.6, bf16[512,2304]{1,0:T(8,128)(2,1)S(1)} %get-tuple-element.44), kind=kOutput, calls=%fused_computation.1 | convolution fusion | flops 403046400 | bytes 2621440 | tf_op jit(solution)/shard_map/dot_general | solution.py:15
  125.4 16.3 %all-to-all-done.1.refs_1_ = bf16[64,16,256]{2,1,0:T(8,128)(2,1)S(1)} async-done(((bf16[64,16,256]{2,1,0:T(8,128)(2,1)}), bf16[64,16,256]{2,1,0:T(8,128)(2,1)S(1)}, u32[]{:S(2)}, u32[]{:S(2)}) %all-to-all-start.1) | async-done | bytes 524320 | tf_op jit(solution)/shard_map/all_to_all | solution.py:248
  (31 shorter events, 4.9 us)
Async XLA Ops:
  0.6 48.8 %copy-start.3 = (bf16[1,768,256]{2,1,0:T(8,128)(2,1)S(1)}, bf16[1,768,256]{2,1,0:T(8,128)(2,1)}, u32[]{:S(2)}) copy-start(bf16[1,768,256]{2,1,0:T(8,128)(2,1)} %param.8) | copy-start | bytes 1179652
  0.6 48.7 %copy-start.1 = (bf16[1,256,1536]{2,1,0:T(8,128)(2,1)S(1)}, bf16[1,256,1536]{2,1,0:T(8,128)(2,1)}, u32[]{:S(2)}) copy-start(bf16[1,256,1536]{2,1,0:T(8,128)(2,1)} %param.7) | copy-start | bytes 2359300
  3.1 42.5 %all-to-all-start = ((bf16[64,16,256]{2,1,0:T(8,128)(2,1)}), bf16[64,16,256]{2,1,0:T(8,128)(2,1)S(1)}, u32[]{:S(2)}, u32[]{:S(2)}) async-start(bf16[64,16,256]{2,1,0:T(8,128)(2,1)} %get-tuple-element.27), calls=%async_computation | async-start | bytes 1048576 | tf_op jit(solution)/shard_map/all_to_all | solution.py:248
  26.2 1.1 copy-start
  27.3 1.0 copy-start.2
  28.4 5.7 %collective-permute-start = (bf16[256,1536]{1,0:T(8,128)(2,1)S(1)}, bf16[256,1536]{1,0:T(8,128)(2,1)S(1)}, u32[]{:S(2)}, u32[]{:S(2)}) collective-permute-start(bf16[256,1536]{1,0:T(8,128)(2,1)S(1)} %get-tuple-element.30), channel_id=1, source_target_pairs={{0,64},{64,0},{128,192},{192,128},{256,320},{320,256},{384,448},{4... | collective-permute-start | bytes 2359304 | tf_op jit(solution)/shard_map/ppermute | solution.py:251
  30.3 3.7 %collective-permute-start.1 = (bf16[768,256]{1,0:T(8,128)(2,1)S(1)}, bf16[768,256]{1,0:T(8,128)(2,1)S(1)}, u32[]{:S(2)}, u32[]{:S(2)}) collective-permute-start(bf16[768,256]{1,0:T(8,128)(2,1)S(1)} %get-tuple-element.31), channel_id=1, source_target_pairs={{0,64},{64,0},{128,192},{192,128},{256,320},{320,256},{384,448},{4... | collective-permute-start | bytes 1179656 | tf_op jit(solution)/shard_map/ppermute | solution.py:251
  45.6 3.8 %collective-permute-start.2 = (bf16[64,16,256]{2,1,0:T(8,128)(2,1)S(1)}, bf16[64,16,256]{2,1,0:T(8,128)(2,1)S(1)}, u32[]{:S(2)}, u32[]{:S(2)}) collective-permute-start(bf16[64,16,256]{2,1,0:T(8,128)(2,1)S(1)} %all-to-all-done.refs_1_), channel_id=1, source_target_pairs={{0,64},{64,0},{128,192},{192,128},{256,320},{320,256},{384,448},{4... | collective-permute-start | bytes 1572872 | tf_op jit(solution)/shard_map/ppermute | solution.py:251
  50.5 0.7 copy-start.5
  51.2 0.7 copy-start.7
  51.9 14.1 %collective-permute-start.4 = (bf16[64,2304]{1,0:T(8,128)(2,1)S(1)}, bf16[64,2304]{1,0:T(8,128)(2,1)S(1)}, u32[]{:S(2)}, u32[]{:S(2)}) collective-permute-start(bf16[64,2304]{1,0:T(8,128)(2,1)S(1)} %get-tuple-element.38), channel_id=1, source_target_pairs={{0,128},{128,256},{256,384},{384,512},{512,640},{640,768},{768,896... | collective-permute-start | bytes 884744 | tf_op jit(solution)/shard_map/ppermute | solution.py:256
  55.3 10.7 %collective-permute-start.5 = (bf16[32,2304]{1,0:T(8,128)(2,1)S(1)}, bf16[32,2304]{1,0:T(8,128)(2,1)S(1)}, u32[]{:S(2)}, u32[]{:S(2)}) collective-permute-start(bf16[32,2304]{1,0:T(8,128)(2,1)S(1)} %get-tuple-element.39), channel_id=1, source_target_pairs={{0,256},{128,384},{256,512},{384,640},{512,768},{640,896},{768,0},... | collective-permute-start | bytes 442376 | tf_op jit(solution)/shard_map/ppermute | solution.py:256
  60.8 8.6 %collective-permute-start.3 = (bf16[64,2304]{1,0:T(8,128)(2,1)S(1)}, bf16[64,2304]{1,0:T(8,128)(2,1)S(1)}, u32[]{:S(2)}, u32[]{:S(2)}) collective-permute-start(bf16[64,2304]{1,0:T(8,128)(2,1)S(1)} %get-tuple-element.36), channel_id=1, source_target_pairs={{0,128},{128,256},{256,384},{384,512},{512,640},{640,768},{768,896... | collective-permute-start | bytes 884744 | tf_op jit(solution)/shard_map/ppermute | solution.py:256
  66.1 13.3 %collective-permute-start.6 = (bf16[64,2304]{1,0:T(8,128)(2,1)S(1)}, bf16[64,2304]{1,0:T(8,128)(2,1)S(1)}, u32[]{:S(2)}, u32[]{:S(2)}) collective-permute-start(bf16[64,2304]{1,0:T(8,128)(2,1)S(1)} %shard_map.96), channel_id=1, source_target_pairs={{0,256},{128,384},{256,512},{384,640},{512,768},{640,896},{768,0},... | collective-permute-start | bytes 884744 | tf_op jit(solution)/shard_map/ppermute | solution.py:256
  79.4 3.9 %collective-permute-start.7 = (f32[64,2304]{1,0:T(8,128)S(1)}, f32[64,2304]{1,0:T(8,128)S(1)}, u32[]{:S(2)}, u32[]{:S(2)}) collective-permute-start(f32[64,2304]{1,0:T(8,128)S(1)} %shard_map.97.arrived_ref), channel_id=1, source_target_pairs={{0,64},{64,0},{128,192},{192,128},{256,320},{320,256},{384,448},{4... | collective-permute-start | bytes 1769480 | tf_op jit(solution)/shard_map/ppermute | solution.py:251
  83.4 8.7 %collective-permute-start.8 = (bf16[64,2304]{1,0:T(8,128)(2,1)S(1)}, bf16[64,2304]{1,0:T(8,128)(2,1)S(1)}, u32[]{:S(2)}, u32[]{:S(2)}) collective-permute-start(bf16[64,2304]{1,0:T(8,128)(2,1)S(1)} %shard_map.98.refs_6_), channel_id=1, source_target_pairs={{0,128},{128,256},{256,384},{384,512},{512,640},{640,768},{768,896... | collective-permute-start | bytes 884744 | tf_op jit(solution)/shard_map/ppermute | solution.py:256
  85.7 14.2 %collective-permute-start.9 = (bf16[64,2304]{1,0:T(8,128)(2,1)S(1)}, bf16[64,2304]{1,0:T(8,128)(2,1)S(1)}, u32[]{:S(2)}, u32[]{:S(2)}) collective-permute-start(bf16[64,2304]{1,0:T(8,128)(2,1)S(1)} %shard_map.98.refs_6_), channel_id=1, source_target_pairs={{0,256},{128,384},{256,512},{384,640},{512,768},{640,896},{768,0},... | collective-permute-start | bytes 884744 | tf_op jit(solution)/shard_map/ppermute | solution.py:256
  92.2 17.2 %collective-permute-start.10 = (bf16[64,2304]{1,0:T(8,128)(2,1)S(1)}, bf16[64,2304]{1,0:T(8,128)(2,1)S(1)}, u32[]{:S(2)}, u32[]{:S(2)}) collective-permute-start(bf16[64,2304]{1,0:T(8,128)(2,1)S(1)} %collective-permute-done.8.refs_3_), channel_id=1, source_target_pairs={{0,256},{128,384},{256,512},{384,640},{512,768},{640,896},{768,0},... | collective-permute-start | bytes 884744 | tf_op jit(solution)/shard_map/ppermute | solution.py:256
  99.9 11.5 %collective-permute-start.11 = (bf16[32,2304]{1,0:T(8,128)(2,1)S(1)}, bf16[32,2304]{1,0:T(8,128)(2,1)S(1)}, u32[]{:S(2)}, u32[]{:S(2)}) collective-permute-start(bf16[32,2304]{1,0:T(8,128)(2,1)S(1)} %slice.12), channel_id=1, source_target_pairs={{0,256},{128,384},{256,512},{384,640},{512,768},{640,896},{768,0},... | collective-permute-start | bytes 442376 | tf_op jit(solution)/shard_map/ppermute | solution.py:256
  105.1 9.7 %collective-permute-start.13 = (bf16[64,2304]{1,0:T(8,128)(2,1)S(1)}, bf16[64,2304]{1,0:T(8,128)(2,1)S(1)}, u32[]{:S(2)}, u32[]{:S(2)}) collective-permute-start(bf16[64,2304]{1,0:T(8,128)(2,1)S(1)} %collective-permute-done.9.refs_4_), channel_id=1, source_target_pairs={{0,64},{64,0},{128,192},{192,128},{256,320},{320,256},{384,448},{4... | collective-permute-start | bytes 884744 | tf_op jit(solution)/shard_map/ppermute | solution.py:251
  107.0 7.8 %collective-permute-start.12 = (bf16[64,2304]{1,0:T(8,128)(2,1)S(1)}, bf16[64,2304]{1,0:T(8,128)(2,1)S(1)}, u32[]{:S(2)}, u32[]{:S(2)}) collective-permute-start(bf16[64,2304]{1,0:T(8,128)(2,1)S(1)} %collective-permute-done.8.refs_3_), channel_id=1, source_target_pairs={{0,64},{64,0},{128,192},{192,128},{256,320},{320,256},{384,448},{4... | collective-permute-start | bytes 884744 | tf_op jit(solution)/shard_map/ppermute | solution.py:251
  109.5 5.3 %collective-permute-start.14 = (bf16[64,2304]{1,0:T(8,128)(2,1)S(1)}, bf16[64,2304]{1,0:T(8,128)(2,1)S(1)}, u32[]{:S(2)}, u32[]{:S(2)}) collective-permute-start(bf16[64,2304]{1,0:T(8,128)(2,1)S(1)} %collective-permute-done.10.refs_5_), channel_id=1, source_target_pairs={{0,64},{64,0},{128,192},{192,128},{256,320},{320,256},{384,448},{4... | collective-permute-start | bytes 884744 | tf_op jit(solution)/shard_map/ppermute | solution.py:251
  111.4 3.4 %collective-permute-start.15 = (bf16[32,2304]{1,0:T(8,128)(2,1)S(1)}, bf16[32,2304]{1,0:T(8,128)(2,1)S(1)}, u32[]{:S(2)}, u32[]{:S(2)}) collective-permute-start(bf16[32,2304]{1,0:T(8,128)(2,1)S(1)} %collective-permute-done.11.refs_7_), channel_id=1, source_target_pairs={{0,64},{64,0},{128,192},{192,128},{256,320},{320,256},{384,448},{4... | collective-permute-start | bytes 442376 | tf_op jit(solution)/shard_map/ppermute | solution.py:251
  116.4 7.5 %copy-start.6 = (bf16[512,256]{1,0:T(8,128)(2,1)S(1)}, bf16[512,256]{1,0:T(8,128)(2,1)}, u32[]{:S(2)}) copy-start(bf16[512,256]{1,0:T(8,128)(2,1)} %copy-done.5) | copy-start | bytes 786436
  116.4 25.3 %all-to-all-start.1 = ((bf16[64,16,256]{2,1,0:T(8,128)(2,1)}), bf16[64,16,256]{2,1,0:T(8,128)(2,1)S(1)}, u32[]{:S(2)}, u32[]{:S(2)}) async-start(bf16[64,16,256]{2,1,0:T(8,128)(2,1)} %get-tuple-element.40), calls=%async_computation.1 | async-start | bytes 1048576 | tf_op jit(solution)/shard_map/all_to_all | solution.py:248
  121.8 19.9 %copy-start.4 = (bf16[512,128]{1,0:T(8,128)(2,1)S(1)}, bf16[512,128]{1,0:T(8,128)(2,1)}, u32[]{:S(2)}) copy-start(bf16[512,128]{1,0:T(8,128)(2,1)} %get-tuple-element.25.refs_0_) | copy-start | bytes 393220

commit v6 on v4

--- a/solution.py
+++ b/solution.py
@@ -124,12 +124,12 @@
 
 
 def sums_kernel(capacity, me_ref, got_ref, twin_got_ref, in_ref, twin_in_ref, out_ref, twin_out_ref,
-                rows_ref, back_ref, own_ref, far_ref, near_ref, middle_ref, third_ref,
-                twin_rows, twin_back):
+                own_ref, far_ref, near_ref, middle_ref, third_ref, rows_ref, back_ref, twin_rows,
+                twin_back):
     experts, _, width = got_ref.shape
-    units = rows_ref.shape[0] // UNIT
+    units = experts * capacity // UNIT
     blocks = UNIT // capacity
-    for k, unit in enumerate(unit_order(me_ref[0], units // 2)):
+    for k, unit in enumerate(unit_order(me_ref[0], units // 2)[6:15]):
         here = slice(k * UNIT, (k + 1) * UNIT)
         for source, row_to, back_to in (
             (got_ref, rows_ref, back_ref),
@@ -138,7 +138,6 @@
             block = source[pl.ds(unit * blocks, blocks)].astype(jnp.float32)
             row_to[here, :] = block[:, :capacity].reshape(UNIT, width).astype(jnp.bfloat16)
             back_to[here, :] = block[:, capacity:].reshape(UNIT, width).astype(jnp.bfloat16)
-    part = slice(6 * UNIT, 15 * UNIT)
     ff = out_ref.shape[0]
 
     def put(columns, total):
@@ -153,14 +152,14 @@
         columns = slice(start, start + step)
         put(
             columns,
-            dot(rows_ref[part, :], in_ref[:, columns]) + dot(twin_rows[part, :], twin_in_ref[:, columns]),
+            dot(rows_ref[...], in_ref[:, columns]) + dot(twin_rows[...], twin_in_ref[:, columns]),
         )
     for start in range(0, ff, step):
         some = slice(start, start + step)
         put(
             slice(2 * ff + start, 2 * ff + start + step),
-            dot(back_ref[part, :], out_ref[some, :], LAST)
-            + dot(twin_back[part, :], twin_out_ref[some, :], LAST),
+            dot(back_ref[...], out_ref[some, :], LAST)
+            + dot(twin_back[...], twin_out_ref[some, :], LAST),
         )
 
 
@@ -190,29 +189,27 @@
 
 
 def results_kernel(capacity, me_ref, in_ref, out_ref, *refs):
-    parts, (back_ref, full_ref) = refs[:-2], refs[-2:]
-    at = 0
+    parts, (back_ref, full_out, full_ref, stored) = refs[:-4], refs[-4:]
+    rows = full_ref.shape[0]
+    order = iter(unit_order(me_ref[0], rows // (2 * UNIT)))
     for part in parts:
-        count = part.shape[0]
-        full_ref[at : at + count, :] = part[...]
-        at += count
+        for at in range(0, part.shape[0], UNIT):
+            to = pl.multiple_of(next(order) * UNIT, UNIT)
+            full_ref[pl.ds(to, UNIT), :] = part[at : at + UNIT, :]
     ff, width = out_ref.shape
+    copy = pltpu.make_async_copy(full_ref, full_out, stored)
+    copy.start()
     out = dot(full_ref[:, :ff], out_ref[...])
     grad = dot(full_ref[:, ff:], in_ref[...], LAST)
-    units = full_ref.shape[0] // UNIT
-    blocks = UNIT // capacity
-    for k, unit in enumerate(unit_order(me_ref[0], units // 2)):
-        here = slice(k * UNIT, (k + 1) * UNIT)
-        back_ref[pl.ds(unit * blocks, blocks)] = jnp.concatenate(
-            [
-                out[here].reshape(blocks, capacity, width),
-                grad[here].reshape(blocks, capacity, width),
-            ],
-            axis=1,
-        ).astype(jnp.bfloat16)
-
-
-def call(kernel, out_shape, flops, *operands, scratch=(), scalar_first=False, in_place=False):
+    experts = rows // capacity
+    back_ref[...] = jnp.concatenate(
+        [out.reshape(experts, capacity, width), grad.reshape(experts, capacity, width)], axis=1
+    ).astype(jnp.bfloat16)
+    copy.wait()
+
+
+def call(kernel, out_shape, flops, *operands, scratch=(), scalar_first=False, in_place=False,
+         outside=()):
     def size(a):
         return a.size * a.dtype.itemsize
 
@@ -221,12 +218,17 @@
     specs = [pl.BlockSpec(memory_space=space) for _ in operands]
     if scalar_first:
         specs[0] = pl.BlockSpec(memory_space=pltpu.SMEM)
+    out_specs = tuple(
+        pl.BlockSpec(memory_space=pl.ANY if i in outside else pltpu.VMEM)
+        for i in range(len(jax.tree.leaves(out_shape)))
+    )
     return pl.pallas_call(
         kernel,
         out_shape=out_shape,
         in_specs=specs,
+        out_specs=out_specs if isinstance(out_shape, tuple) else out_specs[0],
         scratch_shapes=scratch,
-        compiler_params=pltpu.CompilerParams(vmem_limit_bytes=(60 if in_place else 24) * 2**20),
+        compiler_params=pltpu.CompilerParams(vmem_limit_bytes=(60 if in_place else 48) * 2**20),
         cost_estimate=pl.CostEstimate(flops=flops, bytes_accessed=moved, transcendentals=0),
     )(*operands)
 
@@ -284,11 +286,11 @@
     )
     got, twin_in, twin_out = lax.optimization_barrier((exchange(sent), *map(swap, staged)))
     all_columns = 3 * ff
-    routed_rows, routed_back, own, far, near, middle, third = call(
+    routed_rows = got[:, :capacity].reshape(rows, width)
+    routed_back = got[:, capacity:].reshape(rows, width)
+    own, far, near, middle, third = call(
         lambda *refs: sums_kernel(capacity, *refs),
         (
-            array(rows, width, bf16),
-            array(rows, width, bf16),
             array(2 * UNIT, all_columns, f32),
             array(UNIT, all_columns, bf16),
             array(2 * UNIT, all_columns, bf16),
@@ -303,7 +305,7 @@
         twin_in,
         weight_out,
         twin_out,
-        scratch=[pltpu.VMEM((rows, width), bf16), pltpu.VMEM((rows, width), bf16)],
+        scratch=[pltpu.VMEM((9 * UNIT, width), bf16)] * 4,
         scalar_first=True,
     )
     third = along(third, 1)
@@ -340,7 +342,9 @@
         swap(second),
         swap(third),
         swap(far),
+        scratch=[pltpu.VMEM((rows, all_columns), bf16), pltpu.SemaphoreType.DMA],
         scalar_first=True,
+        outside=(1,),
     )
     home = exchange(back)
     hidden, grad_pre = full[:, :ff], full[:, ff:]

time: 143 us -> 143 us (level)
  waiting for transfers between devices: 50.1 us -> 48.5 us
  matrix products: 3.62 us -> 5.21 us
    dot_general x2, matrix products: 3.62 us -> 5.21 us  [dot(): return lax.dot_general(a, b, dims, preferred_element_type=jnp.float32)]
    all_to_all x2, waiting for transfers between devices: 27.8 us -> 26.2 us  [exchange(): lax.all_to_all(values, 'fsdp', split_axis=0, concat_axis=0, tiled=True)]
    unnamed x16 -> x10, local copies, waits for them, and re-layouts: 3.55 us -> 2.14 us
  transfers between devices with their start and end apart: 18 -> 18, of which waited for: 10 -> 10; matrix products, arithmetic and copies ran while one was open for 3% -> 4% of each run, Pallas kernels for 0% -> 0%
where the time goes in v6:
time: 143 us; the launch traced here: 142 us
  starting transfers between devices  77.7 us (54%)
  waiting for transfers between devices  48.5 us (34%)
  Pallas kernels  7.67 us (5%)
  matrix products  5.21 us (4%)
  local copies, waits for them, and re-layouts  2.15 us (2%)
    ppermute x8, starting transfers between devices, along(): return lax.ppermute(values, 'expert', up + down)  32.6 us
    all_to_all x2, starting transfers between devices, exchange(): lax.all_to_all(values, 'fsdp', split_axis=0, concat_axis=0, tiled=True)  28.3 us
    all_to_all x2, waiting for transfers between devices, exchange(): lax.all_to_all(values, 'fsdp', split_axis=0, concat_axis=0, tiled=True)  26.2 us
    ppermute x8, starting transfers between devices, swap(): lax.ppermute(values, 'expert', [(d, d ^ 1) for d in range(2 * chips)])  16.8 us
    ppermute x8, waiting for transfers between devices, along(): return lax.ppermute(values, 'expert', up + down)  16.1 us
    pallas_call x8, Pallas kernels, call(): pl.pallas_call(kernel, out_shape=out_shape, in_specs=specs, out_specs=out...  7.67 us
    ppermute x8, waiting for transfers between devices, swap(): lax.ppermute(values, 'expert', [(d, d ^ 1) for d in range(2 * chips)])  6.16 us
    dot_general x2, matrix products, dot(): return lax.dot_general(a, b, dims, preferred_element_type=jnp.float32)  5.21 us
  transfers between devices with their start and end apart: 18, of which 10 were waited for; matrix products, arithmetic and copies ran while one was open for 4% of the time, Pallas kernels for 0%

profile of v6, /device:TPU:34, one launch (start us, length us, event | category | flops | bytes accessed | tf_op | source)
XLA Modules:
  0.0 142.2 jit_solution(17080910319452375584)
XLA Ops:
  0.7 2.4 %shard_map.93 = (bf16[64,16,256]{2,1,0:T(8,128)(2,1)}, bf16[512,128]{1,0:T(8,128)(2,1)}) custom-call(s32[8,32]{1,0:T(8,128)} %bitcast.21, f32[8,32]{1,0:T(8,128)} %bitcast.22, bf16[32,256]{1,0:T(8,128)(2,1)} %refs_2_.1, bf16[32,256]{1,0:T(8,128)(2,1)} %refs_3_.1), custom_call_target="tpu_custom_call" | custom-call | flops 41943040 | bytes 690176 | tf_op jit(solution)/shard_map/pallas_call | solution.py:225
  3.1 23.1 %all-to-all-start = ((bf16[64,16,256]{2,1,0:T(8,128)(2,1)}), bf16[64,16,256]{2,1,0:T(8,128)(2,1)S(1)}, u32[]{:S(2)}, u32[]{:S(2)}) async-start(bf16[64,16,256]{2,1,0:T(8,128)(2,1)} %get-tuple-element.25), calls=%async_computation | async-start | bytes 1048576 | tf_op jit(solution)/shard_map/all_to_all | solution.py:250
  26.2 1.1 copy-done
  28.4 1.9 %collective-permute-start = (bf16[256,1536]{1,0:T(8,128)(2,1)S(1)}, bf16[256,1536]{1,0:T(8,128)(2,1)S(1)}, u32[]{:S(2)}, u32[]{:S(2)}) collective-permute-start(bf16[256,1536]{1,0:T(8,128)(2,1)S(1)} %get-tuple-element.28), channel_id=1, source_target_pairs={{0,64},{64,0},{128,192},{192,128},{256,320},{320,256},{384,448},{4... | collective-permute-start | bytes 2359304 | tf_op jit(solution)/shard_map/ppermute | solution.py:253
  30.3 2.4 %collective-permute-start.1 = (bf16[768,256]{1,0:T(8,128)(2,1)S(1)}, bf16[768,256]{1,0:T(8,128)(2,1)S(1)}, u32[]{:S(2)}, u32[]{:S(2)}) collective-permute-start(bf16[768,256]{1,0:T(8,128)(2,1)S(1)} %get-tuple-element.29), channel_id=1, source_target_pairs={{0,64},{64,0},{128,192},{192,128},{256,320},{320,256},{384,448},{4... | collective-permute-start | bytes 1179656 | tf_op jit(solution)/shard_map/ppermute | solution.py:253
  32.7 1.3 collective-permute-done.1.refs_6_
  34.1 11.5 %all-to-all-done.refs_1_ = bf16[64,16,256]{2,1,0:T(8,128)(2,1)S(1)} async-done(((bf16[64,16,256]{2,1,0:T(8,128)(2,1)}), bf16[64,16,256]{2,1,0:T(8,128)(2,1)S(1)}, u32[]{:S(2)}, u32[]{:S(2)}) %all-to-all-start) | async-done | bytes 524320 | tf_op jit(solution)/shard_map/all_to_all | solution.py:250
  45.6 1.9 %collective-permute-start.2 = (bf16[64,16,256]{2,1,0:T(8,128)(2,1)S(1)}, bf16[64,16,256]{2,1,0:T(8,128)(2,1)S(1)}, u32[]{:S(2)}, u32[]{:S(2)}) collective-permute-start(bf16[64,16,256]{2,1,0:T(8,128)(2,1)S(1)} %all-to-all-done.refs_1_), channel_id=1, source_target_pairs={{0,64},{64,0},{128,192},{192,128},{256,320},{320,256},{384,448},{4... | collective-permute-start | bytes 1572872 | tf_op jit(solution)/shard_map/ppermute | solution.py:253
  47.5 1.9 %collective-permute-done.2.refs_2_ = bf16[64,16,256]{2,1,0:T(8,128)(2,1)S(1)} collective-permute-done((bf16[64,16,256]{2,1,0:T(8,128)(2,1)S(1)}, bf16[64,16,256]{2,1,0:T(8,128)(2,1)S(1)}, u32[]{:S(2)}, u32[]{:S(2)}) %collective-permute-start.2) | collective-permute-done | bytes 524320 | tf_op jit(solution)/shard_map/ppermute | solution.py:253
  49.4 1.1 shard_map.95
  50.5 3.4 %collective-permute-start.4 = (bf16[64,2304]{1,0:T(8,128)(2,1)S(1)}, bf16[64,2304]{1,0:T(8,128)(2,1)S(1)}, u32[]{:S(2)}, u32[]{:S(2)}) collective-permute-start(bf16[64,2304]{1,0:T(8,128)(2,1)S(1)} %get-tuple-element.36), channel_id=1, source_target_pairs={{0,128},{128,256},{256,384},{384,512},{512,640},{640,768},{768,896... | collective-permute-start | bytes 884744 | tf_op jit(solution)/shard_map/ppermute | solution.py:258
  53.9 5.5 %collective-permute-start.5 = (bf16[32,2304]{1,0:T(8,128)(2,1)S(1)}, bf16[32,2304]{1,0:T(8,128)(2,1)S(1)}, u32[]{:S(2)}, u32[]{:S(2)}) collective-permute-start(bf16[32,2304]{1,0:T(8,128)(2,1)S(1)} %get-tuple-element.37), channel_id=1, source_target_pairs={{0,256},{128,384},{256,512},{384,640},{512,768},{640,896},{768,0},... | collective-permute-start | bytes 442376 | tf_op jit(solution)/shard_map/ppermute | solution.py:258
  59.4 2.5 %collective-permute-start.3 = (bf16[64,2304]{1,0:T(8,128)(2,1)S(1)}, bf16[64,2304]{1,0:T(8,128)(2,1)S(1)}, u32[]{:S(2)}, u32[]{:S(2)}) collective-permute-start(bf16[64,2304]{1,0:T(8,128)(2,1)S(1)} %get-tuple-element.34), channel_id=1, source_target_pairs={{0,128},{128,256},{256,384},{384,512},{512,640},{640,768},{768,896... | collective-permute-start | bytes 884744 | tf_op jit(solution)/shard_map/ppermute | solution.py:258
  61.9 2.6 %collective-permute-done.5.far_ref = bf16[32,2304]{1,0:T(8,128)(2,1)S(1)} collective-permute-done((bf16[32,2304]{1,0:T(8,128)(2,1)S(1)}, bf16[32,2304]{1,0:T(8,128)(2,1)S(1)}, u32[]{:S(2)}, u32[]{:S(2)}) %collective-permute-start.5) | collective-permute-done | bytes 147488 | tf_op jit(solution)/shard_map/ppermute | solution.py:258
  64.7 3.1 %collective-permute-start.6 = (bf16[64,2304]{1,0:T(8,128)(2,1)S(1)}, bf16[64,2304]{1,0:T(8,128)(2,1)S(1)}, u32[]{:S(2)}, u32[]{:S(2)}) collective-permute-start(bf16[64,2304]{1,0:T(8,128)(2,1)S(1)} %shard_map.96), channel_id=1, source_target_pairs={{0,256},{128,384},{256,512},{384,640},{512,768},{640,896},{768,0},... | collective-permute-start | bytes 884744 | tf_op jit(solution)/shard_map/ppermute | solution.py:258
  68.1 9.9 %collective-permute-done.6.passed_ref = bf16[64,2304]{1,0:T(8,128)(2,1)S(1)} collective-permute-done((bf16[64,2304]{1,0:T(8,128)(2,1)S(1)}, bf16[64,2304]{1,0:T(8,128)(2,1)S(1)}, u32[]{:S(2)}, u32[]{:S(2)}) %collective-permute-start.6) | collective-permute-done | bytes 294944 | tf_op jit(solution)/shard_map/ppermute | solution.py:258
  78.0 1.9 %collective-permute-start.7 = (f32[64,2304]{1,0:T(8,128)S(1)}, f32[64,2304]{1,0:T(8,128)S(1)}, u32[]{:S(2)}, u32[]{:S(2)}) collective-permute-start(f32[64,2304]{1,0:T(8,128)S(1)} %shard_map.97.arrived_ref), channel_id=1, source_target_pairs={{0,64},{64,0},{128,192},{192,128},{256,320},{320,256},{384,448},{4... | collective-permute-start | bytes 1769480 | tf_op jit(solution)/shard_map/ppermute | solution.py:253
  79.9 2.0 %collective-permute-done.7.twin_ref = f32[64,2304]{1,0:T(8,128)S(1)} collective-permute-done((f32[64,2304]{1,0:T(8,128)S(1)}, f32[64,2304]{1,0:T(8,128)S(1)}, u32[]{:S(2)}, u32[]{:S(2)}) %collective-permute-start.7) | collective-permute-done | bytes 589856 | tf_op jit(solution)/shard_map/ppermute | solution.py:253
  82.1 1.9 %collective-permute-start.9 = (bf16[64,2304]{1,0:T(8,128)(2,1)S(1)}, bf16[64,2304]{1,0:T(8,128)(2,1)S(1)}, u32[]{:S(2)}, u32[]{:S(2)}) collective-permute-start(bf16[64,2304]{1,0:T(8,128)(2,1)S(1)} %shard_map.98.refs_6_), channel_id=1, source_target_pairs={{0,256},{128,384},{256,512},{384,640},{512,768},{640,896},{768,0},... | collective-permute-start | bytes 884744 | tf_op jit(solution)/shard_map/ppermute | solution.py:258
  84.0 6.8 %collective-permute-start.8 = (bf16[64,2304]{1,0:T(8,128)(2,1)S(1)}, bf16[64,2304]{1,0:T(8,128)(2,1)S(1)}, u32[]{:S(2)}, u32[]{:S(2)}) collective-permute-start(bf16[64,2304]{1,0:T(8,128)(2,1)S(1)} %shard_map.98.refs_6_), channel_id=1, source_target_pairs={{0,128},{128,256},{256,384},{384,512},{512,640},{640,768},{768,896... | collective-permute-start | bytes 884744 | tf_op jit(solution)/shard_map/ppermute | solution.py:258
  90.8 3.3 %collective-permute-done.9.refs_4_ = bf16[64,2304]{1,0:T(8,128)(2,1)S(1)} collective-permute-done((bf16[64,2304]{1,0:T(8,128)(2,1)S(1)}, bf16[64,2304]{1,0:T(8,128)(2,1)S(1)}, u32[]{:S(2)}, u32[]{:S(2)}) %collective-permute-start.9) | collective-permute-done | bytes 294944 | tf_op jit(solution)/shard_map/ppermute | solution.py:258
  94.2 2.7 %collective-permute-start.10 = (bf16[64,2304]{1,0:T(8,128)(2,1)S(1)}, bf16[64,2304]{1,0:T(8,128)(2,1)S(1)}, u32[]{:S(2)}, u32[]{:S(2)}) collective-permute-start(bf16[64,2304]{1,0:T(8,128)(2,1)S(1)} %collective-permute-done.9.refs_4_), channel_id=1, source_target_pairs={{0,128},{128,256},{256,384},{384,512},{512,640},{640,768},{768,896... | collective-permute-start | bytes 884744 | tf_op jit(solution)/shard_map/ppermute | solution.py:258
  96.9 6.6 %collective-permute-start.11 = (bf16[32,2304]{1,0:T(8,128)(2,1)S(1)}, bf16[32,2304]{1,0:T(8,128)(2,1)S(1)}, u32[]{:S(2)}, u32[]{:S(2)}) collective-permute-start(bf16[32,2304]{1,0:T(8,128)(2,1)S(1)} %slice.20), channel_id=1, source_target_pairs={{0,256},{128,384},{256,512},{384,640},{512,768},{640,896},{768,0},... | collective-permute-start | bytes 442376 | tf_op jit(solution)/shard_map/ppermute | solution.py:258
  103.5 1.9 %collective-permute-start.13 = (bf16[64,2304]{1,0:T(8,128)(2,1)S(1)}, bf16[64,2304]{1,0:T(8,128)(2,1)S(1)}, u32[]{:S(2)}, u32[]{:S(2)}) collective-permute-start(bf16[64,2304]{1,0:T(8,128)(2,1)S(1)} %collective-permute-done.9.refs_4_), channel_id=1, source_target_pairs={{0,64},{64,0},{128,192},{192,128},{256,320},{320,256},{384,448},{4... | collective-permute-start | bytes 884744 | tf_op jit(solution)/shard_map/ppermute | solution.py:253
  105.4 2.4 %collective-permute-start.12 = (bf16[64,2304]{1,0:T(8,128)(2,1)S(1)}, bf16[64,2304]{1,0:T(8,128)(2,1)S(1)}, u32[]{:S(2)}, u32[]{:S(2)}) collective-permute-start(bf16[64,2304]{1,0:T(8,128)(2,1)S(1)} %collective-permute-done.8.refs_3_), channel_id=1, source_target_pairs={{0,64},{64,0},{128,192},{192,128},{256,320},{320,256},{384,448},{4... | collective-permute-start | bytes 884744 | tf_op jit(solution)/shard_map/ppermute | solution.py:253
  107.8 1.9 %collective-permute-start.14 = (bf16[64,2304]{1,0:T(8,128)(2,1)S(1)}, bf16[64,2304]{1,0:T(8,128)(2,1)S(1)}, u32[]{:S(2)}, u32[]{:S(2)}) collective-permute-start(bf16[64,2304]{1,0:T(8,128)(2,1)S(1)} %collective-permute-done.10.refs_5_), channel_id=1, source_target_pairs={{0,64},{64,0},{128,192},{192,128},{256,320},{320,256},{384,448},{4... | collective-permute-start | bytes 884744 | tf_op jit(solution)/shard_map/ppermute | solution.py:253
  109.8 2.4 %collective-permute-start.15 = (bf16[32,2304]{1,0:T(8,128)(2,1)S(1)}, bf16[32,2304]{1,0:T(8,128)(2,1)S(1)}, u32[]{:S(2)}, u32[]{:S(2)}) collective-permute-start(bf16[32,2304]{1,0:T(8,128)(2,1)S(1)} %collective-permute-done.11.refs_7_), channel_id=1, source_target_pairs={{0,64},{64,0},{128,192},{192,128},{256,320},{320,256},{384,448},{4... | collective-permute-start | bytes 442376 | tf_op jit(solution)/shard_map/ppermute | solution.py:253
  113.2 2.9 %shard_map.99 = (bf16[64,16,256]{2,1,0:T(8,128)(2,1)}, bf16[512,2304]{1,0:T(8,128)(2,1)}) custom-call(s32[1]{0:T(128)} %bitcast.2.refs_0_, bf16[256,1536]{1,0:T(8,128)(2,1)S(1)} %bitcast.17, bf16[768,256]{1,0:T(8,128)(2,1)S(1)} %bitcast.20, bf16[64,2304]{1,0:T(8,128)(2,1)S(1)} %collective-permute-done.8.refs_3_, ...), custom_call_target="tpu_custom_call" | custom-call | flops 603979776 | bytes 6422532 | tf_op jit(solution)/shard_map/pallas_call | solution.py:225
  116.1 5.2 %all-to-all-start.1 = ((bf16[64,16,256]{2,1,0:T(8,128)(2,1)}), bf16[64,16,256]{2,1,0:T(8,128)(2,1)S(1)}, u32[]{:S(2)}, u32[]{:S(2)}) async-start(bf16[64,16,256]{2,1,0:T(8,128)(2,1)} %get-tuple-element.38), calls=%async_computation.1 | async-start | bytes 1048576 | tf_op jit(solution)/shard_map/all_to_all | solution.py:250
  121.4 2.3 %fusion.2 = bf16[1,768,256]{2,1,0:T(8,128)(2,1)} fusion(bf16[512,2304]{1,0:T(8,128)(2,1)} %get-tuple-element.41, bf16[64,16,256]{2,1,0:T(8,128)(2,1)S(1)} %all-to-all-done.refs_1_), kind=kOutput, calls=%fused_computation.4 | convolution fusion | flops 201523200 | bytes 1441792 | tf_op jit(solution)/shard_map/dot_general | solution.py:15
  123.7 2.9 %fusion = bf16[1,256,1536]{2,1,0:T(8,128)(2,1)} fusion(bf16[512,2304]{1,0:T(8,128)(2,1)} %get-tuple-element.41, bf16[64,16,256]{2,1,0:T(8,128)(2,1)S(1)} %all-to-all-done.refs_1_), kind=kOutput, calls=%fused_computation.1 | convolution fusion | flops 403046400 | bytes 2621440 | tf_op jit(solution)/shard_map/dot_general | solution.py:15
  126.6 14.7 %all-to-all-done.1.refs_1_ = bf16[64,16,256]{2,1,0:T(8,128)(2,1)S(1)} async-done(((bf16[64,16,256]{2,1,0:T(8,128)(2,1)}), bf16[64,16,256]{2,1,0:T(8,128)(2,1)S(1)}, u32[]{:S(2)}, u32[]{:S(2)}) %all-to-all-start.1) | async-done | bytes 524320 | tf_op jit(solution)/shard_map/all_to_all | solution.py:250
  (25 shorter events, 3.5 us)
Async XLA Ops:
  0.6 48.8 %copy-start.3 = (bf16[1,768,256]{2,1,0:T(8,128)(2,1)S(1)}, bf16[1,768,256]{2,1,0:T(8,128)(2,1)}, u32[]{:S(2)}) copy-start(bf16[1,768,256]{2,1,0:T(8,128)(2,1)} %param.8) | copy-start | bytes 1179652
  0.6 48.7 %copy-start.1 = (bf16[1,256,1536]{2,1,0:T(8,128)(2,1)S(1)}, bf16[1,256,1536]{2,1,0:T(8,128)(2,1)}, u32[]{:S(2)}) copy-start(bf16[1,256,1536]{2,1,0:T(8,128)(2,1)} %param.7) | copy-start | bytes 2359300
  3.1 42.5 %all-to-all-start = ((bf16[64,16,256]{2,1,0:T(8,128)(2,1)}), bf16[64,16,256]{2,1,0:T(8,128)(2,1)S(1)}, u32[]{:S(2)}, u32[]{:S(2)}) async-start(bf16[64,16,256]{2,1,0:T(8,128)(2,1)} %get-tuple-element.25), calls=%async_computation | async-start | bytes 1048576 | tf_op jit(solution)/shard_map/all_to_all | solution.py:250
  26.2 1.1 copy-start
  27.3 1.0 copy-start.2
  28.4 5.7 %collective-permute-start = (bf16[256,1536]{1,0:T(8,128)(2,1)S(1)}, bf16[256,1536]{1,0:T(8,128)(2,1)S(1)}, u32[]{:S(2)}, u32[]{:S(2)}) collective-permute-start(bf16[256,1536]{1,0:T(8,128)(2,1)S(1)} %get-tuple-element.28), channel_id=1, source_target_pairs={{0,64},{64,0},{128,192},{192,128},{256,320},{320,256},{384,448},{4... | collective-permute-start | bytes 2359304 | tf_op jit(solution)/shard_map/ppermute | solution.py:253
  30.3 3.7 %collective-permute-start.1 = (bf16[768,256]{1,0:T(8,128)(2,1)S(1)}, bf16[768,256]{1,0:T(8,128)(2,1)S(1)}, u32[]{:S(2)}, u32[]{:S(2)}) collective-permute-start(bf16[768,256]{1,0:T(8,128)(2,1)S(1)} %get-tuple-element.29), channel_id=1, source_target_pairs={{0,64},{64,0},{128,192},{192,128},{256,320},{320,256},{384,448},{4... | collective-permute-start | bytes 1179656 | tf_op jit(solution)/shard_map/ppermute | solution.py:253
  45.6 3.8 %collective-permute-start.2 = (bf16[64,16,256]{2,1,0:T(8,128)(2,1)S(1)}, bf16[64,16,256]{2,1,0:T(8,128)(2,1)S(1)}, u32[]{:S(2)}, u32[]{:S(2)}) collective-permute-start(bf16[64,16,256]{2,1,0:T(8,128)(2,1)S(1)} %all-to-all-done.refs_1_), channel_id=1, source_target_pairs={{0,64},{64,0},{128,192},{192,128},{256,320},{320,256},{384,448},{4... | collective-permute-start | bytes 1572872 | tf_op jit(solution)/shard_map/ppermute | solution.py:253
  50.5 14.1 %collective-permute-start.4 = (bf16[64,2304]{1,0:T(8,128)(2,1)S(1)}, bf16[64,2304]{1,0:T(8,128)(2,1)S(1)}, u32[]{:S(2)}, u32[]{:S(2)}) collective-permute-start(bf16[64,2304]{1,0:T(8,128)(2,1)S(1)} %get-tuple-element.36), channel_id=1, source_target_pairs={{0,128},{128,256},{256,384},{384,512},{512,640},{640,768},{768,896... | collective-permute-start | bytes 884744 | tf_op jit(solution)/shard_map/ppermute | solution.py:258
  53.9 10.7 %collective-permute-start.5 = (bf16[32,2304]{1,0:T(8,128)(2,1)S(1)}, bf16[32,2304]{1,0:T(8,128)(2,1)S(1)}, u32[]{:S(2)}, u32[]{:S(2)}) collective-permute-start(bf16[32,2304]{1,0:T(8,128)(2,1)S(1)} %get-tuple-element.37), channel_id=1, source_target_pairs={{0,256},{128,384},{256,512},{384,640},{512,768},{640,896},{768,0},... | collective-permute-start | bytes 442376 | tf_op jit(solution)/shard_map/ppermute | solution.py:258
  59.4 8.6 %collective-permute-start.3 = (bf16[64,2304]{1,0:T(8,128)(2,1)S(1)}, bf16[64,2304]{1,0:T(8,128)(2,1)S(1)}, u32[]{:S(2)}, u32[]{:S(2)}) collective-permute-start(bf16[64,2304]{1,0:T(8,128)(2,1)S(1)} %get-tuple-element.34), channel_id=1, source_target_pairs={{0,128},{128,256},{256,384},{384,512},{512,640},{640,768},{768,896... | collective-permute-start | bytes 884744 | tf_op jit(solution)/shard_map/ppermute | solution.py:258
  64.7 13.3 %collective-permute-start.6 = (bf16[64,2304]{1,0:T(8,128)(2,1)S(1)}, bf16[64,2304]{1,0:T(8,128)(2,1)S(1)}, u32[]{:S(2)}, u32[]{:S(2)}) collective-permute-start(bf16[64,2304]{1,0:T(8,128)(2,1)S(1)} %shard_map.96), channel_id=1, source_target_pairs={{0,256},{128,384},{256,512},{384,640},{512,768},{640,896},{768,0},... | collective-permute-start | bytes 884744 | tf_op jit(solution)/shard_map/ppermute | solution.py:258
  78.0 3.9 %collective-permute-start.7 = (f32[64,2304]{1,0:T(8,128)S(1)}, f32[64,2304]{1,0:T(8,128)S(1)}, u32[]{:S(2)}, u32[]{:S(2)}) collective-permute-start(f32[64,2304]{1,0:T(8,128)S(1)} %shard_map.97.arrived_ref), channel_id=1, source_target_pairs={{0,64},{64,0},{128,192},{192,128},{256,320},{320,256},{384,448},{4... | collective-permute-start | bytes 1769480 | tf_op jit(solution)/shard_map/ppermute | solution.py:253
  82.1 12.1 %collective-permute-start.9 = (bf16[64,2304]{1,0:T(8,128)(2,1)S(1)}, bf16[64,2304]{1,0:T(8,128)(2,1)S(1)}, u32[]{:S(2)}, u32[]{:S(2)}) collective-permute-start(bf16[64,2304]{1,0:T(8,128)(2,1)S(1)} %shard_map.98.refs_6_), channel_id=1, source_target_pairs={{0,256},{128,384},{256,512},{384,640},{512,768},{640,896},{768,0},... | collective-permute-start | bytes 884744 | tf_op jit(solution)/shard_map/ppermute | solution.py:258
  84.0 21.4 %collective-permute-start.8 = (bf16[64,2304]{1,0:T(8,128)(2,1)S(1)}, bf16[64,2304]{1,0:T(8,128)(2,1)S(1)}, u32[]{:S(2)}, u32[]{:S(2)}) collective-permute-start(bf16[64,2304]{1,0:T(8,128)(2,1)S(1)} %shard_map.98.refs_6_), channel_id=1, source_target_pairs={{0,128},{128,256},{256,384},{384,512},{512,640},{640,768},{768,896... | collective-permute-start | bytes 884744 | tf_op jit(solution)/shard_map/ppermute | solution.py:258
  94.2 13.7 %collective-permute-start.10 = (bf16[64,2304]{1,0:T(8,128)(2,1)S(1)}, bf16[64,2304]{1,0:T(8,128)(2,1)S(1)}, u32[]{:S(2)}, u32[]{:S(2)}) collective-permute-start(bf16[64,2304]{1,0:T(8,128)(2,1)S(1)} %collective-permute-done.9.refs_4_), channel_id=1, source_target_pairs={{0,128},{128,256},{256,384},{384,512},{512,640},{640,768},{768,896... | collective-permute-start | bytes 884744 | tf_op jit(solution)/shard_map/ppermute | solution.py:258
  96.9 12.9 %collective-permute-start.11 = (bf16[32,2304]{1,0:T(8,128)(2,1)S(1)}, bf16[32,2304]{1,0:T(8,128)(2,1)S(1)}, u32[]{:S(2)}, u32[]{:S(2)}) collective-permute-start(bf16[32,2304]{1,0:T(8,128)(2,1)S(1)} %slice.20), channel_id=1, source_target_pairs={{0,256},{128,384},{256,512},{384,640},{512,768},{640,896},{768,0},... | collective-permute-start | bytes 442376 | tf_op jit(solution)/shard_map/ppermute | solution.py:258
  103.5 9.7 %collective-permute-start.13 = (bf16[64,2304]{1,0:T(8,128)(2,1)S(1)}, bf16[64,2304]{1,0:T(8,128)(2,1)S(1)}, u32[]{:S(2)}, u32[]{:S(2)}) collective-permute-start(bf16[64,2304]{1,0:T(8,128)(2,1)S(1)} %collective-permute-done.9.refs_4_), channel_id=1, source_target_pairs={{0,64},{64,0},{128,192},{192,128},{256,320},{320,256},{384,448},{4... | collective-permute-start | bytes 884744 | tf_op jit(solution)/shard_map/ppermute | solution.py:253
  105.4 7.8 %collective-permute-start.12 = (bf16[64,2304]{1,0:T(8,128)(2,1)S(1)}, bf16[64,2304]{1,0:T(8,128)(2,1)S(1)}, u32[]{:S(2)}, u32[]{:S(2)}) collective-permute-start(bf16[64,2304]{1,0:T(8,128)(2,1)S(1)} %collective-permute-done.8.refs_3_), channel_id=1, source_target_pairs={{0,64},{64,0},{128,192},{192,128},{256,320},{320,256},{384,448},{4... | collective-permute-start | bytes 884744 | tf_op jit(solution)/shard_map/ppermute | solution.py:253
  107.8 5.3 %collective-permute-start.14 = (bf16[64,2304]{1,0:T(8,128)(2,1)S(1)}, bf16[64,2304]{1,0:T(8,128)(2,1)S(1)}, u32[]{:S(2)}, u32[]{:S(2)}) collective-permute-start(bf16[64,2304]{1,0:T(8,128)(2,1)S(1)} %collective-permute-done.10.refs_5_), channel_id=1, source_target_pairs={{0,64},{64,0},{128,192},{192,128},{256,320},{320,256},{384,448},{4... | collective-permute-start | bytes 884744 | tf_op jit(solution)/shard_map/ppermute | solution.py:253
  109.8 3.4 %collective-permute-start.15 = (bf16[32,2304]{1,0:T(8,128)(2,1)S(1)}, bf16[32,2304]{1,0:T(8,128)(2,1)S(1)}, u32[]{:S(2)}, u32[]{:S(2)}) collective-permute-start(bf16[32,2304]{1,0:T(8,128)(2,1)S(1)} %collective-permute-done.11.refs_7_), channel_id=1, source_target_pairs={{0,64},{64,0},{128,192},{192,128},{256,320},{320,256},{384,448},{4... | collective-permute-start | bytes 442376 | tf_op jit(solution)/shard_map/ppermute | solution.py:253
  116.1 25.2 %all-to-all-start.1 = ((bf16[64,16,256]{2,1,0:T(8,128)(2,1)}), bf16[64,16,256]{2,1,0:T(8,128)(2,1)S(1)}, u32[]{:S(2)}, u32[]{:S(2)}) async-start(bf16[64,16,256]{2,1,0:T(8,128)(2,1)} %get-tuple-element.38), calls=%async_computation.1 | async-start | bytes 1048576 | tf_op jit(solution)/shard_map/all_to_all | solution.py:250
  121.4 19.9 %copy-start.4 = (bf16[512,128]{1,0:T(8,128)(2,1)S(1)}, bf16[512,128]{1,0:T(8,128)(2,1)}, u32[]{:S(2)}) copy-start(bf16[512,128]{1,0:T(8,128)(2,1)} %get-tuple-element.23.refs_0_) | copy-start | bytes 393220

commit v7 on v4

--- a/solution.py
+++ b/solution.py
@@ -124,20 +124,16 @@
 
 
 def sums_kernel(capacity, me_ref, got_ref, twin_got_ref, in_ref, twin_in_ref, out_ref, twin_out_ref,
-                rows_ref, back_ref, own_ref, far_ref, near_ref, middle_ref, third_ref,
-                twin_rows, twin_back):
+                both_ref, own_ref, far_ref, near_ref, middle_ref, third_ref, twin_ref):
     experts, _, width = got_ref.shape
-    units = rows_ref.shape[0] // UNIT
+    units = both_ref.shape[0] // UNIT
     blocks = UNIT // capacity
     for k, unit in enumerate(unit_order(me_ref[0], units // 2)):
         here = slice(k * UNIT, (k + 1) * UNIT)
-        for source, row_to, back_to in (
-            (got_ref, rows_ref, back_ref),
-            (twin_got_ref, twin_rows, twin_back),
-        ):
+        for source, target in ((got_ref, both_ref), (twin_got_ref, twin_ref)):
             block = source[pl.ds(unit * blocks, blocks)].astype(jnp.float32)
-            row_to[here, :] = block[:, :capacity].reshape(UNIT, width).astype(jnp.bfloat16)
-            back_to[here, :] = block[:, capacity:].reshape(UNIT, width).astype(jnp.bfloat16)
+            target[here, :width] = block[:, :capacity].reshape(UNIT, width).astype(jnp.bfloat16)
+            target[here, width:] = block[:, capacity:].reshape(UNIT, width).astype(jnp.bfloat16)
     part = slice(6 * UNIT, 15 * UNIT)
     ff = out_ref.shape[0]
 
@@ -153,14 +149,14 @@
         columns = slice(start, start + step)
         put(
             columns,
-            dot(rows_ref[part, :], in_ref[:, columns]) + dot(twin_rows[part, :], twin_in_ref[:, columns]),
+            dot(both_ref[part, :width], in_ref[:, columns]) + dot(twin_ref[part, :width], twin_in_ref[:, columns]),
         )
     for start in range(0, ff, step):
         some = slice(start, start + step)
         put(
             slice(2 * ff + start, 2 * ff + start + step),
-            dot(back_ref[part, :], out_ref[some, :], LAST)
-            + dot(twin_back[part, :], twin_out_ref[some, :], LAST),
+            dot(both_ref[part, width:], out_ref[some, :], LAST)
+            + dot(twin_ref[part, width:], twin_out_ref[some, :], LAST),
         )
 
 
@@ -170,12 +166,9 @@
     sum_ref[UNIT:, :] = (total[UNIT:] + far_ref[...].astype(jnp.float32)).astype(jnp.bfloat16)
 
 
-def arrived_kernel(near_ref, passed_ref, sum_ref):
-    sum_ref[...] = near_ref[...].astype(jnp.float32) + passed_ref[...].astype(jnp.float32)
-
-
-def swish_kernel(own_ref, arrived_ref, twin_ref, mid_ref):
-    arrived, twin = arrived_ref[...], twin_ref[...]
+def swish_kernel(own_ref, near_ref, passed_ref, twin_near_ref, twin_passed_ref, mid_ref):
+    arrived = near_ref[...].astype(jnp.float32) + passed_ref[...].astype(jnp.float32)
+    twin = twin_near_ref[...].astype(jnp.float32) + twin_passed_ref[...].astype(jnp.float32)
     share = own_ref[...] + jnp.concatenate(
         [arrived[UNIT:] + twin[:UNIT], arrived[:UNIT] + twin[UNIT:]], axis=0
     )
@@ -284,11 +277,10 @@
     )
     got, twin_in, twin_out = lax.optimization_barrier((exchange(sent), *map(swap, staged)))
     all_columns = 3 * ff
-    routed_rows, routed_back, own, far, near, middle, third = call(
+    routed, own, far, near, middle, third = call(
         lambda *refs: sums_kernel(capacity, *refs),
         (
-            array(rows, width, bf16),
-            array(rows, width, bf16),
+            array(rows, 2 * width, bf16),
             array(2 * UNIT, all_columns, f32),
             array(UNIT, all_columns, bf16),
             array(2 * UNIT, all_columns, bf16),
@@ -303,7 +295,7 @@
         twin_in,
         weight_out,
         twin_out,
-        scratch=[pltpu.VMEM((rows, width), bf16), pltpu.VMEM((rows, width), bf16)],
+        scratch=[pltpu.VMEM((rows, 2 * width), bf16)],
         scalar_first=True,
     )
     third = along(third, 1)
@@ -312,9 +304,15 @@
     passed = along(
         call(gateway_kernel, array(2 * UNIT, all_columns, bf16), rows * ff, middle, third, far), 2
     )
-    arrived = call(arrived_kernel, array(2 * UNIT, all_columns, f32), rows * ff, near, passed)
     chip_mid = call(
-        swish_kernel, array(2 * UNIT, all_columns, bf16), rows * ff, own, arrived, swap(arrived)
+        swish_kernel,
+        array(2 * UNIT, all_columns, bf16),
+        rows * ff,
+        own,
+        near,
+        passed,
+        swap(near),
+        swap(passed),
     )
 
     second = along(chip_mid, 2)
@@ -344,8 +342,8 @@
     )
     home = exchange(back)
     hidden, grad_pre = full[:, :ff], full[:, ff:]
-    grad_input = dot(routed_rows, grad_pre, FIRST).astype(bf16)[None]
-    grad_output = dot(hidden, routed_back, FIRST).astype(bf16)[None]
+    grad_input = dot(routed[:, :width], grad_pre, FIRST).astype(bf16)[None]
+    grad_output = dot(hidden, routed[:, width:], FIRST).astype(bf16)[None]
     mixed, grad_tokens = call(
         lambda *refs: combine_kernel(capacity, *refs),
         (

time: 143 us -> 142 us (level)
  waiting for transfers between devices: 50.1 us -> 47.7 us
  starting transfers between devices: 77.8 us -> 79.7 us
    ppermute x8, waiting for transfers between devices: 16.1 us -> 14.2 us  [along(): return lax.ppermute(values, 'expert', up + down)]
    ppermute x8 -> x9, starting transfers between devices: 16.8 us -> 18.7 us  [swap(): lax.ppermute(values, 'expert', [(d, d ^ 1) for d in range(2 * chips)])]
    unnamed x16 -> x14, local copies, waits for them, and re-layouts: 3.55 us -> 2.93 us
    ppermute x8 -> x9, waiting for transfers between devices: 6.16 us -> 5.71 us  [swap(): lax.ppermute(values, 'expert', [(d, d ^ 1) for d in range(2 * chips)])]
    pallas_call x8 -> x7, Pallas kernels: 6.35 us -> 6.38 us  [call(): pl.pallas_call(kernel, out_shape=out_shape, in_specs=specs, scratch_shape...]
  transfers between devices with their start and end apart: 18 -> 19, of which waited for: 10 -> 10; matrix products, arithmetic and copies ran while one was open for 3% -> 3% of each run, Pallas kernels for 0% -> 0%
where the time goes in v7:
time: 142 us; the launch traced here: 141 us
  starting transfers between devices  79.7 us (56%)
  waiting for transfers between devices  47.7 us (34%)
  Pallas kernels  6.38 us (4%)
  matrix products  3.63 us (3%)
  local copies, waits for them, and re-layouts  2.94 us (2%)
    ppermute x8, starting transfers between devices, along(): return lax.ppermute(values, 'expert', up + down)  32.6 us
    all_to_all x2, starting transfers between devices, exchange(): lax.all_to_all(values, 'fsdp', split_axis=0, concat_axis=0, tiled=True)  28.4 us
    all_to_all x2, waiting for transfers between devices, exchange(): lax.all_to_all(values, 'fsdp', split_axis=0, concat_axis=0, tiled=True)  27.8 us
    ppermute x9, starting transfers between devices, swap(): lax.ppermute(values, 'expert', [(d, d ^ 1) for d in range(2 * chips)])  18.7 us
    ppermute x8, waiting for transfers between devices, along(): return lax.ppermute(values, 'expert', up + down)  14.2 us
    pallas_call x7, Pallas kernels, call(): pl.pallas_call(kernel, out_shape=out_shape, in_specs=specs, scratch_shape...  6.38 us
    ppermute x9, waiting for transfers between devices, swap(): lax.ppermute(values, 'expert', [(d, d ^ 1) for d in range(2 * chips)])  5.71 us
    dot_general x2, matrix products, dot(): return lax.dot_general(a, b, dims, preferred_element_type=jnp.float32)  3.63 us
  transfers between devices with their start and end apart: 19, of which 10 were waited for; matrix products, arithmetic and copies ran while one was open for 3% of the time, Pallas kernels for 0%

profile of v7, /device:TPU:34, one launch (start us, length us, event | category | flops | bytes accessed | tf_op | source)
XLA Modules:
  0.0 141.3 jit_solution(858738593575968635)
XLA Ops:
  0.7 2.4 %shard_map.93 = (bf16[64,16,256]{2,1,0:T(8,128)(2,1)}, bf16[512,128]{1,0:T(8,128)(2,1)}) custom-call(s32[8,32]{1,0:T(8,128)} %bitcast.15, f32[8,32]{1,0:T(8,128)} %bitcast.16, bf16[32,256]{1,0:T(8,128)(2,1)} %refs_2_.1, bf16[32,256]{1,0:T(8,128)(2,1)} %refs_3_.1), custom_call_target="tpu_custom_call" | custom-call | flops 41943040 | bytes 690176 | tf_op jit(solution)/shard_map/pallas_call | solution.py:217
  3.1 23.1 %all-to-all-start = ((bf16[64,16,256]{2,1,0:T(8,128)(2,1)}), bf16[64,16,256]{2,1,0:T(8,128)(2,1)S(1)}, u32[]{:S(2)}, u32[]{:S(2)}) async-start(bf16[64,16,256]{2,1,0:T(8,128)(2,1)} %get-tuple-element.26), calls=%async_computation | async-start | bytes 1048576 | tf_op jit(solution)/shard_map/all_to_all | solution.py:241
  26.2 1.1 copy-done
  28.4 1.9 %collective-permute-start = (bf16[256,1536]{1,0:T(8,128)(2,1)S(1)}, bf16[256,1536]{1,0:T(8,128)(2,1)S(1)}, u32[]{:S(2)}, u32[]{:S(2)}) collective-permute-start(bf16[256,1536]{1,0:T(8,128)(2,1)S(1)} %get-tuple-element.29), channel_id=1, source_target_pairs={{0,64},{64,0},{128,192},{192,128},{256,320},{320,256},{384,448},{4... | collective-permute-start | bytes 2359304 | tf_op jit(solution)/shard_map/ppermute | solution.py:244
  30.3 2.4 %collective-permute-start.1 = (bf16[768,256]{1,0:T(8,128)(2,1)S(1)}, bf16[768,256]{1,0:T(8,128)(2,1)S(1)}, u32[]{:S(2)}, u32[]{:S(2)}) collective-permute-start(bf16[768,256]{1,0:T(8,128)(2,1)S(1)} %get-tuple-element.30), channel_id=1, source_target_pairs={{0,64},{64,0},{128,192},{192,128},{256,320},{320,256},{384,448},{4... | collective-permute-start | bytes 1179656 | tf_op jit(solution)/shard_map/ppermute | solution.py:244
  32.7 1.3 collective-permute-done.1.refs_6_
  34.1 11.5 %all-to-all-done.refs_1_ = bf16[64,16,256]{2,1,0:T(8,128)(2,1)S(1)} async-done(((bf16[64,16,256]{2,1,0:T(8,128)(2,1)}), bf16[64,16,256]{2,1,0:T(8,128)(2,1)S(1)}, u32[]{:S(2)}, u32[]{:S(2)}) %all-to-all-start) | async-done | bytes 524320 | tf_op jit(solution)/shard_map/all_to_all | solution.py:241
  45.6 1.9 %collective-permute-start.2 = (bf16[64,16,256]{2,1,0:T(8,128)(2,1)S(1)}, bf16[64,16,256]{2,1,0:T(8,128)(2,1)S(1)}, u32[]{:S(2)}, u32[]{:S(2)}) collective-permute-start(bf16[64,16,256]{2,1,0:T(8,128)(2,1)S(1)} %all-to-all-done.refs_1_), channel_id=1, source_target_pairs={{0,64},{64,0},{128,192},{192,128},{256,320},{320,256},{384,448},{4... | collective-permute-start | bytes 1572872 | tf_op jit(solution)/shard_map/ppermute | solution.py:244
  47.5 1.9 %collective-permute-done.2.refs_2_ = bf16[64,16,256]{2,1,0:T(8,128)(2,1)S(1)} collective-permute-done((bf16[64,16,256]{2,1,0:T(8,128)(2,1)S(1)}, bf16[64,16,256]{2,1,0:T(8,128)(2,1)S(1)}, u32[]{:S(2)}, u32[]{:S(2)}) %collective-permute-start.2) | collective-permute-done | bytes 524320 | tf_op jit(solution)/shard_map/ppermute | solution.py:244
  51.3 3.4 %collective-permute-start.4 = (bf16[64,2304]{1,0:T(8,128)(2,1)S(1)}, bf16[64,2304]{1,0:T(8,128)(2,1)S(1)}, u32[]{:S(2)}, u32[]{:S(2)}) collective-permute-start(bf16[64,2304]{1,0:T(8,128)(2,1)S(1)} %get-tuple-element.37), channel_id=1, source_target_pairs={{0,128},{128,256},{256,384},{384,512},{512,640},{640,768},{768,896... | collective-permute-start | bytes 884744 | tf_op jit(solution)/shard_map/ppermute | solution.py:249
  54.7 5.5 %collective-permute-start.5 = (bf16[32,2304]{1,0:T(8,128)(2,1)S(1)}, bf16[32,2304]{1,0:T(8,128)(2,1)S(1)}, u32[]{:S(2)}, u32[]{:S(2)}) collective-permute-start(bf16[32,2304]{1,0:T(8,128)(2,1)S(1)} %get-tuple-element.38), channel_id=1, source_target_pairs={{0,256},{128,384},{256,512},{384,640},{512,768},{640,896},{768,0},... | collective-permute-start | bytes 442376 | tf_op jit(solution)/shard_map/ppermute | solution.py:249
  60.2 2.5 %collective-permute-start.3 = (bf16[64,2304]{1,0:T(8,128)(2,1)S(1)}, bf16[64,2304]{1,0:T(8,128)(2,1)S(1)}, u32[]{:S(2)}, u32[]{:S(2)}) collective-permute-start(bf16[64,2304]{1,0:T(8,128)(2,1)S(1)} %get-tuple-element.35), channel_id=1, source_target_pairs={{0,128},{128,256},{256,384},{384,512},{512,640},{640,768},{768,896... | collective-permute-start | bytes 884744 | tf_op jit(solution)/shard_map/ppermute | solution.py:249
  62.7 2.6 %collective-permute-done.5.far_ref = bf16[32,2304]{1,0:T(8,128)(2,1)S(1)} collective-permute-done((bf16[32,2304]{1,0:T(8,128)(2,1)S(1)}, bf16[32,2304]{1,0:T(8,128)(2,1)S(1)}, u32[]{:S(2)}, u32[]{:S(2)}) %collective-permute-start.5) | collective-permute-done | bytes 147488 | tf_op jit(solution)/shard_map/ppermute | solution.py:249
  65.5 3.1 %collective-permute-start.6 = (bf16[64,2304]{1,0:T(8,128)(2,1)S(1)}, bf16[64,2304]{1,0:T(8,128)(2,1)S(1)}, u32[]{:S(2)}, u32[]{:S(2)}) collective-permute-start(bf16[64,2304]{1,0:T(8,128)(2,1)S(1)} %shard_map.96), channel_id=1, source_target_pairs={{0,256},{128,384},{256,512},{384,640},{512,768},{640,896},{768,0},... | collective-permute-start | bytes 884744 | tf_op jit(solution)/shard_map/ppermute | solution.py:249
  68.8 1.9 %collective-permute-start.7 = (bf16[64,2304]{1,0:T(8,128)(2,1)S(1)}, bf16[64,2304]{1,0:T(8,128)(2,1)S(1)}, u32[]{:S(2)}, u32[]{:S(2)}) collective-permute-start(bf16[64,2304]{1,0:T(8,128)(2,1)S(1)} %collective-permute-done.3.near_ref), channel_id=1, source_target_pairs={{0,64},{64,0},{128,192},{192,128},{256,320},{320,256},{384,448},{4... | collective-permute-start | bytes 884744 | tf_op jit(solution)/shard_map/ppermute | solution.py:244
  70.8 8.0 %collective-permute-done.6.passed_ref = bf16[64,2304]{1,0:T(8,128)(2,1)S(1)} collective-permute-done((bf16[64,2304]{1,0:T(8,128)(2,1)S(1)}, bf16[64,2304]{1,0:T(8,128)(2,1)S(1)}, u32[]{:S(2)}, u32[]{:S(2)}) %collective-permute-start.6) | collective-permute-done | bytes 294944 | tf_op jit(solution)/shard_map/ppermute | solution.py:249
  78.7 1.9 %collective-permute-start.8 = (bf16[64,2304]{1,0:T(8,128)(2,1)S(1)}, bf16[64,2304]{1,0:T(8,128)(2,1)S(1)}, u32[]{:S(2)}, u32[]{:S(2)}) collective-permute-start(bf16[64,2304]{1,0:T(8,128)(2,1)S(1)} %collective-permute-done.6.passed_ref), channel_id=1, source_target_pairs={{0,64},{64,0},{128,192},{192,128},{256,320},{320,256},{384,448},{4... | collective-permute-start | bytes 884744 | tf_op jit(solution)/shard_map/ppermute | solution.py:244
  80.7 1.5 %collective-permute-done.8.twin_passed_ref = bf16[64,2304]{1,0:T(8,128)(2,1)S(1)} collective-permute-done((bf16[64,2304]{1,0:T(8,128)(2,1)S(1)}, bf16[64,2304]{1,0:T(8,128)(2,1)S(1)}, u32[]{:S(2)}, u32[]{:S(2)}) %collective-permute-start.8) | collective-permute-done | bytes 294944 | tf_op jit(solution)/shard_map/ppermute | solution.py:244
  82.4 1.9 %collective-permute-start.10 = (bf16[64,2304]{1,0:T(8,128)(2,1)S(1)}, bf16[64,2304]{1,0:T(8,128)(2,1)S(1)}, u32[]{:S(2)}, u32[]{:S(2)}) collective-permute-start(bf16[64,2304]{1,0:T(8,128)(2,1)S(1)} %shard_map.97.refs_6_), channel_id=1, source_target_pairs={{0,256},{128,384},{256,512},{384,640},{512,768},{640,896},{768,0},... | collective-permute-start | bytes 884744 | tf_op jit(solution)/shard_map/ppermute | solution.py:249
  84.4 6.8 %collective-permute-start.9 = (bf16[64,2304]{1,0:T(8,128)(2,1)S(1)}, bf16[64,2304]{1,0:T(8,128)(2,1)S(1)}, u32[]{:S(2)}, u32[]{:S(2)}) collective-permute-start(bf16[64,2304]{1,0:T(8,128)(2,1)S(1)} %shard_map.97.refs_6_), channel_id=1, source_target_pairs={{0,128},{128,256},{256,384},{384,512},{512,640},{640,768},{768,896... | collective-permute-start | bytes 884744 | tf_op jit(solution)/shard_map/ppermute | solution.py:249
  91.2 3.3 %collective-permute-done.10.refs_4_ = bf16[64,2304]{1,0:T(8,128)(2,1)S(1)} collective-permute-done((bf16[64,2304]{1,0:T(8,128)(2,1)S(1)}, bf16[64,2304]{1,0:T(8,128)(2,1)S(1)}, u32[]{:S(2)}, u32[]{:S(2)}) %collective-permute-start.10) | collective-permute-done | bytes 294944 | tf_op jit(solution)/shard_map/ppermute | solution.py:249
  94.5 2.7 %collective-permute-start.11 = (bf16[64,2304]{1,0:T(8,128)(2,1)S(1)}, bf16[64,2304]{1,0:T(8,128)(2,1)S(1)}, u32[]{:S(2)}, u32[]{:S(2)}) collective-permute-start(bf16[64,2304]{1,0:T(8,128)(2,1)S(1)} %collective-permute-done.10.refs_4_), channel_id=1, source_target_pairs={{0,128},{128,256},{256,384},{384,512},{512,640},{640,768},{768,896... | collective-permute-start | bytes 884744 | tf_op jit(solution)/shard_map/ppermute | solution.py:249
  97.3 6.6 %collective-permute-start.12 = (bf16[32,2304]{1,0:T(8,128)(2,1)S(1)}, bf16[32,2304]{1,0:T(8,128)(2,1)S(1)}, u32[]{:S(2)}, u32[]{:S(2)}) collective-permute-start(bf16[32,2304]{1,0:T(8,128)(2,1)S(1)} %slice.20), channel_id=1, source_target_pairs={{0,256},{128,384},{256,512},{384,640},{512,768},{640,896},{768,0},... | collective-permute-start | bytes 442376 | tf_op jit(solution)/shard_map/ppermute | solution.py:249
  103.8 1.9 %collective-permute-start.14 = (bf16[64,2304]{1,0:T(8,128)(2,1)S(1)}, bf16[64,2304]{1,0:T(8,128)(2,1)S(1)}, u32[]{:S(2)}, u32[]{:S(2)}) collective-permute-start(bf16[64,2304]{1,0:T(8,128)(2,1)S(1)} %collective-permute-done.10.refs_4_), channel_id=1, source_target_pairs={{0,64},{64,0},{128,192},{192,128},{256,320},{320,256},{384,448},{4... | collective-permute-start | bytes 884744 | tf_op jit(solution)/shard_map/ppermute | solution.py:244
  105.8 2.4 %collective-permute-start.13 = (bf16[64,2304]{1,0:T(8,128)(2,1)S(1)}, bf16[64,2304]{1,0:T(8,128)(2,1)S(1)}, u32[]{:S(2)}, u32[]{:S(2)}) collective-permute-start(bf16[64,2304]{1,0:T(8,128)(2,1)S(1)} %collective-permute-done.9.refs_3_), channel_id=1, source_target_pairs={{0,64},{64,0},{128,192},{192,128},{256,320},{320,256},{384,448},{4... | collective-permute-start | bytes 884744 | tf_op jit(solution)/shard_map/ppermute | solution.py:244
  108.2 1.9 %collective-permute-start.15 = (bf16[64,2304]{1,0:T(8,128)(2,1)S(1)}, bf16[64,2304]{1,0:T(8,128)(2,1)S(1)}, u32[]{:S(2)}, u32[]{:S(2)}) collective-permute-start(bf16[64,2304]{1,0:T(8,128)(2,1)S(1)} %collective-permute-done.11.refs_5_), channel_id=1, source_target_pairs={{0,64},{64,0},{128,192},{192,128},{256,320},{320,256},{384,448},{4... | collective-permute-start | bytes 884744 | tf_op jit(solution)/shard_map/ppermute | solution.py:244
  110.2 2.4 %collective-permute-start.16 = (bf16[32,2304]{1,0:T(8,128)(2,1)S(1)}, bf16[32,2304]{1,0:T(8,128)(2,1)S(1)}, u32[]{:S(2)}, u32[]{:S(2)}) collective-permute-start(bf16[32,2304]{1,0:T(8,128)(2,1)S(1)} %collective-permute-done.12.refs_7_), channel_id=1, source_target_pairs={{0,64},{64,0},{128,192},{192,128},{256,320},{320,256},{384,448},{4... | collective-permute-start | bytes 442376 | tf_op jit(solution)/shard_map/ppermute | solution.py:244
  113.6 1.6 %shard_map.98 = (bf16[64,16,256]{2,1,0:T(8,128)(2,1)}, bf16[512,2304]{1,0:T(8,128)(2,1)S(1)}) custom-call(s32[1]{0:T(128)} %bitcast.2.refs_0_, bf16[256,1536]{1,0:T(8,128)(2,1)S(1)} %bitcast.11, bf16[768,256]{1,0:T(8,128)(2,1)S(1)} %bitcast.14, bf16[64,2304]{1,0:T(8,128)(2,1)S(1)} %collective-permute-done.9.refs_3_, ...), custom_call_target="tpu_custom_call" | custom-call | flops 603979776 | bytes 6422532 | tf_op jit(solution)/shard_map/pallas_call | solution.py:217
  115.2 5.4 %all-to-all-start.1 = ((bf16[64,16,256]{2,1,0:T(8,128)(2,1)}), bf16[64,16,256]{2,1,0:T(8,128)(2,1)S(1)}, u32[]{:S(2)}, u32[]{:S(2)}) async-start(bf16[64,16,256]{2,1,0:T(8,128)(2,1)} %get-tuple-element.39), calls=%async_computation.1 | async-start | bytes 1048576 | tf_op jit(solution)/shard_map/all_to_all | solution.py:241
  120.5 2.2 %fusion.2 = bf16[1,768,256]{2,1,0:T(8,128)(2,1)} fusion(bf16[512,2304]{1,0:T(8,128)(2,1)S(1)} %get-tuple-element.43, bf16[512,512]{1,0:T(8,128)(2,1)} %copy-done.5), kind=kOutput, calls=%fused_computation.4 | convolution fusion | flops 201523200 | bytes 1441792 | tf_op jit(solution)/shard_map/dot_general | solution.py:15
  122.7 1.5 %fusion = bf16[1,256,1536]{2,1,0:T(8,128)(2,1)} fusion(bf16[512,2304]{1,0:T(8,128)(2,1)S(1)} %get-tuple-element.43, bf16[512,512]{1,0:T(8,128)(2,1)S(1)} %copy-done.6), kind=kOutput, calls=%fused_computation.1 | convolution fusion | flops 403046400 | bytes 2621440 | tf_op jit(solution)/shard_map/dot_general | solution.py:15
  124.2 16.3 %all-to-all-done.1.refs_1_ = bf16[64,16,256]{2,1,0:T(8,128)(2,1)S(1)} async-done(((bf16[64,16,256]{2,1,0:T(8,128)(2,1)}), bf16[64,16,256]{2,1,0:T(8,128)(2,1)S(1)}, u32[]{:S(2)}, u32[]{:S(2)}) %all-to-all-start.1) | async-done | bytes 524320 | tf_op jit(solution)/shard_map/all_to_all | solution.py:241
  (30 shorter events, 5.4 us)
Async XLA Ops:
  0.6 48.8 %copy-start.3 = (bf16[1,768,256]{2,1,0:T(8,128)(2,1)S(1)}, bf16[1,768,256]{2,1,0:T(8,128)(2,1)}, u32[]{:S(2)}) copy-start(bf16[1,768,256]{2,1,0:T(8,128)(2,1)} %param.8) | copy-start | bytes 1179652
  0.6 48.7 %copy-start.1 = (bf16[1,256,1536]{2,1,0:T(8,128)(2,1)S(1)}, bf16[1,256,1536]{2,1,0:T(8,128)(2,1)}, u32[]{:S(2)}) copy-start(bf16[1,256,1536]{2,1,0:T(8,128)(2,1)} %param.7) | copy-start | bytes 2359300
  3.1 42.5 %all-to-all-start = ((bf16[64,16,256]{2,1,0:T(8,128)(2,1)}), bf16[64,16,256]{2,1,0:T(8,128)(2,1)S(1)}, u32[]{:S(2)}, u32[]{:S(2)}) async-start(bf16[64,16,256]{2,1,0:T(8,128)(2,1)} %get-tuple-element.26), calls=%async_computation | async-start | bytes 1048576 | tf_op jit(solution)/shard_map/all_to_all | solution.py:241
  26.2 1.1 copy-start
  27.3 1.0 copy-start.2
  28.4 5.7 %collective-permute-start = (bf16[256,1536]{1,0:T(8,128)(2,1)S(1)}, bf16[256,1536]{1,0:T(8,128)(2,1)S(1)}, u32[]{:S(2)}, u32[]{:S(2)}) collective-permute-start(bf16[256,1536]{1,0:T(8,128)(2,1)S(1)} %get-tuple-element.29), channel_id=1, source_target_pairs={{0,64},{64,0},{128,192},{192,128},{256,320},{320,256},{384,448},{4... | collective-permute-start | bytes 2359304 | tf_op jit(solution)/shard_map/ppermute | solution.py:244
  30.3 3.7 %collective-permute-start.1 = (bf16[768,256]{1,0:T(8,128)(2,1)S(1)}, bf16[768,256]{1,0:T(8,128)(2,1)S(1)}, u32[]{:S(2)}, u32[]{:S(2)}) collective-permute-start(bf16[768,256]{1,0:T(8,128)(2,1)S(1)} %get-tuple-element.30), channel_id=1, source_target_pairs={{0,64},{64,0},{128,192},{192,128},{256,320},{320,256},{384,448},{4... | collective-permute-start | bytes 1179656 | tf_op jit(solution)/shard_map/ppermute | solution.py:244
  45.6 3.8 %collective-permute-start.2 = (bf16[64,16,256]{2,1,0:T(8,128)(2,1)S(1)}, bf16[64,16,256]{2,1,0:T(8,128)(2,1)S(1)}, u32[]{:S(2)}, u32[]{:S(2)}) collective-permute-start(bf16[64,16,256]{2,1,0:T(8,128)(2,1)S(1)} %all-to-all-done.refs_1_), channel_id=1, source_target_pairs={{0,64},{64,0},{128,192},{192,128},{256,320},{320,256},{384,448},{4... | collective-permute-start | bytes 1572872 | tf_op jit(solution)/shard_map/ppermute | solution.py:244
  50.5 0.8 copy-start.5
  51.3 14.1 %collective-permute-start.4 = (bf16[64,2304]{1,0:T(8,128)(2,1)S(1)}, bf16[64,2304]{1,0:T(8,128)(2,1)S(1)}, u32[]{:S(2)}, u32[]{:S(2)}) collective-permute-start(bf16[64,2304]{1,0:T(8,128)(2,1)S(1)} %get-tuple-element.37), channel_id=1, source_target_pairs={{0,128},{128,256},{256,384},{384,512},{512,640},{640,768},{768,896... | collective-permute-start | bytes 884744 | tf_op jit(solution)/shard_map/ppermute | solution.py:249
  54.7 10.7 %collective-permute-start.5 = (bf16[32,2304]{1,0:T(8,128)(2,1)S(1)}, bf16[32,2304]{1,0:T(8,128)(2,1)S(1)}, u32[]{:S(2)}, u32[]{:S(2)}) collective-permute-start(bf16[32,2304]{1,0:T(8,128)(2,1)S(1)} %get-tuple-element.38), channel_id=1, source_target_pairs={{0,256},{128,384},{256,512},{384,640},{512,768},{640,896},{768,0},... | collective-permute-start | bytes 442376 | tf_op jit(solution)/shard_map/ppermute | solution.py:249
  60.2 8.6 %collective-permute-start.3 = (bf16[64,2304]{1,0:T(8,128)(2,1)S(1)}, bf16[64,2304]{1,0:T(8,128)(2,1)S(1)}, u32[]{:S(2)}, u32[]{:S(2)}) collective-permute-start(bf16[64,2304]{1,0:T(8,128)(2,1)S(1)} %get-tuple-element.35), channel_id=1, source_target_pairs={{0,128},{128,256},{256,384},{384,512},{512,640},{640,768},{768,896... | collective-permute-start | bytes 884744 | tf_op jit(solution)/shard_map/ppermute | solution.py:249
  65.5 13.3 %collective-permute-start.6 = (bf16[64,2304]{1,0:T(8,128)(2,1)S(1)}, bf16[64,2304]{1,0:T(8,128)(2,1)S(1)}, u32[]{:S(2)}, u32[]{:S(2)}) collective-permute-start(bf16[64,2304]{1,0:T(8,128)(2,1)S(1)} %shard_map.96), channel_id=1, source_target_pairs={{0,256},{128,384},{256,512},{384,640},{512,768},{640,896},{768,0},... | collective-permute-start | bytes 884744 | tf_op jit(solution)/shard_map/ppermute | solution.py:249
  68.8 11.8 %collective-permute-start.7 = (bf16[64,2304]{1,0:T(8,128)(2,1)S(1)}, bf16[64,2304]{1,0:T(8,128)(2,1)S(1)}, u32[]{:S(2)}, u32[]{:S(2)}) collective-permute-start(bf16[64,2304]{1,0:T(8,128)(2,1)S(1)} %collective-permute-done.3.near_ref), channel_id=1, source_target_pairs={{0,64},{64,0},{128,192},{192,128},{256,320},{320,256},{384,448},{4... | collective-permute-start | bytes 884744 | tf_op jit(solution)/shard_map/ppermute | solution.py:244
  78.7 3.5 %collective-permute-start.8 = (bf16[64,2304]{1,0:T(8,128)(2,1)S(1)}, bf16[64,2304]{1,0:T(8,128)(2,1)S(1)}, u32[]{:S(2)}, u32[]{:S(2)}) collective-permute-start(bf16[64,2304]{1,0:T(8,128)(2,1)S(1)} %collective-permute-done.6.passed_ref), channel_id=1, source_target_pairs={{0,64},{64,0},{128,192},{192,128},{256,320},{320,256},{384,448},{4... | collective-permute-start | bytes 884744 | tf_op jit(solution)/shard_map/ppermute | solution.py:244
  82.4 12.1 %collective-permute-start.10 = (bf16[64,2304]{1,0:T(8,128)(2,1)S(1)}, bf16[64,2304]{1,0:T(8,128)(2,1)S(1)}, u32[]{:S(2)}, u32[]{:S(2)}) collective-permute-start(bf16[64,2304]{1,0:T(8,128)(2,1)S(1)} %shard_map.97.refs_6_), channel_id=1, source_target_pairs={{0,256},{128,384},{256,512},{384,640},{512,768},{640,896},{768,0},... | collective-permute-start | bytes 884744 | tf_op jit(solution)/shard_map/ppermute | solution.py:249
  84.4 21.4 %collective-permute-start.9 = (bf16[64,2304]{1,0:T(8,128)(2,1)S(1)}, bf16[64,2304]{1,0:T(8,128)(2,1)S(1)}, u32[]{:S(2)}, u32[]{:S(2)}) collective-permute-start(bf16[64,2304]{1,0:T(8,128)(2,1)S(1)} %shard_map.97.refs_6_), channel_id=1, source_target_pairs={{0,128},{128,256},{256,384},{384,512},{512,640},{640,768},{768,896... | collective-permute-start | bytes 884744 | tf_op jit(solution)/shard_map/ppermute | solution.py:249
  94.5 13.7 %collective-permute-start.11 = (bf16[64,2304]{1,0:T(8,128)(2,1)S(1)}, bf16[64,2304]{1,0:T(8,128)(2,1)S(1)}, u32[]{:S(2)}, u32[]{:S(2)}) collective-permute-start(bf16[64,2304]{1,0:T(8,128)(2,1)S(1)} %collective-permute-done.10.refs_4_), channel_id=1, source_target_pairs={{0,128},{128,256},{256,384},{384,512},{512,640},{640,768},{768,896... | collective-permute-start | bytes 884744 | tf_op jit(solution)/shard_map/ppermute | solution.py:249
  97.3 12.9 %collective-permute-start.12 = (bf16[32,2304]{1,0:T(8,128)(2,1)S(1)}, bf16[32,2304]{1,0:T(8,128)(2,1)S(1)}, u32[]{:S(2)}, u32[]{:S(2)}) collective-permute-start(bf16[32,2304]{1,0:T(8,128)(2,1)S(1)} %slice.20), channel_id=1, source_target_pairs={{0,256},{128,384},{256,512},{384,640},{512,768},{640,896},{768,0},... | collective-permute-start | bytes 442376 | tf_op jit(solution)/shard_map/ppermute | solution.py:249
  103.8 8.7 %collective-permute-start.14 = (bf16[64,2304]{1,0:T(8,128)(2,1)S(1)}, bf16[64,2304]{1,0:T(8,128)(2,1)S(1)}, u32[]{:S(2)}, u32[]{:S(2)}) collective-permute-start(bf16[64,2304]{1,0:T(8,128)(2,1)S(1)} %collective-permute-done.10.refs_4_), channel_id=1, source_target_pairs={{0,64},{64,0},{128,192},{192,128},{256,320},{320,256},{384,448},{4... | collective-permute-start | bytes 884744 | tf_op jit(solution)/shard_map/ppermute | solution.py:244
  105.8 6.8 %collective-permute-start.13 = (bf16[64,2304]{1,0:T(8,128)(2,1)S(1)}, bf16[64,2304]{1,0:T(8,128)(2,1)S(1)}, u32[]{:S(2)}, u32[]{:S(2)}) collective-permute-start(bf16[64,2304]{1,0:T(8,128)(2,1)S(1)} %collective-permute-done.9.refs_3_), channel_id=1, source_target_pairs={{0,64},{64,0},{128,192},{192,128},{256,320},{320,256},{384,448},{4... | collective-permute-start | bytes 884744 | tf_op jit(solution)/shard_map/ppermute | solution.py:244
  108.2 5.3 %collective-permute-start.15 = (bf16[64,2304]{1,0:T(8,128)(2,1)S(1)}, bf16[64,2304]{1,0:T(8,128)(2,1)S(1)}, u32[]{:S(2)}, u32[]{:S(2)}) collective-permute-start(bf16[64,2304]{1,0:T(8,128)(2,1)S(1)} %collective-permute-done.11.refs_5_), channel_id=1, source_target_pairs={{0,64},{64,0},{128,192},{192,128},{256,320},{320,256},{384,448},{4... | collective-permute-start | bytes 884744 | tf_op jit(solution)/shard_map/ppermute | solution.py:244
  110.2 3.4 %collective-permute-start.16 = (bf16[32,2304]{1,0:T(8,128)(2,1)S(1)}, bf16[32,2304]{1,0:T(8,128)(2,1)S(1)}, u32[]{:S(2)}, u32[]{:S(2)}) collective-permute-start(bf16[32,2304]{1,0:T(8,128)(2,1)S(1)} %collective-permute-done.12.refs_7_), channel_id=1, source_target_pairs={{0,64},{64,0},{128,192},{192,128},{256,320},{320,256},{384,448},{4... | collective-permute-start | bytes 442376 | tf_op jit(solution)/shard_map/ppermute | solution.py:244
  115.2 7.5 %copy-start.6 = (bf16[512,512]{1,0:T(8,128)(2,1)S(1)}, bf16[512,512]{1,0:T(8,128)(2,1)}, u32[]{:S(2)}) copy-start(bf16[512,512]{1,0:T(8,128)(2,1)} %copy-done.5) | copy-start | bytes 1572868
  115.2 25.3 %all-to-all-start.1 = ((bf16[64,16,256]{2,1,0:T(8,128)(2,1)}), bf16[64,16,256]{2,1,0:T(8,128)(2,1)S(1)}, u32[]{:S(2)}, u32[]{:S(2)}) async-start(bf16[64,16,256]{2,1,0:T(8,128)(2,1)} %get-tuple-element.39), calls=%async_computation.1 | async-start | bytes 1048576 | tf_op jit(solution)/shard_map/all_to_all | solution.py:241
  120.5 19.9 %copy-start.4 = (bf16[512,128]{1,0:T(8,128)(2,1)S(1)}, bf16[512,128]{1,0:T(8,128)(2,1)}, u32[]{:S(2)}) copy-start(bf16[512,128]{1,0:T(8,128)(2,1)} %get-tuple-element.24.refs_0_) | copy-start | bytes 393220

commit v8 on v7

--- a/solution.py
+++ b/solution.py
@@ -318,7 +318,7 @@
     second = along(chip_mid, 2)
     first = along(chip_mid, 1)
     third = along(second, 1)
-    far = along(second[:UNIT], 2)
+    far = along(third[:UNIT], 1)
     back, full = call(
         lambda *refs: results_kernel(capacity, *refs),
         (

time: 142 us -> 145 us (1.021)
  the two profiles are of different devices: /device:TPU:34 before, /device:TPU:40 now
where the time goes in v8:
time: 145 us; the launch traced here: 144 us
  waiting for transfers between devices  66.4 us (46%)
  starting transfers between devices  63.5 us (44%)
  Pallas kernels  6.4 us (4%)
  matrix products  3.62 us (2%)
  local copies, waits for them, and re-layouts  2.94 us (2%)
    ppermute x8, waiting for transfers between devices, along(): return lax.ppermute(values, 'expert', up + down)  32.7 us
    all_to_all x2, starting transfers between devices, exchange(): lax.all_to_all(values, 'fsdp', split_axis=0, concat_axis=0, tiled=True)  28.4 us
    all_to_all x2, waiting for transfers between devices, exchange(): lax.all_to_all(values, 'fsdp', split_axis=0, concat_axis=0, tiled=True)  27.6 us
    ppermute x9, starting transfers between devices, swap(): lax.ppermute(values, 'expert', [(d, d ^ 1) for d in range(2 * chips)])  18.2 us
    ppermute x8, starting transfers between devices, along(): return lax.ppermute(values, 'expert', up + down)  16.9 us
    pallas_call x7, Pallas kernels, call(): pl.pallas_call(kernel, out_shape=out_shape, in_specs=specs, scratch_shape...  6.4 us
    ppermute x9, waiting for transfers between devices, swap(): lax.ppermute(values, 'expert', [(d, d ^ 1) for d in range(2 * chips)])  6.07 us
    dot_general x2, matrix products, dot(): return lax.dot_general(a, b, dims, preferred_element_type=jnp.float32)  3.62 us
  transfers between devices with their start and end apart: 19, of which 12 were waited for; matrix products, arithmetic and copies ran while one was open for 3% of the time, Pallas kernels for 0%

profile of v8, /device:TPU:40, one launch (start us, length us, event | category | flops | bytes accessed | tf_op | source)
XLA Modules:
  0.0 143.8 jit_solution(12128404524400162017)
XLA Ops:
  0.7 2.4 %shard_map.93 = (bf16[64,16,256]{2,1,0:T(8,128)(2,1)}, bf16[512,128]{1,0:T(8,128)(2,1)}) custom-call(s32[8,32]{1,0:T(8,128)} %bitcast.15, f32[8,32]{1,0:T(8,128)} %bitcast.16, bf16[32,256]{1,0:T(8,128)(2,1)} %refs_2_.1, bf16[32,256]{1,0:T(8,128)(2,1)} %refs_3_.1), custom_call_target="tpu_custom_call" | custom-call | flops 41943040 | bytes 690176 | tf_op jit(solution)/shard_map/pallas_call | solution.py:217
  3.1 23.1 %all-to-all-start = ((bf16[64,16,256]{2,1,0:T(8,128)(2,1)}), bf16[64,16,256]{2,1,0:T(8,128)(2,1)S(1)}, u32[]{:S(2)}, u32[]{:S(2)}) async-start(bf16[64,16,256]{2,1,0:T(8,128)(2,1)} %get-tuple-element.26), calls=%async_computation | async-start | bytes 1048576 | tf_op jit(solution)/shard_map/all_to_all | solution.py:241
  28.4 1.9 %collective-permute-start = (bf16[256,1536]{1,0:T(8,128)(2,1)S(1)}, bf16[256,1536]{1,0:T(8,128)(2,1)S(1)}, u32[]{:S(2)}, u32[]{:S(2)}) collective-permute-start(bf16[256,1536]{1,0:T(8,128)(2,1)S(1)} %get-tuple-element.29), channel_id=1, source_target_pairs={{0,64},{64,0},{128,192},{192,128},{256,320},{320,256},{384,448},{4... | collective-permute-start | bytes 2359304 | tf_op jit(solution)/shard_map/ppermute | solution.py:244
  30.3 2.4 %collective-permute-start.1 = (bf16[768,256]{1,0:T(8,128)(2,1)S(1)}, bf16[768,256]{1,0:T(8,128)(2,1)S(1)}, u32[]{:S(2)}, u32[]{:S(2)}) collective-permute-start(bf16[768,256]{1,0:T(8,128)(2,1)S(1)} %get-tuple-element.30), channel_id=1, source_target_pairs={{0,64},{64,0},{128,192},{192,128},{256,320},{320,256},{384,448},{4... | collective-permute-start | bytes 1179656 | tf_op jit(solution)/shard_map/ppermute | solution.py:244
  34.1 11.5 %all-to-all-done.refs_1_ = bf16[64,16,256]{2,1,0:T(8,128)(2,1)S(1)} async-done(((bf16[64,16,256]{2,1,0:T(8,128)(2,1)}), bf16[64,16,256]{2,1,0:T(8,128)(2,1)S(1)}, u32[]{:S(2)}, u32[]{:S(2)}) %all-to-all-start) | async-done | bytes 524320 | tf_op jit(solution)/shard_map/all_to_all | solution.py:241
  45.6 1.9 %collective-permute-start.2 = (bf16[64,16,256]{2,1,0:T(8,128)(2,1)S(1)}, bf16[64,16,256]{2,1,0:T(8,128)(2,1)S(1)}, u32[]{:S(2)}, u32[]{:S(2)}) collective-permute-start(bf16[64,16,256]{2,1,0:T(8,128)(2,1)S(1)} %all-to-all-done.refs_1_), channel_id=1, source_target_pairs={{0,64},{64,0},{128,192},{192,128},{256,320},{320,256},{384,448},{4... | collective-permute-start | bytes 1572872 | tf_op jit(solution)/shard_map/ppermute | solution.py:244
  47.5 1.9 %collective-permute-done.2.refs_2_ = bf16[64,16,256]{2,1,0:T(8,128)(2,1)S(1)} collective-permute-done((bf16[64,16,256]{2,1,0:T(8,128)(2,1)S(1)}, bf16[64,16,256]{2,1,0:T(8,128)(2,1)S(1)}, u32[]{:S(2)}, u32[]{:S(2)}) %collective-permute-start.2) | collective-permute-done | bytes 524320 | tf_op jit(solution)/shard_map/ppermute | solution.py:244
  51.3 2.5 %collective-permute-start.4 = (bf16[64,2304]{1,0:T(8,128)(2,1)S(1)}, bf16[64,2304]{1,0:T(8,128)(2,1)S(1)}, u32[]{:S(2)}, u32[]{:S(2)}) collective-permute-start(bf16[64,2304]{1,0:T(8,128)(2,1)S(1)} %get-tuple-element.37), channel_id=1, source_target_pairs={{0,128},{128,256},{256,384},{384,512},{512,640},{640,768},{768,896... | collective-permute-start | bytes 884744 | tf_op jit(solution)/shard_map/ppermute | solution.py:249
  53.8 2.5 %collective-permute-start.5 = (bf16[32,2304]{1,0:T(8,128)(2,1)S(1)}, bf16[32,2304]{1,0:T(8,128)(2,1)S(1)}, u32[]{:S(2)}, u32[]{:S(2)}) collective-permute-start(bf16[32,2304]{1,0:T(8,128)(2,1)S(1)} %get-tuple-element.38), channel_id=1, source_target_pairs={{0,256},{128,384},{256,512},{384,640},{512,768},{640,896},{768,0},... | collective-permute-start | bytes 442376 | tf_op jit(solution)/shard_map/ppermute | solution.py:249
  56.3 2.3 %collective-permute-start.3 = (bf16[64,2304]{1,0:T(8,128)(2,1)S(1)}, bf16[64,2304]{1,0:T(8,128)(2,1)S(1)}, u32[]{:S(2)}, u32[]{:S(2)}) collective-permute-start(bf16[64,2304]{1,0:T(8,128)(2,1)S(1)} %get-tuple-element.35), channel_id=1, source_target_pairs={{0,128},{128,256},{256,384},{384,512},{512,640},{640,768},{768,896... | collective-permute-start | bytes 884744 | tf_op jit(solution)/shard_map/ppermute | solution.py:249
  58.6 6.0 %collective-permute-done.5.far_ref = bf16[32,2304]{1,0:T(8,128)(2,1)S(1)} collective-permute-done((bf16[32,2304]{1,0:T(8,128)(2,1)S(1)}, bf16[32,2304]{1,0:T(8,128)(2,1)S(1)}, u32[]{:S(2)}, u32[]{:S(2)}) %collective-permute-start.5) | collective-permute-done | bytes 147488 | tf_op jit(solution)/shard_map/ppermute | solution.py:249
  64.7 1.9 %collective-permute-start.6 = (bf16[64,2304]{1,0:T(8,128)(2,1)S(1)}, bf16[64,2304]{1,0:T(8,128)(2,1)S(1)}, u32[]{:S(2)}, u32[]{:S(2)}) collective-permute-start(bf16[64,2304]{1,0:T(8,128)(2,1)S(1)} %shard_map.96), channel_id=1, source_target_pairs={{0,256},{128,384},{256,512},{384,640},{512,768},{640,896},{768,0},... | collective-permute-start | bytes 884744 | tf_op jit(solution)/shard_map/ppermute | solution.py:249
  67.4 1.9 %collective-permute-start.7 = (bf16[64,2304]{1,0:T(8,128)(2,1)S(1)}, bf16[64,2304]{1,0:T(8,128)(2,1)S(1)}, u32[]{:S(2)}, u32[]{:S(2)}) collective-permute-start(bf16[64,2304]{1,0:T(8,128)(2,1)S(1)} %collective-permute-done.3.near_ref), channel_id=1, source_target_pairs={{0,64},{64,0},{128,192},{192,128},{256,320},{320,256},{384,448},{4... | collective-permute-start | bytes 884744 | tf_op jit(solution)/shard_map/ppermute | solution.py:244
  69.3 9.2 %collective-permute-done.6.passed_ref = bf16[64,2304]{1,0:T(8,128)(2,1)S(1)} collective-permute-done((bf16[64,2304]{1,0:T(8,128)(2,1)S(1)}, bf16[64,2304]{1,0:T(8,128)(2,1)S(1)}, u32[]{:S(2)}, u32[]{:S(2)}) %collective-permute-start.6) | collective-permute-done | bytes 294944 | tf_op jit(solution)/shard_map/ppermute | solution.py:249
  78.5 1.9 %collective-permute-start.8 = (bf16[64,2304]{1,0:T(8,128)(2,1)S(1)}, bf16[64,2304]{1,0:T(8,128)(2,1)S(1)}, u32[]{:S(2)}, u32[]{:S(2)}) collective-permute-start(bf16[64,2304]{1,0:T(8,128)(2,1)S(1)} %collective-permute-done.6.passed_ref), channel_id=1, source_target_pairs={{0,64},{64,0},{128,192},{192,128},{256,320},{320,256},{384,448},{4... | collective-permute-start | bytes 884744 | tf_op jit(solution)/shard_map/ppermute | solution.py:244
  80.4 1.5 %collective-permute-done.8.twin_passed_ref = bf16[64,2304]{1,0:T(8,128)(2,1)S(1)} collective-permute-done((bf16[64,2304]{1,0:T(8,128)(2,1)S(1)}, bf16[64,2304]{1,0:T(8,128)(2,1)S(1)}, u32[]{:S(2)}, u32[]{:S(2)}) %collective-permute-start.8) | collective-permute-done | bytes 294944 | tf_op jit(solution)/shard_map/ppermute | solution.py:244
  82.2 1.9 %collective-permute-start.10 = (bf16[64,2304]{1,0:T(8,128)(2,1)S(1)}, bf16[64,2304]{1,0:T(8,128)(2,1)S(1)}, u32[]{:S(2)}, u32[]{:S(2)}) collective-permute-start(bf16[64,2304]{1,0:T(8,128)(2,1)S(1)} %shard_map.97.refs_6_), channel_id=1, source_target_pairs={{0,256},{128,384},{256,512},{384,640},{512,768},{640,896},{768,0},... | collective-permute-start | bytes 884744 | tf_op jit(solution)/shard_map/ppermute | solution.py:249
  84.1 1.9 %collective-permute-start.9 = (bf16[64,2304]{1,0:T(8,128)(2,1)S(1)}, bf16[64,2304]{1,0:T(8,128)(2,1)S(1)}, u32[]{:S(2)}, u32[]{:S(2)}) collective-permute-start(bf16[64,2304]{1,0:T(8,128)(2,1)S(1)} %shard_map.97.refs_6_), channel_id=1, source_target_pairs={{0,128},{128,256},{256,384},{384,512},{512,640},{640,768},{768,896... | collective-permute-start | bytes 884744 | tf_op jit(solution)/shard_map/ppermute | solution.py:249
  86.1 8.8 %collective-permute-done.10.refs_4_ = bf16[64,2304]{1,0:T(8,128)(2,1)S(1)} collective-permute-done((bf16[64,2304]{1,0:T(8,128)(2,1)S(1)}, bf16[64,2304]{1,0:T(8,128)(2,1)S(1)}, u32[]{:S(2)}, u32[]{:S(2)}) %collective-permute-start.10) | collective-permute-done | bytes 294944 | tf_op jit(solution)/shard_map/ppermute | solution.py:249
  94.9 1.9 %collective-permute-start.11 = (bf16[64,2304]{1,0:T(8,128)(2,1)S(1)}, bf16[64,2304]{1,0:T(8,128)(2,1)S(1)}, u32[]{:S(2)}, u32[]{:S(2)}) collective-permute-start(bf16[64,2304]{1,0:T(8,128)(2,1)S(1)} %collective-permute-done.10.refs_4_), channel_id=1, source_target_pairs={{0,128},{128,256},{256,384},{384,512},{512,640},{640,768},{768,896... | collective-permute-start | bytes 884744 | tf_op jit(solution)/shard_map/ppermute | solution.py:249
  96.8 1.9 %collective-permute-start.14 = (bf16[64,2304]{1,0:T(8,128)(2,1)S(1)}, bf16[64,2304]{1,0:T(8,128)(2,1)S(1)}, u32[]{:S(2)}, u32[]{:S(2)}) collective-permute-start(bf16[64,2304]{1,0:T(8,128)(2,1)S(1)} %collective-permute-done.10.refs_4_), channel_id=1, source_target_pairs={{0,64},{64,0},{128,192},{192,128},{256,320},{320,256},{384,448},{4... | collective-permute-start | bytes 884744 | tf_op jit(solution)/shard_map/ppermute | solution.py:244
  98.7 2.4 %collective-permute-start.13 = (bf16[64,2304]{1,0:T(8,128)(2,1)S(1)}, bf16[64,2304]{1,0:T(8,128)(2,1)S(1)}, u32[]{:S(2)}, u32[]{:S(2)}) collective-permute-start(bf16[64,2304]{1,0:T(8,128)(2,1)S(1)} %collective-permute-done.9.refs_3_), channel_id=1, source_target_pairs={{0,64},{64,0},{128,192},{192,128},{256,320},{320,256},{384,448},{4... | collective-permute-start | bytes 884744 | tf_op jit(solution)/shard_map/ppermute | solution.py:244
  101.2 3.5 %collective-permute-done.11.refs_5_ = bf16[64,2304]{1,0:T(8,128)(2,1)S(1)} collective-permute-done((bf16[64,2304]{1,0:T(8,128)(2,1)S(1)}, bf16[64,2304]{1,0:T(8,128)(2,1)S(1)}, u32[]{:S(2)}, u32[]{:S(2)}) %collective-permute-start.11) | collective-permute-done | bytes 294944 | tf_op jit(solution)/shard_map/ppermute | solution.py:249
  104.7 1.9 %collective-permute-start.12 = (bf16[32,2304]{1,0:T(8,128)(2,1)S(1)}, bf16[32,2304]{1,0:T(8,128)(2,1)S(1)}, u32[]{:S(2)}, u32[]{:S(2)}) collective-permute-start(bf16[32,2304]{1,0:T(8,128)(2,1)S(1)} %slice.20), channel_id=1, source_target_pairs={{0,128},{128,256},{256,384},{384,512},{512,640},{640,768},{768,896... | collective-permute-start | bytes 442376 | tf_op jit(solution)/shard_map/ppermute | solution.py:249
  106.6 1.9 %collective-permute-start.15 = (bf16[64,2304]{1,0:T(8,128)(2,1)S(1)}, bf16[64,2304]{1,0:T(8,128)(2,1)S(1)}, u32[]{:S(2)}, u32[]{:S(2)}) collective-permute-start(bf16[64,2304]{1,0:T(8,128)(2,1)S(1)} %collective-permute-done.11.refs_5_), channel_id=1, source_target_pairs={{0,64},{64,0},{128,192},{192,128},{256,320},{320,256},{384,448},{4... | collective-permute-start | bytes 884744 | tf_op jit(solution)/shard_map/ppermute | solution.py:244
  108.6 4.4 %collective-permute-done.12.refs_7_ = bf16[32,2304]{1,0:T(8,128)(2,1)S(1)} collective-permute-done((bf16[32,2304]{1,0:T(8,128)(2,1)S(1)}, bf16[32,2304]{1,0:T(8,128)(2,1)S(1)}, u32[]{:S(2)}, u32[]{:S(2)}) %collective-permute-start.12) | collective-permute-done | bytes 147488 | tf_op jit(solution)/shard_map/ppermute | solution.py:249
  113.0 1.9 %collective-permute-start.16 = (bf16[32,2304]{1,0:T(8,128)(2,1)S(1)}, bf16[32,2304]{1,0:T(8,128)(2,1)S(1)}, u32[]{:S(2)}, u32[]{:S(2)}) collective-permute-start(bf16[32,2304]{1,0:T(8,128)(2,1)S(1)} %collective-permute-done.12.refs_7_), channel_id=1, source_target_pairs={{0,64},{64,0},{128,192},{192,128},{256,320},{320,256},{384,448},{4... | collective-permute-start | bytes 442376 | tf_op jit(solution)/shard_map/ppermute | solution.py:244
  116.2 1.6 %shard_map.98 = (bf16[64,16,256]{2,1,0:T(8,128)(2,1)}, bf16[512,2304]{1,0:T(8,128)(2,1)S(1)}) custom-call(s32[1]{0:T(128)} %bitcast.2.refs_0_, bf16[256,1536]{1,0:T(8,128)(2,1)S(1)} %bitcast.11, bf16[768,256]{1,0:T(8,128)(2,1)S(1)} %bitcast.14, bf16[64,2304]{1,0:T(8,128)(2,1)S(1)} %collective-permute-done.9.refs_3_, ...), custom_call_target="tpu_custom_call" | custom-call | flops 603979776 | bytes 6422532 | tf_op jit(solution)/shard_map/pallas_call | solution.py:217
  117.8 5.3 %all-to-all-start.1 = ((bf16[64,16,256]{2,1,0:T(8,128)(2,1)}), bf16[64,16,256]{2,1,0:T(8,128)(2,1)S(1)}, u32[]{:S(2)}, u32[]{:S(2)}) async-start(bf16[64,16,256]{2,1,0:T(8,128)(2,1)} %get-tuple-element.39), calls=%async_computation.1 | async-start | bytes 1048576 | tf_op jit(solution)/shard_map/all_to_all | solution.py:241
  123.2 2.2 %fusion.2 = bf16[1,768,256]{2,1,0:T(8,128)(2,1)} fusion(bf16[512,2304]{1,0:T(8,128)(2,1)S(1)} %get-tuple-element.43, bf16[512,512]{1,0:T(8,128)(2,1)} %copy-done.5), kind=kOutput, calls=%fused_computation.4 | convolution fusion | flops 201523200 | bytes 1441792 | tf_op jit(solution)/shard_map/dot_general | solution.py:15
  125.4 1.5 %fusion = bf16[1,256,1536]{2,1,0:T(8,128)(2,1)} fusion(bf16[512,2304]{1,0:T(8,128)(2,1)S(1)} %get-tuple-element.43, bf16[512,512]{1,0:T(8,128)(2,1)S(1)} %copy-done.6), kind=kOutput, calls=%fused_computation.1 | convolution fusion | flops 403046400 | bytes 2621440 | tf_op jit(solution)/shard_map/dot_general | solution.py:15
  126.8 16.1 %all-to-all-done.1.refs_1_ = bf16[64,16,256]{2,1,0:T(8,128)(2,1)S(1)} async-done(((bf16[64,16,256]{2,1,0:T(8,128)(2,1)}), bf16[64,16,256]{2,1,0:T(8,128)(2,1)S(1)}, u32[]{:S(2)}, u32[]{:S(2)}) %all-to-all-start.1) | async-done | bytes 524320 | tf_op jit(solution)/shard_map/all_to_all | solution.py:241
  (30 shorter events, 8.7 us)
Async XLA Ops:
  0.6 48.8 %copy-start.3 = (bf16[1,768,256]{2,1,0:T(8,128)(2,1)S(1)}, bf16[1,768,256]{2,1,0:T(8,128)(2,1)}, u32[]{:S(2)}) copy-start(bf16[1,768,256]{2,1,0:T(8,128)(2,1)} %param.8) | copy-start | bytes 1179652
  0.6 48.8 %copy-start.1 = (bf16[1,256,1536]{2,1,0:T(8,128)(2,1)S(1)}, bf16[1,256,1536]{2,1,0:T(8,128)(2,1)}, u32[]{:S(2)}) copy-start(bf16[1,256,1536]{2,1,0:T(8,128)(2,1)} %param.7) | copy-start | bytes 2359300
  3.1 42.5 %all-to-all-start = ((bf16[64,16,256]{2,1,0:T(8,128)(2,1)}), bf16[64,16,256]{2,1,0:T(8,128)(2,1)S(1)}, u32[]{:S(2)}, u32[]{:S(2)}) async-start(bf16[64,16,256]{2,1,0:T(8,128)(2,1)} %get-tuple-element.26), calls=%async_computation | async-start | bytes 1048576 | tf_op jit(solution)/shard_map/all_to_all | solution.py:241
  26.2 1.1 copy-start
  27.3 1.0 copy-start.2
  28.4 5.7 %collective-permute-start = (bf16[256,1536]{1,0:T(8,128)(2,1)S(1)}, bf16[256,1536]{1,0:T(8,128)(2,1)S(1)}, u32[]{:S(2)}, u32[]{:S(2)}) collective-permute-start(bf16[256,1536]{1,0:T(8,128)(2,1)S(1)} %get-tuple-element.29), channel_id=1, source_target_pairs={{0,64},{64,0},{128,192},{192,128},{256,320},{320,256},{384,448},{4... | collective-permute-start | bytes 2359304 | tf_op jit(solution)/shard_map/ppermute | solution.py:244
  30.3 3.7 %collective-permute-start.1 = (bf16[768,256]{1,0:T(8,128)(2,1)S(1)}, bf16[768,256]{1,0:T(8,128)(2,1)S(1)}, u32[]{:S(2)}, u32[]{:S(2)}) collective-permute-start(bf16[768,256]{1,0:T(8,128)(2,1)S(1)} %get-tuple-element.30), channel_id=1, source_target_pairs={{0,64},{64,0},{128,192},{192,128},{256,320},{320,256},{384,448},{4... | collective-permute-start | bytes 1179656 | tf_op jit(solution)/shard_map/ppermute | solution.py:244
  45.6 3.8 %collective-permute-start.2 = (bf16[64,16,256]{2,1,0:T(8,128)(2,1)S(1)}, bf16[64,16,256]{2,1,0:T(8,128)(2,1)S(1)}, u32[]{:S(2)}, u32[]{:S(2)}) collective-permute-start(bf16[64,16,256]{2,1,0:T(8,128)(2,1)S(1)} %all-to-all-done.refs_1_), channel_id=1, source_target_pairs={{0,64},{64,0},{128,192},{192,128},{256,320},{320,256},{384,448},{4... | collective-permute-start | bytes 1572872 | tf_op jit(solution)/shard_map/ppermute | solution.py:244
  50.5 0.8 copy-start.5
  51.3 13.4 %collective-permute-start.4 = (bf16[64,2304]{1,0:T(8,128)(2,1)S(1)}, bf16[64,2304]{1,0:T(8,128)(2,1)S(1)}, u32[]{:S(2)}, u32[]{:S(2)}) collective-permute-start(bf16[64,2304]{1,0:T(8,128)(2,1)S(1)} %get-tuple-element.37), channel_id=1, source_target_pairs={{0,128},{128,256},{256,384},{384,512},{512,640},{640,768},{768,896... | collective-permute-start | bytes 884744 | tf_op jit(solution)/shard_map/ppermute | solution.py:249
  53.8 10.9 %collective-permute-start.5 = (bf16[32,2304]{1,0:T(8,128)(2,1)S(1)}, bf16[32,2304]{1,0:T(8,128)(2,1)S(1)}, u32[]{:S(2)}, u32[]{:S(2)}) collective-permute-start(bf16[32,2304]{1,0:T(8,128)(2,1)S(1)} %get-tuple-element.38), channel_id=1, source_target_pairs={{0,256},{128,384},{256,512},{384,640},{512,768},{640,896},{768,0},... | collective-permute-start | bytes 442376 | tf_op jit(solution)/shard_map/ppermute | solution.py:249
  56.3 11.1 %collective-permute-start.3 = (bf16[64,2304]{1,0:T(8,128)(2,1)S(1)}, bf16[64,2304]{1,0:T(8,128)(2,1)S(1)}, u32[]{:S(2)}, u32[]{:S(2)}) collective-permute-start(bf16[64,2304]{1,0:T(8,128)(2,1)S(1)} %get-tuple-element.35), channel_id=1, source_target_pairs={{0,128},{128,256},{256,384},{384,512},{512,640},{640,768},{768,896... | collective-permute-start | bytes 884744 | tf_op jit(solution)/shard_map/ppermute | solution.py:249
  64.7 13.8 %collective-permute-start.6 = (bf16[64,2304]{1,0:T(8,128)(2,1)S(1)}, bf16[64,2304]{1,0:T(8,128)(2,1)S(1)}, u32[]{:S(2)}, u32[]{:S(2)}) collective-permute-start(bf16[64,2304]{1,0:T(8,128)(2,1)S(1)} %shard_map.96), channel_id=1, source_target_pairs={{0,256},{128,384},{256,512},{384,640},{512,768},{640,896},{768,0},... | collective-permute-start | bytes 884744 | tf_op jit(solution)/shard_map/ppermute | solution.py:249
  67.4 13.0 %collective-permute-start.7 = (bf16[64,2304]{1,0:T(8,128)(2,1)S(1)}, bf16[64,2304]{1,0:T(8,128)(2,1)S(1)}, u32[]{:S(2)}, u32[]{:S(2)}) collective-permute-start(bf16[64,2304]{1,0:T(8,128)(2,1)S(1)} %collective-permute-done.3.near_ref), channel_id=1, source_target_pairs={{0,64},{64,0},{128,192},{192,128},{256,320},{320,256},{384,448},{4... | collective-permute-start | bytes 884744 | tf_op jit(solution)/shard_map/ppermute | solution.py:244
  78.5 3.5 %collective-permute-start.8 = (bf16[64,2304]{1,0:T(8,128)(2,1)S(1)}, bf16[64,2304]{1,0:T(8,128)(2,1)S(1)}, u32[]{:S(2)}, u32[]{:S(2)}) collective-permute-start(bf16[64,2304]{1,0:T(8,128)(2,1)S(1)} %collective-permute-done.6.passed_ref), channel_id=1, source_target_pairs={{0,64},{64,0},{128,192},{192,128},{256,320},{320,256},{384,448},{4... | collective-permute-start | bytes 884744 | tf_op jit(solution)/shard_map/ppermute | solution.py:244
  82.2 12.7 %collective-permute-start.10 = (bf16[64,2304]{1,0:T(8,128)(2,1)S(1)}, bf16[64,2304]{1,0:T(8,128)(2,1)S(1)}, u32[]{:S(2)}, u32[]{:S(2)}) collective-permute-start(bf16[64,2304]{1,0:T(8,128)(2,1)S(1)} %shard_map.97.refs_6_), channel_id=1, source_target_pairs={{0,256},{128,384},{256,512},{384,640},{512,768},{640,896},{768,0},... | collective-permute-start | bytes 884744 | tf_op jit(solution)/shard_map/ppermute | solution.py:249
  84.1 14.6 %collective-permute-start.9 = (bf16[64,2304]{1,0:T(8,128)(2,1)S(1)}, bf16[64,2304]{1,0:T(8,128)(2,1)S(1)}, u32[]{:S(2)}, u32[]{:S(2)}) collective-permute-start(bf16[64,2304]{1,0:T(8,128)(2,1)S(1)} %shard_map.97.refs_6_), channel_id=1, source_target_pairs={{0,128},{128,256},{256,384},{384,512},{512,640},{640,768},{768,896... | collective-permute-start | bytes 884744 | tf_op jit(solution)/shard_map/ppermute | solution.py:249
  94.9 9.8 %collective-permute-start.11 = (bf16[64,2304]{1,0:T(8,128)(2,1)S(1)}, bf16[64,2304]{1,0:T(8,128)(2,1)S(1)}, u32[]{:S(2)}, u32[]{:S(2)}) collective-permute-start(bf16[64,2304]{1,0:T(8,128)(2,1)S(1)} %collective-permute-done.10.refs_4_), channel_id=1, source_target_pairs={{0,128},{128,256},{256,384},{384,512},{512,640},{640,768},{768,896... | collective-permute-start | bytes 884744 | tf_op jit(solution)/shard_map/ppermute | solution.py:249
  96.8 18.1 %collective-permute-start.14 = (bf16[64,2304]{1,0:T(8,128)(2,1)S(1)}, bf16[64,2304]{1,0:T(8,128)(2,1)S(1)}, u32[]{:S(2)}, u32[]{:S(2)}) collective-permute-start(bf16[64,2304]{1,0:T(8,128)(2,1)S(1)} %collective-permute-done.10.refs_4_), channel_id=1, source_target_pairs={{0,64},{64,0},{128,192},{192,128},{256,320},{320,256},{384,448},{4... | collective-permute-start | bytes 884744 | tf_op jit(solution)/shard_map/ppermute | solution.py:244
  98.7 16.2 %collective-permute-start.13 = (bf16[64,2304]{1,0:T(8,128)(2,1)S(1)}, bf16[64,2304]{1,0:T(8,128)(2,1)S(1)}, u32[]{:S(2)}, u32[]{:S(2)}) collective-permute-start(bf16[64,2304]{1,0:T(8,128)(2,1)S(1)} %collective-permute-done.9.refs_3_), channel_id=1, source_target_pairs={{0,64},{64,0},{128,192},{192,128},{256,320},{320,256},{384,448},{4... | collective-permute-start | bytes 884744 | tf_op jit(solution)/shard_map/ppermute | solution.py:244
  104.7 8.2 %collective-permute-start.12 = (bf16[32,2304]{1,0:T(8,128)(2,1)S(1)}, bf16[32,2304]{1,0:T(8,128)(2,1)S(1)}, u32[]{:S(2)}, u32[]{:S(2)}) collective-permute-start(bf16[32,2304]{1,0:T(8,128)(2,1)S(1)} %slice.20), channel_id=1, source_target_pairs={{0,128},{128,256},{256,384},{384,512},{512,640},{640,768},{768,896... | collective-permute-start | bytes 442376 | tf_op jit(solution)/shard_map/ppermute | solution.py:249
  106.6 9.6 %collective-permute-start.15 = (bf16[64,2304]{1,0:T(8,128)(2,1)S(1)}, bf16[64,2304]{1,0:T(8,128)(2,1)S(1)}, u32[]{:S(2)}, u32[]{:S(2)}) collective-permute-start(bf16[64,2304]{1,0:T(8,128)(2,1)S(1)} %collective-permute-done.11.refs_5_), channel_id=1, source_target_pairs={{0,64},{64,0},{128,192},{192,128},{256,320},{320,256},{384,448},{4... | collective-permute-start | bytes 884744 | tf_op jit(solution)/shard_map/ppermute | solution.py:244
  113.0 3.3 %collective-permute-start.16 = (bf16[32,2304]{1,0:T(8,128)(2,1)S(1)}, bf16[32,2304]{1,0:T(8,128)(2,1)S(1)}, u32[]{:S(2)}, u32[]{:S(2)}) collective-permute-start(bf16[32,2304]{1,0:T(8,128)(2,1)S(1)} %collective-permute-done.12.refs_7_), channel_id=1, source_target_pairs={{0,64},{64,0},{128,192},{192,128},{256,320},{320,256},{384,448},{4... | collective-permute-start | bytes 442376 | tf_op jit(solution)/shard_map/ppermute | solution.py:244
  117.8 7.5 %copy-start.6 = (bf16[512,512]{1,0:T(8,128)(2,1)S(1)}, bf16[512,512]{1,0:T(8,128)(2,1)}, u32[]{:S(2)}) copy-start(bf16[512,512]{1,0:T(8,128)(2,1)} %copy-done.5) | copy-start | bytes 1572868
  117.8 25.1 %all-to-all-start.1 = ((bf16[64,16,256]{2,1,0:T(8,128)(2,1)}), bf16[64,16,256]{2,1,0:T(8,128)(2,1)S(1)}, u32[]{:S(2)}, u32[]{:S(2)}) async-start(bf16[64,16,256]{2,1,0:T(8,128)(2,1)} %get-tuple-element.39), calls=%async_computation.1 | async-start | bytes 1048576 | tf_op jit(solution)/shard_map/all_to_all | solution.py:241
  123.2 19.7 %copy-start.4 = (bf16[512,128]{1,0:T(8,128)(2,1)S(1)}, bf16[512,128]{1,0:T(8,128)(2,1)}, u32[]{:S(2)}) copy-start(bf16[512,128]{1,0:T(8,128)(2,1)} %get-tuple-element.24.refs_0_) | copy-start | bytes 393220
